TPU v7x, 32 devices: a whole 2x2x4 slice. The times are simulated.
32 devices in a mesh: dp: 4 (over z), tm: 4 (over y, x), tile: 2 (over core).
Axes of the slice: x: 2, y: 2, z: 4, core: 2. Of those that a mesh axis runs over, the one named last changes fastest.
Arguments:
- activations: bfloat16 [4, 32, 16, 32, 128], P('dp', 'tm', 'tile'), may hold values from -6 to 6
- kernel: bfloat16 [3456, 128], replicated, may hold values from -0.109375 to 0.109375
- conv_bias: float32 [128], replicated, may hold values from -3 to 3
- cotangent: bfloat16 [4, 32, 16, 32, 128], P('dp', 'tm', 'tile'), may hold values from -6 to 6
Outputs:
- block_out: bfloat16 [4, 32, 16, 32, 128], P('dp', 'tm', 'tile')
- grad_input: bfloat16 [4, 32, 16, 32, 128], P('dp', 'tm', 'tile')
- weight_grad: float32 [3456, 128], P('dp')
- bias_grad: float32 [128], P('dp')
All inputs are finite; a program needn't handle non-finite values.
Results may differ from a plain program's by a relative error of at most 0.0095.
Values may be sent and summed in bfloat16 or wider, within the bound.
No kernel may reach another device: no remote copies, remote signals or barrier semaphores. Data moves between devices by JAX's collectives and lax.ppermute only.
A program may use at most 64 MiB of HBM per device.

v0:
```python
import math

import jax
import jax.numpy as jnp
from jax import lax
from jax.sharding import PartitionSpec as P


def passed_along(block, axis, distance):
    devices = range(lax.axis_size(axis))
    route = [(i - distance, i) for i in devices if i - distance in devices]
    return lax.ppermute(block, axis, route)


def padded_2(cells, sides, width):
    for axis, dim in sides:
        count = lax.axis_size(axis)
        ends = count - 1
        head = lax.slice_in_dim(cells, 0, width, axis=dim)
        tail = lax.slice_in_dim(cells, cells.shape[dim] - width, cells.shape[dim], axis=dim)
        cells = jnp.concatenate(
            [
                lax.ppermute(tail, axis, [(i, (i + 1) % count) for i in range(ends)]),
                cells,
                lax.ppermute(head, axis, [((i + 1) % count, i) for i in range(ends)]),
            ],
            axis=dim,
        )
    return cells


def stack_columns(window, breadth, starts):
    return jnp.concatenate([window[:, :, :, begin : begin + breadth] for begin in starts], axis=4)


def body(activations, kernel, conv_bias, cotangent):
    clip_count, frames, height, breadth, channels = activations.shape
    weights = kernel.reshape(3, 3, 3 * channels, channels)
    flipped = (
        kernel.reshape(3, 3, 3, channels, channels)
        .transpose(0, 1, 2, 4, 3)
        .reshape(3, 3, 3 * channels, channels)
    )
    earlier = passed_along(activations[:, frames - 2 :], "tm", 1)
    extended = jnp.concatenate([earlier, activations], axis=1)
    rimmed = padded_2(extended, (("tile", 2),), 1)
    padded = jnp.pad(rimmed, ((0, 0), (0, 0), (0, 0), (1, 1), (0, 0)))
    running = jnp.zeros((clip_count, frames, height, breadth, channels), jnp.float32) + conv_bias
    for tap_time in range(3):
        for tap_row in range(3):
            window = padded[:, tap_time : tap_time + frames, tap_row : tap_row + height]
            stacked = stack_columns(window, breadth, (0, 1, 2))
            running = running + jnp.einsum(
                "bfrwk,kd->bfrwd",
                stacked,
                weights[tap_time, tap_row],
                preferred_element_type=jnp.float32,
            )
    sigma = jax.nn.sigmoid(running)
    block_out = (activations.astype(jnp.float32) + running * sigma).astype(jnp.bfloat16)
    grad_pre = (cotangent.astype(jnp.float32) * sigma * (1.0 + running * (1.0 - sigma))).astype(
        jnp.bfloat16
    )
    later = passed_along(grad_pre[:, 0:2], "tm", -1)
    grad_extended = jnp.concatenate([grad_pre, later], axis=1)
    grad_rimmed = padded_2(grad_extended, (("tile", 2),), 1)
    grad_padded = jnp.pad(grad_rimmed, ((0, 0), (0, 0), (0, 0), (1, 1), (0, 0)))
    back = cotangent.astype(jnp.float32)
    pieces = []
    for tap_time in range(3):
        for tap_row in range(3):
            window = grad_padded[
                :, 2 - tap_time : 2 - tap_time + frames, 2 - tap_row : 2 - tap_row + height
            ]
            stacked = stack_columns(window, breadth, (2, 1, 0))
            back = back + jnp.einsum(
                "bfrwk,kd->bfrwd",
                stacked,
                flipped[tap_time, tap_row],
                preferred_element_type=jnp.float32,
            )
            source = stack_columns(
                padded[:, tap_time : tap_time + frames, tap_row : tap_row + height],
                breadth,
                (0, 1, 2),
            )
            pieces.append(
                jnp.einsum("bfrwk,bfrwd->kd", source, grad_pre, preferred_element_type=jnp.float32)
            )
    grad_input = back.astype(jnp.bfloat16)
    local_weight = jnp.stack(pieces).reshape(27 * channels, channels)
    local_bias = jnp.sum(grad_pre.astype(jnp.float32), axis=(0, 1, 2, 3))
    whole_weight, whole_bias = lax.psum((local_weight, local_bias), ("tm", "tile"))
    shard_weight, shard_bias = (
        lax.psum_scatter(whole_weight, "dp", scatter_dimension=0, tiled=True),
        lax.psum_scatter(whole_bias, "dp", scatter_dimension=0, tiled=True),
    )
    positions = (
        clip_count
        * frames
        * height
        * breadth
        * lax.axis_size("dp")
        * lax.axis_size("tm")
        * lax.axis_size("tile")
    )
    scale = 1.0 / math.sqrt(positions)
    return (block_out, grad_input, shard_weight * scale, shard_bias * scale)


def solution(mesh):
    return jax.shard_map(
        body,
        mesh=mesh,
        in_specs=(P("dp", "tm", "tile", None, None), P(), P(), P("dp", "tm", "tile", None, None)),
        out_specs=(
            P("dp", "tm", "tile", None, None),
            P("dp", "tm", "tile", None, None),
            P("dp", None),
            P("dp"),
        ),
        check_vma=False,
    )
```

profile of v0, /device:TPU:0, one launch (start us, length us, event | category | flops | bytes accessed | tf_op | source)
XLA Modules:
  0.0 151.5 jit_solution(17597154954212374362)
XLA Ops:
  7.2 1.0 slice.374
  8.2 4.8 %collective-permute-start = (bf16[1,2,8,32,128]{4,3,2,1,0:T(8,128)(2,1)S(1)}, bf16[1,2,8,32,128]{4,3,2,1,0:T(8,128)(2,1)S(1)}, u32[]{:S(2)}, u32[]{:S(2)}) collective-permute-start(bf16[1,2,8,32,128]{4,3,2,1,0:T(8,128)(2,1)S(1)} %slice.374), channel_id=1, source_target_pairs={{0,2},{2,4},{4,6},{1,3},{3,5},{5,7},{8,10},{10,12},{12,14},{9,11},... | collective-permute-start | bytes 393224 | tf_op jit(solution)/shard_map/ppermute | solution.py:12
  13.1 2.7 %collective-permute-done = bf16[1,2,8,32,128]{4,3,2,1,0:T(8,128)(2,1)S(1)} collective-permute-done((bf16[1,2,8,32,128]{4,3,2,1,0:T(8,128)(2,1)S(1)}, bf16[1,2,8,32,128]{4,3,2,1,0:T(8,128)(2,1)S(1)}, u32[]{:S(2)}, u32[]{:S(2)}) %collective-permute-start) | collective-permute-done | bytes 131104 | tf_op jit(solution)/shard_map/ppermute | solution.py:12
  15.8 1.1 constant_dynamic-update-slice_fusion
  17.0 1.3 collective-permute-start.1
  18.3 1.3 collective-permute-start.2
  19.6 1.7 %copy.9 = bf16[3,3,3,128,128]{3,4,2,1,0:T(8,128)(2,1)} copy(bf16[3,3,3,128,128]{4,3,2,1,0:T(8,128)(2,1)S(1)} %bitcast.387) | data formatting | bytes 1769472 | tf_op jit(solution)/shard_map/reshape | solution.py:40
  23.0 2.8 %fusion.138 = (bf16[1,8,8,32,128]{4,3,2,1,0:T(8,128)(2,1)S(1)}, bf16[1,8,8,32,128]{4,3,2,1,0:T(8,128)(2,1)S(1)}, bf16[1,8,8,32,128]{4,3,2,1,0:T(8,128)(2,1)S(1)}...) fusion(bf16[1,10,10,34,128]{4,3,2,1,0:T(8,128)(2,1)S(1)} %selec, ...), kind=kLoop, calls=%fused_computation.212 | loop fusion | bytes 18874368 | tf_op jit(solution)/shard_map/slice | solution.py:33
  31.6 1.8 %convert_reduce_fusion = (f32[128]{0:T(128)S(1)}, bf16[1,8,8,32,128]{4,3,2,1,0:T(8,128)(2,1)S(1)}, bf16[1,8,8,32,128]{4,3,2,1,0:T(8,128)(2,1)}) fusion(bf16[1,8,8,32,128]{4,3,2,1,0:T(8,128)(2,1)S(1)} %copy-done.4, bf16[1,8,8,32,128]{4,3,2,1,0:T(8,128)(2,1)S(1)} %copy-done.3, f32[8,8,32,128]{3,2,1,0:T(8,128)S(1)} %fusion.66, ...), kind=kOutput, calls=%fused_computation.125 | convolution fusion | flops 212074368 | bytes 5030400 | tf_op jit(solution)/shard_map/bfrwk,kd->bfrwd/dot_general | solution.py:53
  34.6 0.6 fusion.83
  35.3 0.6 fusion.82
  36.5 0.6 fusion.80
  37.8 0.6 fusion.78
  39.1 1.2 copy-done
  40.4 1.3 collective-permute-start.3
  41.7 12.2 %all-reduce.2 = f32[128]{0:T(128)S(1)} all-reduce(f32[128]{0:T(128)S(1)} %get-tuple-element.4), channel_id=3, replica_groups=mesh['dp'=4,'tm'=4,'tile'=2] {'dp'}, use_global_device_ids=true, to_apply=%region_4.5.clone | all-reduce | flops 128 | bytes 1024
  54.0 16.6 %psum.17 = f32[32]{0:T(128)S(1)} all-reduce(f32[32]{0:T(128)S(1)} %dynamic-slice.1), channel_id=1, replica_groups=mesh['dp'=4,'tm'=4,'tile'=2] {'tm','tile'}, use_global_device_ids=true, to_apply=%region_3.4 | all-reduce | flops 32 | bytes 256 | tf_op jit(solution)/shard_map/psum | solution.py:93
  71.1 1.3 collective-permute-start.4
  72.4 1.3 collective-permute-start.5
  73.8 1.8 %collective-permute-done.5 = bf16[1,10,1,32,128]{4,3,2,1,0:T(8,128)(2,1)S(1)} collective-permute-done((bf16[1,10,1,32,128]{4,3,2,1,0:T(8,128)(2,1)S(1)}, bf16[1,10,1,32,128]{4,3,2,1,0:T(8,128)(2,1)S(1)}, u32[]{:S(2)}, u32[]{:S(2)}) %collective-permute-start.5) | collective-permute-done | bytes 81952 | tf_op jit(solution)/shard_map/ppermute | solution.py:25
  76.2 2.8 %fusion.137 = (bf16[1,8,8,32,128]{4,3,2,1,0:T(8,128)(2,1)S(1)}, bf16[1,8,8,32,128]{4,3,2,1,0:T(8,128)(2,1)S(1)}, bf16[1,8,8,32,128]{4,3,2,1,0:T(8,128)(2,1)S(1)}...) fusion(bf16[1,10,10,34,128]{4,3,2,1,0:T(8,128)(2,1)S(1)} %selec, ...), kind=kLoop, calls=%fused_computation.211 | loop fusion | bytes 18874368 | tf_op jit(solution)/shard_map/slice | solution.py:33
  79.0 1.6 %fusion.56 = f32[1,8,8,32,128]{4,3,2,1,0:T(8,128)} fusion(bf16[1,8,8,32,128]{4,3,2,1,0:T(8,128)(2,1)S(1)} %get-tuple-element.9, bf16[1,8,8,32,128]{4,3,2,1,0:T(8,128)(2,1)S(1)} %get-tuple-element.5, bf16[1,8,8,32,128]{4,3,2,1,0:T(8,128)(2,1)S(1)} %get-tuple-element.10, bf16[3,3,384,128]{3,2,1,0:T(8,128)(2,1)S(1)} %bitcast.378), kind=kOutput, calls=%fused_computation.75 | convolution fusion | flops 206045184 | bytes 2719744 | tf_op jit(solution)/shard_map/bfrwk,kd->bfrwd/dot_general | solution.py:76
  80.6 1.5 %fusion.61 = f32[1,8,8,32,128]{4,3,2,1,0:T(8,128)} fusion(bf16[1,8,8,32,128]{4,3,2,1,0:T(8,128)(2,1)S(1)} %get-tuple-element.21, bf16[1,8,8,32,128]{4,3,2,1,0:T(8,128)(2,1)S(1)} %fusion.91, bf16[1,8,8,32,128]{4,3,2,1,0:T(8,128)(2,1)S(1)} %get-tuple-element.22, bf16[3,3,384,128]{3,2,1,0:T(8,128)(2,1)S(1)} %bitcast.379), kind=kOutput, calls=%fused_computation.80 | convolution fusion | flops 206045184 | bytes 2719744 | tf_op jit(solution)/shard_map/bfrwk,kd->bfrwd/dot_general | solution.py:76
  82.7 1.6 %fusion.60 = f32[1,8,8,32,128]{4,3,2,1,0:T(8,128)} fusion(bf16[1,8,8,32,128]{4,3,2,1,0:T(8,128)(2,1)S(1)} %get-tuple-element.19, bf16[1,8,8,32,128]{4,3,2,1,0:T(8,128)(2,1)S(1)} %get-tuple-element.65, bf16[1,8,8,32,128]{4,3,2,1,0:T(8,128)(2,1)S(1)} %get-tuple-element.20, bf16[3,3,384,128]{3,2,1,0:T(8,128)(2,1)S(1)} %bitcast.380), kind=kOutput, calls=%fused_computation.79 | convolution fusion | flops 206045184 | bytes 2719744 | tf_op jit(solution)/shard_map/bfrwk,kd->bfrwd/dot_general | solution.py:76
  84.4 1.6 %fusion.59 = f32[1,8,8,32,128]{4,3,2,1,0:T(8,128)} fusion(bf16[1,8,8,32,128]{4,3,2,1,0:T(8,128)(2,1)S(1)} %get-tuple-element.17, bf16[1,8,8,32,128]{4,3,2,1,0:T(8,128)(2,1)S(1)} %get-tuple-element.45, bf16[1,8,8,32,128]{4,3,2,1,0:T(8,128)(2,1)S(1)} %get-tuple-element.18, bf16[3,3,384,128]{3,2,1,0:T(8,128)(2,1)S(1)} %bitcast.381), kind=kOutput, calls=%fused_computation.78 | convolution fusion | flops 206045184 | bytes 2719744 | tf_op jit(solution)/shard_map/bfrwk,kd->bfrwd/dot_general | solution.py:76
  85.9 1.6 %fusion.58 = f32[1,8,8,32,128]{4,3,2,1,0:T(8,128)} fusion(bf16[1,8,8,32,128]{4,3,2,1,0:T(8,128)(2,1)S(1)} %get-tuple-element.13, bf16[1,8,8,32,128]{4,3,2,1,0:T(8,128)(2,1)S(1)} %get-tuple-element.63, bf16[1,8,8,32,128]{4,3,2,1,0:T(8,128)(2,1)S(1)} %get-tuple-element.14, bf16[3,3,384,128]{3,2,1,0:T(8,128)(2,1)S(1)} %bitcast.382), kind=kOutput, calls=%fused_computation.77 | convolution fusion | flops 206045184 | bytes 2719744 | tf_op jit(solution)/shard_map/bfrwk,kd->bfrwd/dot_general | solution.py:76
  87.5 1.6 %fusion.57 = f32[1,8,8,32,128]{4,3,2,1,0:T(8,128)} fusion(bf16[1,8,8,32,128]{4,3,2,1,0:T(8,128)(2,1)S(1)} %get-tuple-element.11, bf16[1,8,8,32,128]{4,3,2,1,0:T(8,128)(2,1)S(1)} %get-tuple-element.44, bf16[1,8,8,32,128]{4,3,2,1,0:T(8,128)(2,1)S(1)} %get-tuple-element.12, bf16[3,3,384,128]{3,2,1,0:T(8,128)(2,1)S(1)} %bitcast.383), kind=kOutput, calls=%fused_computation.76 | convolution fusion | flops 206045184 | bytes 2719744 | tf_op jit(solution)/shard_map/bfrwk,kd->bfrwd/dot_general | solution.py:76
  89.0 1.6 %fusion.55 = f32[1,8,8,32,128]{4,3,2,1,0:T(8,128)} fusion(bf16[1,8,8,32,128]{4,3,2,1,0:T(8,128)(2,1)S(1)} %get-tuple-element.24, bf16[1,8,8,32,128]{4,3,2,1,0:T(8,128)(2,1)S(1)} %get-tuple-element.64, bf16[1,8,8,32,128]{4,3,2,1,0:T(8,128)(2,1)S(1)} %get-tuple-element.8, bf16[3,3,384,128]{3,2,1,0:T(8,128)(2,1)S(1)} %bitcast.384), kind=kOutput, calls=%fused_computation.74 | convolution fusion | flops 206045184 | bytes 2719744 | tf_op jit(solution)/shard_map/bfrwk,kd->bfrwd/dot_general | solution.py:76
  90.6 1.6 %fusion.63 = f32[1,8,8,32,128]{4,3,2,1,0:T(8,128)} fusion(bf16[1,2,8,32,128]{4,3,2,1,0:T(8,128)(2,1)S(1)} %collective-permute-done.3, bf16[1,8,8,32,128]{4,3,2,1,0:T(8,128)(2,1)S(1)} %get-tuple-element.5, bf16[1,8,8,32,128]{4,3,2,1,0:T(8,128)(2,1)S(1)} %get-tuple-element.15, bf16[1,8,8,32,128]{4,3,2,1,0:T(8,128)(2,1)S(1)} %get-tuple-element.16, ...), kind=kOutput, calls=%fused_computation.82 | convolution fusion | flops 207618048 | bytes 2850816 | tf_op jit(solution)/shard_map/bfrwk,kd->bfrwd/dot_general | solution.py:76
  92.2 5.2 %fusion.76 = bf16[1,8,8,32,128]{4,3,2,1,0:T(8,128)(2,1)} fusion(f32[1,8,8,32,128]{4,3,2,1,0:T(8,128)} %fusion.55, f32[1,8,8,32,128]{4,3,2,1,0:T(8,128)} %fusion.56, f32[1,8,8,32,128]{4,3,2,1,0:T(8,128)} %fusion.57, f32[1,8,8,32,128]{4,3,2,1,0:T(8,128)} %fusion.58, f32[1,8,8,32,128]{4,3,2,1,0:T(8,128)} %fusion.63, f32[1,8,8,32,128]{4,3,2,1,0:T(8,128)} %fusion.59, ...), kind=kOutput, calls=%fused_computation.102 | convolution fusion | flops 208928768 | bytes 11108352 | tf_op jit(solution)/shard_map/bfrwk,kd->bfrwd/dot_general | solution.py:76
  97.4 45.5 %all-reduce.5.cloned.1.call-done = f32[864,128]{1,0:T(8,128)} async-done(((f32[864,128]{1,0:T(8,128)}), f32[864,128]{1,0:T(8,128)}) %all-reduce.5.cloned.1.call-update) | async-done | bytes 442384 | tf_op jit(solution)/shard_map/psum | solution.py:93
  142.8 1.8 %broadcast_multiply_fusion = f32[864,128]{1,0:T(8,128)} fusion(f32[864,128]{1,0:T(8,128)} %all-reduce.5.cloned.1.call-done), kind=kLoop, calls=%fused_computation.160 | loop fusion | flops 110592 | bytes 884736 | tf_op jit(solution)/shard_map/mul | solution.py:108
  (48 shorter events, 12.0 us)
Async XLA Ops:
  7.2 12.4 %copy-start.2 = (bf16[3456,128]{1,0:T(8,128)(2,1)S(1)}, bf16[3456,128]{1,0:T(8,128)(2,1)}, u32[]{:S(2)}) copy-start(bf16[3456,128]{1,0:T(8,128)(2,1)} %param.5) | copy-start | bytes 2654212
  7.2 85.0 %reduce-scatter.2.cloned.1.call-start = ((), (), s32[]{:S(2)}) async-start(), calls=%async_computation.1 | async-start | bytes 2211840 | tf_op jit(solution)/shard_map/reduce_scatter | solution.py:95
  8.2 13.0 %copy-start.6 = (u32[32]{0:T(128)S(1)}, u32[32]{0:T(128)}, u32[]{:S(2)}) copy-start(u32[32]{0:T(128)} %constant.18) | copy-start | bytes 388
  8.2 7.6 %collective-permute-start = (bf16[1,2,8,32,128]{4,3,2,1,0:T(8,128)(2,1)S(1)}, bf16[1,2,8,32,128]{4,3,2,1,0:T(8,128)(2,1)S(1)}, u32[]{:S(2)}, u32[]{:S(2)}) collective-permute-start(bf16[1,2,8,32,128]{4,3,2,1,0:T(8,128)(2,1)S(1)} %slice.374), channel_id=1, source_target_pairs={{0,2},{2,4},{4,6},{1,3},{3,5},{5,7},{8,10},{10,12},{12,14},{9,11},... | collective-permute-start | bytes 393224 | tf_op jit(solution)/shard_map/ppermute | solution.py:12
  17.0 5.5 %collective-permute-start.1 = (bf16[1,10,1,32,128]{4,3,2,1,0:T(8,128)(2,1)S(1)}, bf16[1,10,1,32,128]{4,3,2,1,0:T(8,128)(2,1)S(1)}, u32[]{:S(2)}, u32[]{:S(2)}) collective-permute-start(bf16[1,10,1,32,128]{4,3,2,1,0:T(8,128)(2,1)S(1)} %get-tuple-element.61), channel_id=1, source_target_pairs={{0,1},{2,3},{4,5},{6,7},{8,9},{10,11},{12,13},{14,15},{16,17},{18,... | collective-permute-start | bytes 245768 | tf_op jit(solution)/shard_map/ppermute | solution.py:23
  18.3 4.2 %collective-permute-start.2 = (bf16[1,10,1,32,128]{4,3,2,1,0:T(8,128)(2,1)S(1)}, bf16[1,10,1,32,128]{4,3,2,1,0:T(8,128)(2,1)S(1)}, u32[]{:S(2)}, u32[]{:S(2)}) collective-permute-start(bf16[1,10,1,32,128]{4,3,2,1,0:T(8,128)(2,1)S(1)} %get-tuple-element.62), channel_id=1, source_target_pairs={{1,0},{3,2},{5,4},{7,6},{9,8},{11,10},{13,12},{15,14},{17,16},{19,... | collective-permute-start | bytes 245768 | tf_op jit(solution)/shard_map/ppermute | solution.py:25
  23.0 2.8 %copy-start.3 = (bf16[1,8,8,32,128]{4,3,2,1,0:T(8,128)(2,1)S(1)}, bf16[1,8,8,32,128]{4,3,2,1,0:T(8,128)(2,1)}, u32[]{:S(2)}) copy-start(bf16[1,8,8,32,128]{4,3,2,1,0:T(8,128)(2,1)} %param.4) | copy-start | bytes 1572868
  26.4 0.7 copy-start.5
  30.6 1.0 copy-start.4
  39.1 1.2 copy-start
  40.3 102.5 %all-reduce.5.cloned.1.call-start = ((), (), s32[]{:S(2)}) async-start(), calls=%async_computation.2 | async-start | bytes 884736 | tf_op jit(solution)/shard_map/psum | solution.py:93
  40.4 30.7 %collective-permute-start.3 = (bf16[1,2,8,32,128]{4,3,2,1,0:T(8,128)(2,1)S(1)}, bf16[1,2,8,32,128]{4,3,2,1,0:T(8,128)(2,1)S(1)}, u32[]{:S(2)}, u32[]{:S(2)}) collective-permute-start(bf16[1,2,8,32,128]{4,3,2,1,0:T(8,128)(2,1)S(1)} %slice.489), channel_id=1, source_target_pairs={{2,0},{4,2},{6,4},{3,1},{5,3},{7,5},{10,8},{12,10},{14,12},{11,9},... | collective-permute-start | bytes 393224 | tf_op jit(solution)/shard_map/ppermute | solution.py:12
  71.1 2.7 %collective-permute-start.4 = (bf16[1,10,1,32,128]{4,3,2,1,0:T(8,128)(2,1)S(1)}, bf16[1,10,1,32,128]{4,3,2,1,0:T(8,128)(2,1)S(1)}, u32[]{:S(2)}, u32[]{:S(2)}) collective-permute-start(bf16[1,10,1,32,128]{4,3,2,1,0:T(8,128)(2,1)S(1)} %get-tuple-element.55), channel_id=1, source_target_pairs={{0,1},{2,3},{4,5},{6,7},{8,9},{10,11},{12,13},{14,15},{16,17},{18,... | collective-permute-start | bytes 245768 | tf_op jit(solution)/shard_map/ppermute | solution.py:23
  72.4 3.2 %collective-permute-start.5 = (bf16[1,10,1,32,128]{4,3,2,1,0:T(8,128)(2,1)S(1)}, bf16[1,10,1,32,128]{4,3,2,1,0:T(8,128)(2,1)S(1)}, u32[]{:S(2)}, u32[]{:S(2)}) collective-permute-start(bf16[1,10,1,32,128]{4,3,2,1,0:T(8,128)(2,1)S(1)} %get-tuple-element.56), channel_id=1, source_target_pairs={{1,0},{3,2},{5,4},{7,6},{9,8},{11,10},{13,12},{15,14},{17,16},{19,... | collective-permute-start | bytes 245768 | tf_op jit(solution)/shard_map/ppermute | solution.py:25
  76.2 2.8 %copy-start.1 = (bf16[3,3,3,128,128]{3,4,2,1,0:T(8,128)(2,1)S(1)}, bf16[3,3,3,128,128]{3,4,2,1,0:T(8,128)(2,1)}, u32[]{:S(2)}) copy-start(bf16[3,3,3,128,128]{3,4,2,1,0:T(8,128)(2,1)} %copy.9) | copy-start | bytes 2654212
Sparse Core Ops, SparseCore 0:
  40.4 41.3 reduce-scatter.1
  92.3 50.4 all-reduce.4
where the time goes:
time: 152 us; the launch traced here: 151 us
  waiting for transfers between devices  50.1 us (33%)
  matrix products  29.7 us (20%)
  blocking collectives  28.8 us (19%)
  between operations  15.1 us (10%)
  local copies, waits for them, and re-layouts  12.7 us (8%)
  starting transfers between devices  11.4 us (8%)
  other arithmetic  3.75 us (2%)
    psum x1, waiting for transfers between devices, body(): lax.psum((local_weight, local_bias), ('tm', 'tile'))  45.5 us
    dot_general x9, matrix products, body(): jnp.einsum('bfrwk,kd->bfrwd', stacked, flipped[tap_time, tap_row], prefer...  17.7 us
    psum x1, blocking collectives, body(): lax.psum((local_weight, local_bias), ('tm', 'tile'))  16.6 us
    unnamed x1, blocking collectives  12.2 us
    dot_general x9, matrix products, body(): jnp.einsum('bfrwk,kd->bfrwd', stacked, weights[tap_time, tap_row], prefer...  6.37 us
    ppermute x2, starting transfers between devices, passed_along(): return lax.ppermute(block, axis, route)  6.14 us
    slice x3, local copies, waits for them, and re-layouts, stack_columns(): window[:, :, :, begin:begin + breadth]  6.14 us
    dot_general x9, matrix products, body(): jnp.einsum('bfrwk,bfrwd->kd', source, grad_pre, preferred_element_type=jn...  5.62 us
  transfers between devices with their start and end apart: 8, of which 3 were waited for; matrix products, arithmetic and copies ran while one was open for 16% of the time, Pallas kernels for 0%

commit v1 on v0

v1 whole, which is shorter than its diff:
```python
import functools
import math

import jax
import jax.numpy as jnp
from jax import lax
from jax.experimental import pallas as pl
from jax.experimental.pallas import tpu as pltpu
from jax.sharding import PartitionSpec as P

F32 = jnp.float32
BF16 = jnp.bfloat16


def shifted_columns(cells, breadth):
    count = cells.shape[0]
    wide = cells.astype(F32)
    column = lax.broadcasted_iota(jnp.int32, cells.shape, 0) % breadth
    left = jnp.where(column == 0, 0.0, pltpu.roll(wide, 1, 0))
    right = jnp.where(column == breadth - 1, 0.0, pltpu.roll(wide, count - 1, 0))
    return left.astype(BF16), cells, right.astype(BF16)


def fill_windows(windows, frame, inner, edge, tile):
    height, breadth, channels = inner.shape
    parts = shifted_columns(inner.reshape(height * breadth, channels), breadth)
    edges = shifted_columns(edge, breadth)
    for e in range(3):
        lanes = slice(e * channels, (e + 1) * channels)
        windows[frame, 1 : height + 1, :, lanes] = parts[e].reshape(height, breadth, channels)
        rim = edges[e]
        none = jnp.zeros_like(rim)
        windows[frame, 0, :, lanes] = jnp.where(tile == 0, none, rim)
        windows[frame, height + 1, :, lanes] = jnp.where(tile == 0, rim, none)


def window_block(windows, first, height):
    blocks = []
    for f in range(4):
        for b in range(3):
            block = windows[first + f, b : b + height]
            blocks.append(block.reshape(-1, block.shape[-1]))
    return jnp.concatenate(blocks, axis=1)


def forward_kernel(
    x, edge, before, kernel, bias, cotangent, block_out, grad_pre, edge_out, *rest, arranged
):
    outs, (windows, taps, grads) = rest[:-3], rest[-3:]
    frames, height, breadth, channels = x.shape
    area = height * breadth
    tile = lax.axis_index("tile")
    rows = 9 * channels
    taps[0 : 3 * rows, 0:channels] = kernel[...]
    taps[3 * rows :, 0:channels] = jnp.zeros((rows, channels), BF16)
    taps[0:rows, channels:] = jnp.zeros((rows, channels), BF16)
    taps[rows:, channels:] = kernel[...]
    for f in range(2):
        fill_windows(windows, f, before[f * height : (f + 1) * height], before[2 * height + f], tile)
    for f in range(frames):
        fill_windows(windows, f + 2, x[f], edge[f], tile)
    both = jnp.concatenate([bias[...], bias[...]], axis=1)
    total = jnp.zeros((1, channels), F32)
    for p in range(frames // 2):
        pre = both + jnp.dot(
            window_block(windows, 2 * p, height), taps[...], preferred_element_type=F32
        )
        for s in range(2):
            t = 2 * p + s
            part = pre[:, s * channels : (s + 1) * channels]
            sigma = jax.nn.sigmoid(part)
            source = x[t].reshape(area, channels).astype(F32)
            upstream = cotangent[t].reshape(area, channels).astype(F32)
            block_out[t] = (source + part * sigma).astype(BF16).reshape(height, breadth, channels)
            grad = (upstream * sigma * (1.0 + part * (1.0 - sigma))).astype(BF16)
            grads[p * area : (p + 1) * area, s * channels : (s + 1) * channels] = grad
            total = total + jnp.sum(grad.astype(F32), axis=0, keepdims=True)
            cube = grad.reshape(height, breadth, channels)
            grad_pre[t] = cube
            edge_out[t] = jnp.where(tile == 0, cube[height - 1], cube[0])
    turned = grads[...].T
    sums = [[None] * 9 for _ in range(3)]
    for b in range(3):
        for f in range(4):
            source = jnp.concatenate(
                [
                    windows[2 * p + f, b : b + height].reshape(area, 3 * channels)
                    for p in range(frames // 2)
                ],
                axis=0,
            )
            low = 0 if f < 3 else channels
            high = 2 * channels if f > 0 else channels
            product = jnp.dot(turned[low:high], source, preferred_element_type=F32)
            for e in range(3):
                for s in range(2):
                    a = f - s
                    if 0 <= a < 3:
                        piece = product[
                            s * channels - low : (s + 1) * channels - low,
                            e * channels : (e + 1) * channels,
                        ]
                        at = b * 3 + e
                        sums[a][at] = piece if sums[a][at] is None else sums[a][at] + piece
    if not arranged:
        for a in range(3):
            for at in range(9):
                outs[0][a * 9 + at] = sums[a][at].T.astype(BF16)
        outs[1][...] = total
        return
    kept, sent = outs
    count, half = kept.shape[0], kept.shape[1]
    share = 27 * channels // count
    me = lax.axis_index("dp")
    places = [place_of(me, j, count, tile) for j in range(count)]
    theirs = [place_of(me, j, count, 1 - tile) for j in range(count)]

    def put(j, start, rows):
        done = 0
        while done < rows.shape[0]:
            h = (start + done) // half
            stop = min(rows.shape[0], (h + 1) * half - start)
            at = start + done - h * half
            piece = rows[done:stop]

            @pl.when(tile == h)
            def _():
                kept[places[j], at : at + piece.shape[0]] = piece

            @pl.when(tile != h)
            def _():
                sent[theirs[j], at : at + piece.shape[0]] = piece

            done = stop

    for k in range(27):
        block = sums[k // 9][k % 9].T.astype(BF16)
        at = k * channels
        end = at + channels
        while at < end:
            j = at // share
            stop = min(end, (j + 1) * share)
            put(j, at - j * share, block[at - k * channels : stop - k * channels])
            at = stop
    pad = 2 * half - share
    line = jnp.concatenate([total, jnp.zeros((pad - 1, channels), F32)], axis=0).astype(BF16)
    for j in range(count):
        put(j, share, line)


def input_kernel(g, edge, after, kernel, cotangent, grad_input, windows, taps):
    frames, height, breadth, channels = g.shape
    area = height * breadth
    tile = lax.axis_index("tile")
    for f in range(4):
        for s in range(2):
            a = 2 - f + s
            for b in range(3):
                for e in range(3):
                    lanes = ((f * 3 + b) * 3 + e) * channels
                    where = (slice(s * channels, (s + 1) * channels), slice(lanes, lanes + channels))
                    if 0 <= a < 3:
                        k = ((a * 3 + 2 - b) * 3 + 2 - e) * channels
                        taps[where] = kernel[k : k + channels]
                    else:
                        taps[where] = jnp.zeros((channels, channels), BF16)
    for f in range(frames):
        fill_windows(windows, f, g[f], edge[f], tile)
    for f in range(2):
        fill_windows(
            windows, frames + f, after[f * height : (f + 1) * height], after[2 * height + f], tile
        )
    for p in range(frames // 2):
        back = lax.dot_general(
            window_block(windows, 2 * p, height),
            taps[...],
            (((1,), (1,)), ((), ())),
            preferred_element_type=F32,
        )
        for s in range(2):
            t = 2 * p + s
            part = back[:, s * channels : (s + 1) * channels].reshape(height, breadth, channels)
            grad_input[t] = (cotangent[t].astype(F32) + part).astype(BF16)


def bits_of(count):
    return count.bit_length() - 1


def place_of(me, shard, count, tile):
    apart = me ^ shard
    n = bits_of(count)
    plain = apart * 0
    turned = apart * 0
    for k in range(n):
        bit = (apart >> k) & 1
        plain = plain | (bit << (n - 1 - k))
        turned = turned | (bit << k)
    return jnp.where(tile == 0, plain, turned)


def exchange(block, axis, count, bits):
    route = []
    for i in range(count):
        for c in range(2):
            route.append((i * 2 + c, (i ^ bits[c]) * 2 + c))
    return lax.ppermute(block, (axis, "tile"), route)


def added(a, b):
    return (a.astype(F32) + b.astype(F32)).astype(BF16)


def passed_along(block, axis, distance):
    count = lax.axis_size(axis)
    route = [(i - distance, i) for i in range(count) if 0 <= i - distance < count]
    return lax.ppermute(block, axis, route)


def swapped(block):
    return lax.ppermute(block, "tile", [(0, 1), (1, 0)])


def body(activations, kernel, conv_bias, cotangent):
    clip_count, frames, height, breadth, channels = activations.shape
    x, upstream = activations[0], cotangent[0]
    tile = lax.axis_index("tile")
    shards = lax.axis_size("dp")
    steps = lax.axis_size("tm")
    share = 27 * channels // shards
    half = -(-(share + 1) // 32) * 16
    arranged = share % 32 == 0

    edge = swapped(jnp.where(tile == 0, x[:, height - 1], x[:, 0]))
    before = passed_along(
        jnp.concatenate(
            [x[frames - 2 :].reshape(2 * height, breadth, channels), edge[frames - 2 :]], axis=0
        ),
        "tm",
        1,
    )
    cells = jax.ShapeDtypeStruct(x.shape, BF16)
    lines = jax.ShapeDtypeStruct((frames, breadth, channels), BF16)
    if arranged:
        partial = [jax.ShapeDtypeStruct((shards, half, channels), BF16)] * 2
    else:
        partial = [
            jax.ShapeDtypeStruct((27, channels, channels), BF16),
            jax.ShapeDtypeStruct((1, channels), F32),
        ]
    scratch = [pltpu.VMEM((frames + 2, height + 2, breadth, 3 * channels), BF16)]
    block_out, grad_pre, grad_edge, *parts = pl.pallas_call(
        functools.partial(forward_kernel, arranged=arranged),
        out_shape=[cells, cells, lines] + partial,
        scratch_shapes=scratch
        + [
            pltpu.VMEM((36 * channels, 2 * channels), BF16),
            pltpu.VMEM((frames // 2 * height * breadth, 2 * channels), BF16),
        ],
        compiler_params=pltpu.CompilerParams(vmem_limit_bytes=40 * 2**20),
        name="forward_and_weights",
    )(x, edge, before, kernel, conv_bias.reshape(1, channels), upstream)
    if arranged:
        kept, sent = parts
    else:
        weight = parts[0].reshape(shards, share, channels)
        line = jnp.broadcast_to(parts[1].astype(BF16)[None], (shards, 1, channels))
        pad = jnp.zeros((shards, 2 * half - share - 1, channels), BF16)
        whole = jnp.concatenate([weight, line, pad], axis=1)
        me = lax.axis_index("dp")
        whole = whole.reshape(shards, 2, half, channels)
        kept, sent = (
            jnp.zeros((shards, half, channels), BF16)
            .at[place_of(me, jnp.arange(shards), shards, side)]
            .set(lax.dynamic_index_in_dim(whole, side, 1, False))
            for side in (tile, 1 - tile)
        )

    total = added(kept, swapped(sent))
    n = bits_of(shards)
    for k in range(n):
        middle = total.shape[0] // 2
        total = added(
            total[:middle], exchange(total[middle:], "dp", shards, (1 << k, 1 << (n - 1 - k)))
        )
    total = total[0]
    n = bits_of(steps)
    for k in range(n):
        total = added(total, exchange(total, "tm", steps, (1 << k, 1 << (n - 1 - k))))
    other = swapped(total)
    whole = jnp.where(
        tile == 0,
        jnp.concatenate([total, other], axis=0),
        jnp.concatenate([other, total], axis=0),
    ).astype(F32)

    edge = swapped(grad_edge)
    after = passed_along(
        jnp.concatenate(
            [grad_pre[:2].reshape(2 * height, breadth, channels), edge[:2]], axis=0
        ),
        "tm",
        -1,
    )
    grad_input = pl.pallas_call(
        input_kernel,
        out_shape=cells,
        scratch_shapes=scratch + [pltpu.VMEM((2 * channels, 36 * channels), BF16)],
        compiler_params=pltpu.CompilerParams(vmem_limit_bytes=32 * 2**20),
        cost_estimate=pl.CostEstimate(
            flops=2 * 27 * channels * channels * frames * height * breadth,
            bytes_accessed=8 * 2**20,
            transcendentals=0,
        ),
        name="input_gradient",
    )(grad_pre, edge, after, kernel, upstream)

    positions = (
        clip_count * frames * height * breadth * shards * steps * lax.axis_size("tile")
    )
    scale = 1.0 / math.sqrt(positions)
    bias_share = channels // shards
    bias_row = lax.dynamic_slice_in_dim(
        whole[share], lax.axis_index("dp") * bias_share, bias_share, 0
    )
    return block_out[None], grad_input[None], whole[:share] * scale, bias_row * scale


def solution(mesh):
    return jax.shard_map(
        body,
        mesh=mesh,
        in_specs=(P("dp", "tm", "tile", None, None), P(), P(), P("dp", "tm", "tile", None, None)),
        out_specs=(
            P("dp", "tm", "tile", None, None),
            P("dp", "tm", "tile", None, None),
            P("dp", None),
            P("dp"),
        ),
        check_vma=False,
    )
```

time: 152 us -> 59.8 us (0.39)
  matrix products: 29.7 us -> 0 us
  blocking collectives: 28.8 us -> 0 us
  waiting for transfers between devices: 50.1 us -> 25.6 us
  between operations: 15.1 us -> 0.78 us
  Pallas kernels: 0 us -> 12.7 us
  local copies, waits for them, and re-layouts: 12.7 us -> 2.95 us
  starting transfers between devices: 11.4 us -> 15.7 us
  other arithmetic: 3.75 us -> 1.75 us
    psum x1 -> x0, waiting for transfers between devices: 45.5 us -> none  [body(): lax.psum((local_weight, local_bias), ('tm', 'tile'))]
    dot_general x27 -> x0, matrix products: 29.7 us -> none  [the longest x9 17.7 us: body(): jnp.einsum('bfrwk,kd->bfrwd', stacked, flipped[tap_time, tap_row], prefer...]
    psum x1 -> x0, blocking collectives: 16.6 us -> none  [body(): lax.psum((local_weight, local_bias), ('tm', 'tile'))]
    ppermute x4 -> x8, waiting for transfers between devices: 1.81 us -> 18.1 us  [the longest x4 14.1 us: exchange(): return lax.ppermute(block, (axis, 'tile'), route)]
    pallas_call x0 -> x2, Pallas kernels: none -> 12.7 us  [the longest x1 9.2 us: body(): pl.pallas_call(functools.partial(forward_kernel, arranged=arranged), out_...]
    unnamed x1 -> x0, blocking collectives: 12.2 us -> none
    slice x6 -> x8, local copies, waits for them, and re-layouts: 7.15 us -> 0.05 us  [the longest x2 0.03 us: body(): total[middle:]]
    ppermute x2, waiting for transfers between devices: 2.73 us -> 7.57 us  [passed_along(): return lax.ppermute(block, axis, route)]
  transfers between devices with their start and end apart: 8 -> 10, of which waited for: 3 -> 9; matrix products, arithmetic and copies ran while one was open for 16% -> 0% of each run, Pallas kernels for 0% -> 6%
where the time goes in v1:
time: 59.8 us; the launch traced here: 59.5 us
  waiting for transfers between devices  25.6 us (43%)
  starting transfers between devices  15.7 us (26%)
  Pallas kernels  12.7 us (21%)
  local copies, waits for them, and re-layouts  2.95 us (5%)
  other arithmetic  1.75 us (3%)
  between operations  0.78 us (1%)
    ppermute x4, waiting for transfers between devices, exchange(): return lax.ppermute(block, (axis, 'tile'), route)  14.1 us
    pallas_call x1, Pallas kernels, body(): pl.pallas_call(functools.partial(forward_kernel, arranged=arranged), out_...  9.2 us
    ppermute x4, starting transfers between devices, exchange(): return lax.ppermute(block, (axis, 'tile'), route)  9.06 us
    ppermute x2, waiting for transfers between devices, passed_along(): return lax.ppermute(block, axis, route)  7.57 us
    ppermute x2, starting transfers between devices, passed_along(): return lax.ppermute(block, axis, route)  6.04 us
    ppermute x4, waiting for transfers between devices, swapped(): return lax.ppermute(block, 'tile', [(0, 1), (1, 0)])  3.94 us
    pallas_call x1, Pallas kernels, body(): pl.pallas_call(input_kernel, out_shape=cells, scratch_shapes=scratch + [p...  3.53 us
    unnamed x11, local copies, waits for them, and re-layouts  2.9 us
  transfers between devices with their start and end apart: 10, of which 9 were waited for; matrix products, arithmetic and copies ran while one was open for 0% of the time, Pallas kernels for 6%

profile of v1, /device:TPU:0, one launch (start us, length us, event | category | flops | bytes accessed | tf_op | source)
XLA Modules:
  0.0 59.5 jit_solution(7271326424691373963)
XLA Ops:
  0.6 0.0 copy-start
  0.7 1.2 %copy.12 = bf16[1,8,8,32,128]{4,3,1,2,0:T(8,128)(2,1)S(1)} copy(bf16[1,8,8,32,128]{4,3,2,1,0:T(8,128)(2,1)} %param.4) | data formatting | bytes 1048576 | tf_op args[0]
  1.9 0.0 slice-start
  1.9 0.5 collective-permute-start
  2.4 0.9 %collective-permute-done.edge = bf16[8,32,128]{2,1,0:T(8,128)(2,1)S(1)} collective-permute-done((bf16[8,32,128]{2,1,0:T(8,128)(2,1)S(1)}, bf16[8,32,128]{2,1,0:T(8,128)(2,1)S(1)}, u32[]{:S(2)}, u32[]{:S(2)}) %collective-permute-start) | collective-permute-done | bytes 65568 | tf_op jit(solution)/shard_map/ppermute | solution.py:221
  3.3 4.8 %collective-permute-start.1 = (bf16[18,32,128]{2,1,0:T(8,128)(2,1)S(1)}, bf16[18,32,128]{2,1,0:T(8,128)(2,1)S(1)}, u32[]{:S(2)}, u32[]{:S(2)}) collective-permute-start(bf16[18,32,128]{2,1,0:T(8,128)(2,1)S(1)} %pad_maximum_fusion), channel_id=1, source_target_pairs={{0,2},{2,4},{4,6},{1,3},{3,5},{5,7},{8,10},{10,12},{12,14},{9,11},... | collective-permute-start | bytes 442376 | tf_op jit(solution)/shard_map/ppermute | solution.py:217
  8.1 3.4 %collective-permute-done.1.before = bf16[18,32,128]{2,1,0:T(8,128)(2,1)S(1)} collective-permute-done((bf16[18,32,128]{2,1,0:T(8,128)(2,1)S(1)}, bf16[18,32,128]{2,1,0:T(8,128)(2,1)S(1)}, u32[]{:S(2)}, u32[]{:S(2)}) %collective-permute-start.1) | collective-permute-done | bytes 147488 | tf_op jit(solution)/shard_map/ppermute | solution.py:217
  11.5 0.6 %copy-done.4 = f32[128]{0:T(128)S(1)} copy-done((f32[128]{0:T(128)S(1)}, f32[128]{0:T(128)}, u32[]{:S(2)}) %copy-start.4) | copy-done | bytes 536
  12.2 1.0 %copy-done.2 = bf16[1,8,8,32,128]{4,3,2,1,0:T(8,128)(2,1)S(1)} copy-done((bf16[1,8,8,32,128]{4,3,2,1,0:T(8,128)(2,1)S(1)}, bf16[1,8,8,32,128]{4,3,2,1,0:T(8,128)(2,1)}, u32[]{:S(2)}) %copy-start.2) | copy-done | bytes 524312
  13.2 9.2 %forward_and_weights.1 = (bf16[8,8,32,128]{3,2,1,0:T(8,128)(2,1)}, bf16[8,8,32,128]{3,2,1,0:T(8,128)(2,1)S(1)}, bf16[8,32,128]{2,1,0:T(8,128)(2,1)S(1)}, bf16[4,...) custom-call(bf16[8,8,32,128]{3,2,1,0:T(8,128)(2,1)S(1)} %bitcast.16, bf16[8,32,128]{2,1,0:T(8,128)(2,1)S(1)} %collective-permute-done.edge, ...), custom_call_target="tpu_custom_call" | custom-call | tf_op jit(solution)/shard_map/forward_and_weights/pallas_call | solution.py:252
  22.4 0.0 collective-permute-start.4
  22.4 1.8 %collective-permute-done.4 = bf16[4,448,128]{2,1,0:T(8,128)(2,1)S(1)} collective-permute-done((bf16[4,448,128]{2,1,0:T(8,128)(2,1)S(1)}, bf16[4,448,128]{2,1,0:T(8,128)(2,1)S(1)}, u32[]{:S(2)}, u32[]{:S(2)}) %collective-permute-start.4) | collective-permute-done | bytes 458784 | tf_op jit(solution)/shard_map/ppermute | solution.py:221
  24.2 0.1 add_convert_fusion
  24.4 1.6 %collective-permute-start.5 = (bf16[2,448,128]{2,1,0:T(8,128)(2,1)S(1)}, bf16[2,448,128]{2,1,0:T(8,128)(2,1)S(1)}, u32[]{:S(2)}, u32[]{:S(2)}) collective-permute-start(bf16[2,448,128]{2,1,0:T(8,128)(2,1)S(1)} %slice.54), channel_id=1, source_target_pairs={{0,8},{1,17},{8,0},{9,25},{16,24},{17,1},{24,16},{25,9},{2,10},{3,... | collective-permute-start | bytes 688136 | tf_op jit(solution)/shard_map/ppermute | solution.py:207
  26.0 6.8 %collective-permute-done.5 = bf16[2,448,128]{2,1,0:T(8,128)(2,1)S(1)} collective-permute-done((bf16[2,448,128]{2,1,0:T(8,128)(2,1)S(1)}, bf16[2,448,128]{2,1,0:T(8,128)(2,1)S(1)}, u32[]{:S(2)}, u32[]{:S(2)}) %collective-permute-start.5) | collective-permute-done | bytes 229408 | tf_op jit(solution)/shard_map/ppermute | solution.py:207
  32.8 0.1 add_convert_fusion.1
  32.9 1.8 %collective-permute-start.6 = (bf16[1,448,128]{2,1,0:T(8,128)(2,1)S(1)}, bf16[1,448,128]{2,1,0:T(8,128)(2,1)S(1)}, u32[]{:S(2)}, u32[]{:S(2)}) collective-permute-start(bf16[1,448,128]{2,1,0:T(8,128)(2,1)S(1)} %slice.56), channel_id=1, source_target_pairs={{0,16},{1,9},{8,24},{9,1},{16,0},{17,25},{24,8},{25,17},{2,18},{3,... | collective-permute-start | bytes 344072 | tf_op jit(solution)/shard_map/ppermute | solution.py:207
  34.7 4.3 %collective-permute-done.6 = bf16[1,448,128]{2,1,0:T(8,128)(2,1)S(1)} collective-permute-done((bf16[1,448,128]{2,1,0:T(8,128)(2,1)S(1)}, bf16[1,448,128]{2,1,0:T(8,128)(2,1)S(1)}, u32[]{:S(2)}, u32[]{:S(2)}) %collective-permute-start.6) | collective-permute-done | bytes 114720 | tf_op jit(solution)/shard_map/ppermute | solution.py:207
  39.1 2.5 %collective-permute-start.7 = (bf16[448,128]{1,0:T(8,128)(2,1)S(1)}, bf16[448,128]{1,0:T(8,128)(2,1)S(1)}, u32[]{:S(2)}, u32[]{:S(2)}) collective-permute-start(bf16[448,128]{1,0:T(8,128)(2,1)S(1)} %fusion.1), channel_id=1, source_target_pairs={{0,2},{1,5},{2,0},{3,7},{4,6},{5,1},{6,4},{7,3},{8,10},{9,13},{10,... | collective-permute-start | bytes 344072 | tf_op jit(solution)/shard_map/ppermute | solution.py:207
  41.6 0.0 collective-permute-start.2
  41.6 0.0 copy-start.3
  41.6 1.2 %collective-permute-done.2.edge = bf16[8,32,128]{2,1,0:T(8,128)(2,1)S(1)} collective-permute-done((bf16[8,32,128]{2,1,0:T(8,128)(2,1)S(1)}, bf16[8,32,128]{2,1,0:T(8,128)(2,1)S(1)}, u32[]{:S(2)}, u32[]{:S(2)}) %collective-permute-start.2) | collective-permute-done | bytes 65568 | tf_op jit(solution)/shard_map/ppermute | solution.py:221
  42.9 1.5 %collective-permute-done.7 = bf16[448,128]{1,0:T(8,128)(2,1)S(1)} collective-permute-done((bf16[448,128]{1,0:T(8,128)(2,1)S(1)}, bf16[448,128]{1,0:T(8,128)(2,1)S(1)}, u32[]{:S(2)}, u32[]{:S(2)}) %collective-permute-start.7) | collective-permute-done | bytes 114720 | tf_op jit(solution)/shard_map/ppermute | solution.py:207
  44.4 3.1 %collective-permute-start.8 = (bf16[448,128]{1,0:T(8,128)(2,1)S(1)}, bf16[448,128]{1,0:T(8,128)(2,1)S(1)}, u32[]{:S(2)}, u32[]{:S(2)}) collective-permute-start(bf16[448,128]{1,0:T(8,128)(2,1)S(1)} %add_convert_fusion.3), channel_id=1, source_target_pairs={{0,4},{1,3},{2,6},{3,1},{4,0},{5,7},{6,2},{7,5},{8,12},{9,11},{10,... | collective-permute-start | bytes 344072 | tf_op jit(solution)/shard_map/ppermute | solution.py:207
  47.5 1.3 %collective-permute-start.3 = (bf16[18,32,128]{2,1,0:T(8,128)(2,1)S(1)}, bf16[18,32,128]{2,1,0:T(8,128)(2,1)S(1)}, u32[]{:S(2)}, u32[]{:S(2)}) collective-permute-start(bf16[18,32,128]{2,1,0:T(8,128)(2,1)S(1)} %pad_maximum_fusion.1), channel_id=1, source_target_pairs={{2,0},{4,2},{6,4},{3,1},{5,3},{7,5},{10,8},{12,10},{14,12},{11,9},... | collective-permute-start | bytes 442376 | tf_op jit(solution)/shard_map/ppermute | solution.py:217
  48.8 1.5 %collective-permute-done.8 = bf16[448,128]{1,0:T(8,128)(2,1)S(1)} collective-permute-done((bf16[448,128]{1,0:T(8,128)(2,1)S(1)}, bf16[448,128]{1,0:T(8,128)(2,1)S(1)}, u32[]{:S(2)}, u32[]{:S(2)}) %collective-permute-start.8) | collective-permute-done | bytes 114720 | tf_op jit(solution)/shard_map/ppermute | solution.py:207
  50.3 0.1 collective-permute-start.9
  50.4 4.2 %collective-permute-done.3.after = bf16[18,32,128]{2,1,0:T(8,128)(2,1)S(1)} collective-permute-done((bf16[18,32,128]{2,1,0:T(8,128)(2,1)S(1)}, bf16[18,32,128]{2,1,0:T(8,128)(2,1)S(1)}, u32[]{:S(2)}, u32[]{:S(2)}) %collective-permute-start.3) | collective-permute-done | bytes 147488 | tf_op jit(solution)/shard_map/ppermute | solution.py:217
  54.6 3.5 %input_gradient.1 = bf16[8,8,32,128]{3,2,1,0:T(8,128)(2,1)} custom-call(bf16[8,8,32,128]{3,2,1,0:T(8,128)(2,1)S(1)} %get-tuple-element.10.g, bf16[8,32,128]{2,1,0:T(8,128)(2,1)S(1)} %collective-permute-done.2.edge, bf16[18,32,128]{2,1,0:T(8,128)(2,1)S(1)} %collective-permute-done.3.after, bf16[3456,128]{1,0:T(8,128)(2,1)S(1)} %copy-done.1, ...), custom_call_target="tpu_custom_call" | custom-call | flops 1811939328 | bytes 8388608 | tf_op jit(solution)/shard_map/input_gradient/pallas_call | solution.py:305
  58.1 0.0 collective-permute-done.9
  58.2 0.8 %slice_multiply_fusion = f32[864,128]{1,0:T(8,128)} fusion(f32[896,128]{1,0:T(8,128)S(1)} %fusion), kind=kLoop, calls=%fused_computation.3 | loop fusion | flops 110592 | bytes 884736 | tf_op jit(solution)/shard_map/mul | solution.py:326
  58.9 0.6 multiply_bitcast_fusion
  (20 shorter events, 0.2 us)
Async XLA Ops:
  0.6 10.9 %copy-start = (bf16[1,8,8,32,128]{4,3,2,1,0:T(8,128)(2,1)S(1)}, bf16[1,8,8,32,128]{4,3,2,1,0:T(8,128)(2,1)}, u32[]{:S(2)}) copy-start(bf16[1,8,8,32,128]{4,3,2,1,0:T(8,128)(2,1)} %param.4) | copy-start | bytes 1572868
  0.6 10.9 %copy-start.1 = (bf16[3456,128]{1,0:T(8,128)(2,1)S(1)}, bf16[3456,128]{1,0:T(8,128)(2,1)}, u32[]{:S(2)}) copy-start(bf16[3456,128]{1,0:T(8,128)(2,1)} %kernel.3) | copy-start | bytes 2654212
  1.9 1.4 %slice-start = ((bf16[1,8,8,32,128]{4,3,2,1,0:T(8,128)(2,1)}), bf16[1,2,8,32,128]{4,3,2,1,0:T(8,128)(2,1)S(1)}, s32[]{:S(2)}) async-start(bf16[1,8,8,32,128]{4,3,2,1,0:T(8,128)(2,1)} %param.4), calls=%async_computation | async-start | bytes 262144 | tf_op jit(solution)/shard_map/slice | solution.py:237
  1.9 1.4 %collective-permute-start = (bf16[8,32,128]{2,1,0:T(8,128)(2,1)S(1)}, bf16[8,32,128]{2,1,0:T(8,128)(2,1)S(1)}, u32[]{:S(2)}, u32[]{:S(2)}) collective-permute-start(bf16[8,32,128]{2,1,0:T(8,128)(2,1)S(1)} %fusion.2), channel_id=1, source_target_pairs={{0,1},{1,0},{2,3},{3,2},{4,5},{5,4},{6,7},{7,6},{8,9},{9,8},{10,11... | collective-permute-start | bytes 196616 | tf_op jit(solution)/shard_map/ppermute | solution.py:221
  3.3 8.2 %collective-permute-start.1 = (bf16[18,32,128]{2,1,0:T(8,128)(2,1)S(1)}, bf16[18,32,128]{2,1,0:T(8,128)(2,1)S(1)}, u32[]{:S(2)}, u32[]{:S(2)}) collective-permute-start(bf16[18,32,128]{2,1,0:T(8,128)(2,1)S(1)} %pad_maximum_fusion), channel_id=1, source_target_pairs={{0,2},{2,4},{4,6},{1,3},{3,5},{5,7},{8,10},{10,12},{12,14},{9,11},... | collective-permute-start | bytes 442376 | tf_op jit(solution)/shard_map/ppermute | solution.py:217
  11.5 0.7 %copy-start.4 = (f32[128]{0:T(128)S(1)}, f32[128]{0:T(128)}, u32[]{:S(2)}) copy-start(f32[128]{0:T(128)} %param.6) | copy-start | bytes 1540
  12.2 1.0 %copy-start.2 = (bf16[1,8,8,32,128]{4,3,2,1,0:T(8,128)(2,1)S(1)}, bf16[1,8,8,32,128]{4,3,2,1,0:T(8,128)(2,1)}, u32[]{:S(2)}) copy-start(bf16[1,8,8,32,128]{4,3,2,1,0:T(8,128)(2,1)} %param.7) | copy-start | bytes 1572868
  22.4 1.8 %collective-permute-start.4 = (bf16[4,448,128]{2,1,0:T(8,128)(2,1)S(1)}, bf16[4,448,128]{2,1,0:T(8,128)(2,1)S(1)}, u32[]{:S(2)}, u32[]{:S(2)}) collective-permute-start(bf16[4,448,128]{2,1,0:T(8,128)(2,1)S(1)} %get-tuple-element.13), channel_id=1, source_target_pairs={{0,1},{1,0},{2,3},{3,2},{4,5},{5,4},{6,7},{7,6},{8,9},{9,8},{10,11... | collective-permute-start | bytes 1376264 | tf_op jit(solution)/shard_map/ppermute | solution.py:221
  24.4 8.5 %collective-permute-start.5 = (bf16[2,448,128]{2,1,0:T(8,128)(2,1)S(1)}, bf16[2,448,128]{2,1,0:T(8,128)(2,1)S(1)}, u32[]{:S(2)}, u32[]{:S(2)}) collective-permute-start(bf16[2,448,128]{2,1,0:T(8,128)(2,1)S(1)} %slice.54), channel_id=1, source_target_pairs={{0,8},{1,17},{8,0},{9,25},{16,24},{17,1},{24,16},{25,9},{2,10},{3,... | collective-permute-start | bytes 688136 | tf_op jit(solution)/shard_map/ppermute | solution.py:207
  32.9 6.1 %collective-permute-start.6 = (bf16[1,448,128]{2,1,0:T(8,128)(2,1)S(1)}, bf16[1,448,128]{2,1,0:T(8,128)(2,1)S(1)}, u32[]{:S(2)}, u32[]{:S(2)}) collective-permute-start(bf16[1,448,128]{2,1,0:T(8,128)(2,1)S(1)} %slice.56), channel_id=1, source_target_pairs={{0,16},{1,9},{8,24},{9,1},{16,0},{17,25},{24,8},{25,17},{2,18},{3,... | collective-permute-start | bytes 344072 | tf_op jit(solution)/shard_map/ppermute | solution.py:207
  39.1 5.3 %collective-permute-start.7 = (bf16[448,128]{1,0:T(8,128)(2,1)S(1)}, bf16[448,128]{1,0:T(8,128)(2,1)S(1)}, u32[]{:S(2)}, u32[]{:S(2)}) collective-permute-start(bf16[448,128]{1,0:T(8,128)(2,1)S(1)} %fusion.1), channel_id=1, source_target_pairs={{0,2},{1,5},{2,0},{3,7},{4,6},{5,1},{6,4},{7,3},{8,10},{9,13},{10,... | collective-permute-start | bytes 344072 | tf_op jit(solution)/shard_map/ppermute | solution.py:207
  41.6 1.3 %collective-permute-start.2 = (bf16[8,32,128]{2,1,0:T(8,128)(2,1)S(1)}, bf16[8,32,128]{2,1,0:T(8,128)(2,1)S(1)}, u32[]{:S(2)}, u32[]{:S(2)}) collective-permute-start(bf16[8,32,128]{2,1,0:T(8,128)(2,1)S(1)} %get-tuple-element.11), channel_id=1, source_target_pairs={{0,1},{1,0},{2,3},{3,2},{4,5},{5,4},{6,7},{7,6},{8,9},{9,8},{10,11... | collective-permute-start | bytes 196616 | tf_op jit(solution)/shard_map/ppermute | solution.py:221
  41.6 12.9 %copy-start.3 = (bf16[1,8,8,32,128]{4,3,2,1,0:T(8,128)(2,1)S(1)}, bf16[1,8,8,32,128]{4,3,2,1,0:T(8,128)(2,1)}, u32[]{:S(2)}) copy-start(bf16[1,8,8,32,128]{4,3,2,1,0:T(8,128)(2,1)} %param.7) | copy-start | bytes 1572868
  44.4 5.9 %collective-permute-start.8 = (bf16[448,128]{1,0:T(8,128)(2,1)S(1)}, bf16[448,128]{1,0:T(8,128)(2,1)S(1)}, u32[]{:S(2)}, u32[]{:S(2)}) collective-permute-start(bf16[448,128]{1,0:T(8,128)(2,1)S(1)} %add_convert_fusion.3), channel_id=1, source_target_pairs={{0,4},{1,3},{2,6},{3,1},{4,0},{5,7},{6,2},{7,5},{8,12},{9,11},{10,... | collective-permute-start | bytes 344072 | tf_op jit(solution)/shard_map/ppermute | solution.py:207
  47.5 7.0 %collective-permute-start.3 = (bf16[18,32,128]{2,1,0:T(8,128)(2,1)S(1)}, bf16[18,32,128]{2,1,0:T(8,128)(2,1)S(1)}, u32[]{:S(2)}, u32[]{:S(2)}) collective-permute-start(bf16[18,32,128]{2,1,0:T(8,128)(2,1)S(1)} %pad_maximum_fusion.1), channel_id=1, source_target_pairs={{2,0},{4,2},{6,4},{3,1},{5,3},{7,5},{10,8},{12,10},{14,12},{11,9},... | collective-permute-start | bytes 442376 | tf_op jit(solution)/shard_map/ppermute | solution.py:217
  50.3 7.8 %collective-permute-start.9 = (bf16[448,128]{1,0:T(8,128)(2,1)S(1)}, bf16[448,128]{1,0:T(8,128)(2,1)S(1)}, u32[]{:S(2)}, u32[]{:S(2)}) collective-permute-start(bf16[448,128]{1,0:T(8,128)(2,1)S(1)} %add_convert_fusion.2), channel_id=1, source_target_pairs={{0,1},{1,0},{2,3},{3,2},{4,5},{5,4},{6,7},{7,6},{8,9},{9,8},{10,11... | collective-permute-start | bytes 344072 | tf_op jit(solution)/shard_map/ppermute | solution.py:221

commit v2 on v1

v2 whole, which is shorter than its diff:
```python
import functools
import math

import jax
import jax.numpy as jnp
from jax import lax
from jax.experimental import pallas as pl
from jax.experimental.pallas import tpu as pltpu
from jax.sharding import PartitionSpec as P

F32 = jnp.float32
BF16 = jnp.bfloat16


def shifted_columns(cells, breadth):
    count = cells.shape[0]
    wide = cells.astype(F32)
    column = lax.broadcasted_iota(jnp.int32, cells.shape, 0) % breadth
    left = jnp.where(column == 0, 0.0, pltpu.roll(wide, 1, 0))
    right = jnp.where(column == breadth - 1, 0.0, pltpu.roll(wide, count - 1, 0))
    return left.astype(BF16), cells, right.astype(BF16)


def fill_windows(windows, frame, inner, edge, tile):
    height, breadth, channels = inner.shape
    parts = shifted_columns(inner.reshape(height * breadth, channels), breadth)
    edges = shifted_columns(edge, breadth)
    for e in range(3):
        lanes = slice(e * channels, (e + 1) * channels)
        windows[frame, 1 : height + 1, :, lanes] = parts[e].reshape(height, breadth, channels)
        rim = edges[e]
        none = jnp.zeros_like(rim)
        windows[frame, 0, :, lanes] = jnp.where(tile == 0, none, rim)
        windows[frame, height + 1, :, lanes] = jnp.where(tile == 0, rim, none)


def window_rows(pieces, frame, b, height):
    for first, ref in pieces:
        if first <= frame < first + ref.shape[0]:
            block = ref[frame - first, b : b + height]
            return block.reshape(-1, block.shape[-1])


def window_block(pieces, first, height):
    return jnp.concatenate(
        [window_rows(pieces, first + f, b, height) for f in range(4) for b in range(3)], axis=1
    )


def activate(pre, source, upstream):
    sigma = jax.nn.sigmoid(pre)
    result = (source.astype(F32) + pre * sigma).astype(BF16)
    grad = (upstream.astype(F32) * sigma * (1.0 + pre * (1.0 - sigma))).astype(BF16)
    return result, grad


def forward_pair(pieces, p, taps, bias, x_pair, upstream, height):
    channels = bias.shape[1]
    both = jnp.concatenate([bias[...], bias[...]], axis=1)
    pre = both + jnp.dot(
        window_block(pieces, 2 * p, height), taps[...], preferred_element_type=F32
    )
    return [
        activate(
            pre[:, s * channels : (s + 1) * channels],
            x_pair[s].reshape(-1, channels),
            upstream[s].reshape(-1, channels),
        )
        for s in range(2)
    ]


def interior_kernel(
    x,
    edge,
    kernel,
    bias,
    cotangent,
    block_out,
    windows,
    taps,
    turned,
    grad_pre,
    edge_out,
    total,
    bias_here,
    upstream,
    result,
    arriving,
    leaving,
):
    frames, height, breadth, channels = x.shape
    area = height * breadth
    tile = lax.axis_index("tile")
    bias_copy = pltpu.make_async_copy(bias, bias_here, arriving.at[0])
    up_copy = pltpu.make_async_copy(cotangent.at[2:frames], upstream, arriving.at[1])
    bias_copy.start()
    up_copy.start()
    rows = 9 * channels
    taps[0 : 3 * rows, 0:channels] = kernel[...]
    taps[3 * rows :, 0:channels] = jnp.zeros((rows, channels), BF16)
    taps[0:rows, channels:] = jnp.zeros((rows, channels), BF16)
    taps[rows:, channels:] = kernel[...]
    for f in range(frames):
        fill_windows(windows, f, x[f], edge[f], tile)
    bias_copy.wait()
    up_copy.wait()
    summed = jnp.zeros((1, channels), F32)
    copies = []
    for p in range(1, frames // 2):
        grads = []
        outs = forward_pair(
            [(2, windows)],
            p,
            taps,
            bias_here,
            [x[2 * p], x[2 * p + 1]],
            [upstream[2 * p - 2], upstream[2 * p - 1]],
            height,
        )
        for s in range(2):
            t = 2 * p + s - 2
            result[t] = outs[s][0].reshape(height, breadth, channels)
            grad = outs[s][1]
            grads.append(grad)
            summed = summed + jnp.sum(grad.astype(F32), axis=0, keepdims=True)
            cube = grad.reshape(height, breadth, channels)
            grad_pre[t] = cube
            edge_out[t] = jnp.where(tile == 0, cube[height - 1], cube[0])
        turned[:, (p - 1) * area : p * area] = jnp.concatenate(grads, axis=1).T
        copy = pltpu.make_async_copy(
            result.at[2 * p - 2 : 2 * p], block_out.at[2 * p : 2 * p + 2], leaving.at[p - 1]
        )
        copy.start()
        copies.append(copy)
    total[...] = summed
    for copy in copies:
        copy.wait()


def first_frames_kernel(
    block_in,
    x,
    edge,
    before,
    bias,
    cotangent,
    windows,
    taps,
    turned,
    edge_in,
    total,
    block_out,
    grad_pre,
    edge_out,
    *rest,
    arranged,
):
    outs, (early, bias_here, upstream, result, arriving, leaving) = rest[:-6], rest[-6:]
    frames, height, breadth, channels = x.shape
    area = height * breadth
    tile = lax.axis_index("tile")
    bias_copy = pltpu.make_async_copy(bias, bias_here, arriving.at[0])
    up_copy = pltpu.make_async_copy(cotangent.at[0:2], upstream, arriving.at[1])
    bias_copy.start()
    up_copy.start()
    for f in range(2):
        fill_windows(early, f, before[f * height : (f + 1) * height], before[2 * height + f], tile)
    bias_copy.wait()
    up_copy.wait()
    pieces = [(0, early), (2, windows)]
    summed = total[...]
    firsts = forward_pair(
        pieces, 0, taps, bias_here, [x[0], x[1]], [upstream[0], upstream[1]], height
    )
    for s in range(2):
        result[s] = firsts[s][0].reshape(height, breadth, channels)
        cube = firsts[s][1].reshape(height, breadth, channels)
        summed = summed + jnp.sum(firsts[s][1].astype(F32), axis=0, keepdims=True)
        grad_pre[s] = cube
        edge_out[s] = jnp.where(tile == 0, cube[height - 1], cube[0])
    edge_out[2:frames] = edge_in[...]
    copy = pltpu.make_async_copy(result, block_out.at[0:2], leaving)
    copy.start()
    grads = jnp.concatenate(
        [jnp.concatenate([firsts[0][1], firsts[1][1]], axis=1).T, turned[...]], axis=1
    )
    sums = [[None] * 9 for _ in range(3)]
    for b in range(3):
        for f in range(4):
            source = jnp.concatenate(
                [window_rows(pieces, 2 * p + f, b, height) for p in range(frames // 2)], axis=0
            )
            low = 0 if f < 3 else channels
            high = 2 * channels if f > 0 else channels
            product = jnp.dot(grads[low:high], source, preferred_element_type=F32)
            for e in range(3):
                for s in range(2):
                    a = f - s
                    if 0 <= a < 3:
                        piece = product[
                            s * channels - low : (s + 1) * channels - low,
                            e * channels : (e + 1) * channels,
                        ]
                        at = b * 3 + e
                        sums[a][at] = piece if sums[a][at] is None else sums[a][at] + piece
    if not arranged:
        for k in range(27):
            outs[0][k] = sums[k // 9][k % 9].T.astype(BF16)
        outs[1][...] = summed
        copy.wait()
        return
    (parts,) = outs
    count, half = parts.shape[1], parts.shape[2]
    share = 27 * channels // count
    me = lax.axis_index("dp")

    def put(j, start, rows):
        done = 0
        while done < rows.shape[0]:
            h = (start + done) // half
            stop = min(rows.shape[0], (h + 1) * half - start)
            at = start + done - h * half
            place = place_of(me, j, count, h)
            parts[tile ^ h, place, at : at + stop - done] = rows[done:stop]
            done = stop

    for k in range(27):
        block = sums[k // 9][k % 9].astype(BF16).T
        at = k * channels
        end = at + channels
        while at < end:
            j = at // share
            stop = min(end, (j + 1) * share)
            put(j, at - j * share, block[at - k * channels : stop - k * channels])
            at = stop
    pad = 2 * half - share
    line = jnp.concatenate([summed, jnp.zeros((pad - 1, channels), F32)], axis=0).astype(BF16)
    for j in range(count):
        put(j, share, line)
    copy.wait()


def back_pair(pieces, p, taps, upstream, height):
    back = lax.dot_general(
        window_block(pieces, 2 * p, height),
        taps[...],
        (((1,), (1,)), ((), ())),
        preferred_element_type=F32,
    )
    channels = back.shape[1] // 2
    return [
        (
            upstream[s].astype(F32)
            + back[:, s * channels : (s + 1) * channels].reshape(upstream[s].shape)
        ).astype(BF16)
        for s in range(2)
    ]


def back_interior_kernel(
    early, g, edge, kernel, cotangent, grad_input, last, taps, windows, upstream, result, arriving, leaving
):
    frames, height, breadth, channels = cotangent.shape
    tile = lax.axis_index("tile")
    up_copy = pltpu.make_async_copy(cotangent.at[0 : frames - 2], upstream, arriving)
    up_copy.start()
    for f in range(4):
        for s in range(2):
            a = 2 - f + s
            for b in range(3):
                for e in range(3):
                    lanes = ((f * 3 + b) * 3 + e) * channels
                    where = (slice(s * channels, (s + 1) * channels), slice(lanes, lanes + channels))
                    if 0 <= a < 3:
                        k = ((a * 3 + 2 - b) * 3 + 2 - e) * channels
                        taps[where] = kernel[k : k + channels]
                    else:
                        taps[where] = jnp.zeros((channels, channels), BF16)
    for f in range(frames):
        cells = early[f] if f < 2 else g[f - 2]
        if f < frames - 2:
            fill_windows(windows, f, cells, edge[f], tile)
        else:
            fill_windows(last, f - (frames - 2), cells, edge[f], tile)
    up_copy.wait()
    copies = []
    for p in range(frames // 2 - 1):
        pair = back_pair(
            [(0, windows), (frames - 2, last)],
            p,
            taps,
            [upstream[2 * p], upstream[2 * p + 1]],
            height,
        )
        for s in range(2):
            result[2 * p + s] = pair[s]
        copy = pltpu.make_async_copy(
            result.at[2 * p : 2 * p + 2], grad_input.at[2 * p : 2 * p + 2], leaving.at[p]
        )
        copy.start()
        copies.append(copy)
    for copy in copies:
        copy.wait()


def back_last_kernel(
    grad_in, last, after, taps, cotangent, grad_input, windows, upstream, result, arriving, leaving
):
    frames, height, breadth, channels = cotangent.shape
    tile = lax.axis_index("tile")
    up_copy = pltpu.make_async_copy(cotangent.at[frames - 2 : frames], upstream, arriving)
    up_copy.start()
    for f in range(2):
        fill_windows(windows, f, after[f * height : (f + 1) * height], after[2 * height + f], tile)
    up_copy.wait()
    pair = back_pair(
        [(frames - 2, last), (frames, windows)],
        frames // 2 - 1,
        taps,
        [upstream[0], upstream[1]],
        height,
    )
    for s in range(2):
        result[s] = pair[s]
    copy = pltpu.make_async_copy(result, grad_input.at[frames - 2 : frames], leaving)
    copy.start()
    copy.wait()


def bits_of(count):
    return count.bit_length() - 1


def place_of(me, shard, count, tile):
    apart = me ^ shard
    n = bits_of(count)
    plain = apart * 0
    turned = apart * 0
    for k in range(n):
        bit = (apart >> k) & 1
        plain = plain | (bit << (n - 1 - k))
        turned = turned | (bit << k)
    return jnp.where(tile == 0, plain, turned)


def exchange(block, axis, count, bits):
    route = []
    for i in range(count):
        for c in range(2):
            route.append((i * 2 + c, (i ^ bits[c]) * 2 + c))
    return lax.ppermute(block, (axis, "tile"), route)


def added(a, b):
    return (a.astype(F32) + b.astype(F32)).astype(BF16)


def passed_along(block, axis, distance):
    count = lax.axis_size(axis)
    route = [(i - distance, i) for i in range(count) if 0 <= i - distance < count]
    return lax.ppermute(block, axis, route)


def swapped(block):
    return lax.ppermute(block, "tile", [(0, 1), (1, 0)])


def body(activations, kernel, conv_bias, cotangent):
    clip_count, frames, height, breadth, channels = activations.shape
    x, upstream = activations[0], cotangent[0]
    tile = lax.axis_index("tile")
    shards = lax.axis_size("dp")
    steps = lax.axis_size("tm")
    share = 27 * channels // shards
    half = -(-(share + 1) // 32) * 16
    arranged = share % 32 == 0

    row = jnp.where(tile == 0, height - 1, 0)
    edge = swapped(lax.dynamic_index_in_dim(x, row, 1, False))
    before = passed_along(
        jnp.concatenate(
            [x[frames - 2 :].reshape(2 * height, breadth, channels), edge[frames - 2 :]], axis=0
        ),
        "tm",
        1,
    )
    area = height * breadth
    bias = conv_bias.reshape(1, channels)
    cells = jax.ShapeDtypeStruct(x.shape, BF16)

    def arrays(*shapes, kind=BF16):
        return [jax.ShapeDtypeStruct(shape, kind) for shape in shapes]

    def windows_shape(count):
        return (count, height + 2, breadth, 3 * channels)

    def frames_shape(count):
        return (count, height, breadth, channels)

    def call(kernel_body, name, share, shapes, scratch, far_in, far_out, args, aliases=None):
        here, there = pl.BlockSpec(memory_space=pltpu.VMEM), pl.BlockSpec(memory_space=pltpu.HBM)
        return pl.pallas_call(
            kernel_body,
            out_shape=shapes,
            in_specs=[there if i in far_in else here for i in range(len(args))],
            out_specs=[there if i in far_out else here for i in range(len(shapes))],
            scratch_shapes=scratch,
            input_output_aliases=aliases or {},
            compiler_params=pltpu.CompilerParams(vmem_limit_bytes=32 * 2**20),
            cost_estimate=pl.CostEstimate(
                flops=int(share * 4 * 27 * channels * channels * frames * area),
                bytes_accessed=4 * 2**20,
                transcendentals=0,
            ),
            name=name,
        )(*args)

    dma, vmem = pltpu.SemaphoreType.DMA, pltpu.VMEM
    block_out, windows, taps, turned, later_grads, later_edge, total = call(
        interior_kernel,
        "forward_interior",
        0.75,
        [cells]
        + arrays(
            windows_shape(frames),
            (36 * channels, 2 * channels),
            (2 * channels, (frames // 2 - 1) * area),
            frames_shape(frames - 2),
            (frames - 2, breadth, channels),
        )
        + arrays((1, channels), kind=F32),
        [
            vmem((1, channels), F32),
            vmem(frames_shape(frames - 2), BF16),
            vmem(frames_shape(frames - 2), BF16),
            dma((2,)),
            dma((frames // 2 - 1,)),
        ],
        (3, 4),
        (0,),
        (x, edge, kernel, bias, upstream),
    )
    if arranged:
        partial = arrays((2, shards, half, channels))
    else:
        partial = arrays((27, channels, channels)) + arrays((1, channels), kind=F32)
    block_out, early_grads, grad_edge, *parts = call(
        functools.partial(first_frames_kernel, arranged=arranged),
        "first_frames_and_weights",
        1.25,
        [cells] + arrays(frames_shape(2), (frames, breadth, channels)) + partial,
        [
            vmem(windows_shape(2), BF16),
            vmem((1, channels), F32),
            vmem(frames_shape(2), BF16),
            vmem(frames_shape(2), BF16),
            dma((2,)),
            dma,
        ],
        (0, 4, 5),
        (0,),
        (
            block_out,
            x,
            edge,
            before,
            bias,
            upstream,
            windows,
            taps,
            turned,
            later_edge,
            total,
        ),
        {0: 0},
    )
    if arranged:
        kept, sent = parts[0][0], parts[0][1]
    else:
        weight = parts[0].reshape(shards, share, channels)
        line = jnp.broadcast_to(parts[1].astype(BF16)[None], (shards, 1, channels))
        pad = jnp.zeros((shards, 2 * half - share - 1, channels), BF16)
        whole = jnp.concatenate([weight, line, pad], axis=1)
        me = lax.axis_index("dp")
        whole = whole.reshape(shards, 2, half, channels)
        kept, sent = (
            jnp.zeros((shards, half, channels), BF16)
            .at[place_of(me, jnp.arange(shards), shards, side)]
            .set(lax.dynamic_index_in_dim(whole, side, 1, False))
            for side in (tile, 1 - tile)
        )

    total = added(kept, swapped(sent))
    edge = swapped(grad_edge)
    after = passed_along(
        jnp.concatenate(
            [early_grads.reshape(2 * height, breadth, channels), edge[:2]], axis=0
        ),
        "tm",
        -1,
    )
    grad_input, last, taps = call(
        back_interior_kernel,
        "input_gradient_interior",
        0.75,
        [cells] + arrays(windows_shape(2), (2 * channels, 36 * channels)),
        [
            vmem(windows_shape(frames - 2), BF16),
            vmem(frames_shape(frames - 2), BF16),
            vmem(frames_shape(frames - 2), BF16),
            dma,
            dma((frames // 2 - 1,)),
        ],
        (4,),
        (0,),
        (early_grads, later_grads, edge, kernel, upstream),
    )
    n = bits_of(shards)
    for k in range(n):
        if k == n - 1:
            total, grad_input = lax.optimization_barrier((total, grad_input))
        middle = total.shape[0] // 2
        total = added(
            total[:middle], exchange(total[middle:], "dp", shards, (1 << k, 1 << (n - 1 - k)))
        )
    (grad_input,) = call(
        back_last_kernel,
        "input_gradient_last",
        0.25,
        [cells],
        [
            vmem(windows_shape(2), BF16),
            vmem(frames_shape(2), BF16),
            vmem(frames_shape(2), BF16),
            dma,
            dma,
        ],
        (0, 4),
        (0,),
        (grad_input, last, after, taps, upstream),
        {0: 0},
    )
    total = total[0]
    n = bits_of(steps)
    for k in range(n):
        if k == n - 1:
            total, grad_input = lax.optimization_barrier((total, grad_input))
        total = added(total, exchange(total, "tm", steps, (1 << k, 1 << (n - 1 - k))))
    other = swapped(total)
    whole = jnp.where(
        tile == 0,
        jnp.concatenate([total, other], axis=0),
        jnp.concatenate([other, total], axis=0),
    ).astype(F32)

    positions = (
        clip_count * frames * height * breadth * shards * steps * lax.axis_size("tile")
    )
    scale = 1.0 / math.sqrt(positions)
    bias_share = channels // shards
    bias_row = lax.dynamic_slice_in_dim(
        whole[share], lax.axis_index("dp") * bias_share, bias_share, 0
    )
    return block_out[None], grad_input[None], whole[:share] * scale, bias_row * scale


def solution(mesh):
    return jax.shard_map(
        body,
        mesh=mesh,
        in_specs=(P("dp", "tm", "tile", None, None), P(), P(), P("dp", "tm", "tile", None, None)),
        out_specs=(
            P("dp", "tm", "tile", None, None),
            P("dp", "tm", "tile", None, None),
            P("dp", None),
            P("dp"),
        ),
        check_vma=False,
    )
```

time: 59.8 us -> 51.4 us (0.86)
  waiting for transfers between devices: 25.6 us -> 13.7 us
  local copies, waits for them, and re-layouts: 2.95 us -> 5.74 us
  Pallas kernels: 12.7 us -> 15.1 us
  starting transfers between devices: 15.7 us -> 13.6 us
    ppermute x2, waiting for transfers between devices: 7.57 us -> 1.15 us  [passed_along(): return lax.ppermute(block, axis, route)]
    ppermute x4, waiting for transfers between devices: 14.1 us -> 9.87 us  [exchange(): return lax.ppermute(block, (axis, 'tile'), route)]
    ppermute x4, starting transfers between devices: 9.06 us -> 6.48 us  [exchange(): return lax.ppermute(block, (axis, 'tile'), route)]
    pallas_call x2 -> x4, Pallas kernels: 12.7 us -> 15.1 us  [call(): pl.pallas_call(kernel_body, out_shape=shapes, in_specs=[there if i in far...]
    ppermute x4, waiting for transfers between devices: 3.94 us -> 2.71 us  [swapped(): return lax.ppermute(block, 'tile', [(0, 1), (1, 0)])]
    unnamed x11 -> x14, local copies, waits for them, and re-layouts: 2.9 us -> 3.91 us
    slice x2 -> x1, local copies, waits for them, and re-layouts: 0.01 us -> 0.91 us  [body(): x[frames - 2:].reshape(2 * height, breadth, channels)]
    squeeze x0 -> x2, local copies, waits for them, and re-layouts: none -> 0.88 us  [the longest x1 0.85 us: body(): edge = swapped(lax.dynamic_index_in_dim(x, row, 1, False))]
  transfers between devices with their start and end apart: 10 -> 10, of which waited for: 9 -> 7; matrix products, arithmetic and copies ran while one was open for 0% -> 2% of each run, Pallas kernels for 6% -> 19%
where the time goes in v2:
time: 51.4 us; the launch traced here: 50.7 us
  Pallas kernels  15.1 us (29%)
  waiting for transfers between devices  13.7 us (27%)
  starting transfers between devices  13.6 us (26%)
  local copies, waits for them, and re-layouts  5.74 us (11%)
  other arithmetic  1.74 us (3%)
  between operations  0.85 us (2%)
    pallas_call x4, Pallas kernels, call(): pl.pallas_call(kernel_body, out_shape=shapes, in_specs=[there if i in far...  15.1 us
    ppermute x4, waiting for transfers between devices, exchange(): return lax.ppermute(block, (axis, 'tile'), route)  9.87 us
    ppermute x4, starting transfers between devices, exchange(): return lax.ppermute(block, (axis, 'tile'), route)  6.48 us
    ppermute x2, starting transfers between devices, passed_along(): return lax.ppermute(block, axis, route)  6 us
    unnamed x14, local copies, waits for them, and re-layouts  3.91 us
    ppermute x4, waiting for transfers between devices, swapped(): return lax.ppermute(block, 'tile', [(0, 1), (1, 0)])  2.71 us
    ppermute x2, waiting for transfers between devices, passed_along(): return lax.ppermute(block, axis, route)  1.15 us
    ppermute x4, starting transfers between devices, swapped(): return lax.ppermute(block, 'tile', [(0, 1), (1, 0)])  1.09 us
  transfers between devices with their start and end apart: 10, of which 7 were waited for; matrix products, arithmetic and copies ran while one was open for 2% of the time, Pallas kernels for 19%

profile of v2, /device:TPU:0, one launch (start us, length us, event | category | flops | bytes accessed | tf_op | source)
XLA Modules:
  0.0 50.7 jit_solution(14607467547878248503)
XLA Ops:
  0.6 0.9 %dynamic-slice_bitcast_fusion = bf16[8,32,128]{2,1,0:T(8,128)(2,1)S(1)} fusion(bf16[1,8,8,32,128]{4,3,2,1,0:T(8,128)(2,1)} %param.4, s32[]{:T(128)S(6)} %select_n.17), kind=kLoop, calls=%fused_computation.13 | loop fusion | bytes 131076 | tf_op jit(solution)/shard_map/jit(dynamic_index_in_dim)/squeeze | solution.py:380
  1.5 0.5 collective-permute-start
  1.9 0.9 %slice.34 = bf16[1,2,8,32,128]{4,3,2,1,0:T(8,128)(2,1)S(1)} slice(bf16[1,8,8,32,128]{4,3,2,1,0:T(8,128)(2,1)} %param.4), slice={[0:1], [6:8], [0:8], [0:32], [0:128]} | slice | bytes 262144 | tf_op jit(solution)/shard_map/slice | solution.py:383
  2.9 4.7 %collective-permute-start.1 = (bf16[18,32,128]{2,1,0:T(8,128)(2,1)S(1)}, bf16[18,32,128]{2,1,0:T(8,128)(2,1)S(1)}, u32[]{:S(2)}, u32[]{:S(2)}) collective-permute-start(bf16[18,32,128]{2,1,0:T(8,128)(2,1)S(1)} %pad_maximum_fusion), channel_id=1, source_target_pairs={{0,2},{2,4},{4,6},{1,3},{3,5},{5,7},{8,10},{10,12},{12,14},{9,11},... | collective-permute-start | bytes 442376 | tf_op jit(solution)/shard_map/ppermute | solution.py:362
  7.6 0.0 copy-start
  7.6 1.0 %copy-done = bf16[1,8,8,32,128]{4,3,2,1,0:T(8,128)(2,1)S(1)} copy-done((bf16[1,8,8,32,128]{4,3,2,1,0:T(8,128)(2,1)S(1)}, bf16[1,8,8,32,128]{4,3,2,1,0:T(8,128)(2,1)}, u32[]{:S(2)}) %copy-start) | copy-done | bytes 524312
  8.7 1.0 %copy-done.2 = bf16[1,8,8,32,128]{4,3,2,1,0:T(8,128)(2,1)S(1)} copy-done((bf16[1,8,8,32,128]{4,3,2,1,0:T(8,128)(2,1)S(1)}, bf16[1,8,8,32,128]{4,3,2,1,0:T(8,128)(2,1)}, u32[]{:S(2)}) %copy-start.2) | copy-done | bytes 524312
  9.7 1.2 %copy-done.3 = bf16[3456,128]{1,0:T(8,128)(2,1)S(1)} copy-done((bf16[3456,128]{1,0:T(8,128)(2,1)S(1)}, bf16[3456,128]{1,0:T(8,128)(2,1)}, u32[]{:S(2)}) %copy-start.3) | copy-done | bytes 884760
  10.9 0.7 %copy-done.5 = f32[128]{0:T(128)S(1)} copy-done((f32[128]{0:T(128)S(1)}, f32[128]{0:T(128)}, u32[]{:S(2)}) %copy-start.5) | copy-done | bytes 536
  11.5 4.0 %forward_interior.1 = (bf16[8,8,32,128]{3,2,1,0:T(8,128)(2,1)}, bf16[8,10,32,384]{3,2,1,0:T(8,128)(2,1)S(1)}, bf16[4608,256]{1,0:T(8,128)(2,1)S(1)}, bf16[256,76...) custom-call(bf16[8,8,32,128]{3,2,1,0:T(8,128)(2,1)S(1)} %bitcast.23,, ...), custom_call_target="tpu_custom_call" | custom-call | flops 2717908992 | bytes 4194304 | tf_op jit(solution)/shard_map/forward_interior/pallas_call | solution.py:403
  15.6 5.6 %first_frames_and_weights.1 = (bf16[8,8,32,128]{3,2,1,0:T(8,128)(2,1)}, bf16[2,8,32,128]{3,2,1,0:T(8,128)(2,1)S(1)}, bf16[8,32,128]{2,1,0:T(8,128)(2,1)S(1)}, bf16[2,4,448,128]{3,2,1,0:T(8,128)(2,1)S(1)}) custom-call(bf16[8,8,32,128]{3,2,1,0:T(8,128)(2,1)} %get-tuple-element.22.block_in, ...), custom_call_target="tpu_custom_call", output_to_operand_aliasing={{0}: (0, {})} | custom-call | flops 4529848320 | bytes 4194304 | tf_op jit(solution)/shard_map/first_frames_and_weights/pallas_call | solution.py:403
  21.2 0.1 collective-permute-start.2
  21.3 0.5 collective-permute-start.4
  21.8 1.4 %collective-permute-done.4.edge = bf16[8,32,128]{2,1,0:T(8,128)(2,1)S(1)} collective-permute-done((bf16[8,32,128]{2,1,0:T(8,128)(2,1)S(1)}, bf16[8,32,128]{2,1,0:T(8,128)(2,1)S(1)}, u32[]{:S(2)}, u32[]{:S(2)}) %collective-permute-start.4) | collective-permute-done | bytes 65568 | tf_op jit(solution)/shard_map/ppermute | solution.py:366
  23.2 0.1 fusion
  23.4 1.6 %collective-permute-start.3 = (bf16[2,448,128]{2,1,0:T(8,128)(2,1)S(1)}, bf16[2,448,128]{2,1,0:T(8,128)(2,1)S(1)}, u32[]{:S(2)}, u32[]{:S(2)}) collective-permute-start(bf16[2,448,128]{2,1,0:T(8,128)(2,1)S(1)} %slice.47), channel_id=1, source_target_pairs={{0,8},{1,17},{8,0},{9,25},{16,24},{17,1},{24,16},{25,9},{2,10},{3,... | collective-permute-start | bytes 688136 | tf_op jit(solution)/shard_map/ppermute | solution.py:352
  25.0 3.7 %input_gradient_interior.1 = (bf16[8,8,32,128]{3,2,1,0:T(8,128)(2,1)}, bf16[2,10,32,384]{3,2,1,0:T(8,128)(2,1)S(1)}, bf16[256,4608]{1,0:T(8,128)(2,1)S(1)}) custom-call(bf16[2,8,32,128]{3,2,1,0:T(8,128)(2,1)S(1)} %get-tuple-element.30.early, bf16[6,8,32,128]{3,2,1,0:T(8,128)(2,1)S(1)} %get-tuple-element.31.g, ...), custom_call_target="tpu_custom_call" | custom-call | flops 2717908992 | bytes 4194304 | tf_op jit(solution)/shard_map/input_gradient_interior/pallas_call | solution.py:403
  28.7 3.1 %collective-permute-done.3 = bf16[2,448,128]{2,1,0:T(8,128)(2,1)S(1)} collective-permute-done((bf16[2,448,128]{2,1,0:T(8,128)(2,1)S(1)}, bf16[2,448,128]{2,1,0:T(8,128)(2,1)S(1)}, u32[]{:S(2)}, u32[]{:S(2)}) %collective-permute-start.3) | collective-permute-done | bytes 229408 | tf_op jit(solution)/shard_map/ppermute | solution.py:352
  31.8 0.1 add_convert_fusion
  31.9 1.8 %collective-permute-start.5 = (bf16[1,448,128]{2,1,0:T(8,128)(2,1)S(1)}, bf16[1,448,128]{2,1,0:T(8,128)(2,1)S(1)}, u32[]{:S(2)}, u32[]{:S(2)}) collective-permute-start(bf16[1,448,128]{2,1,0:T(8,128)(2,1)S(1)} %slice.41), channel_id=1, source_target_pairs={{0,16},{1,9},{8,24},{9,1},{16,0},{17,25},{24,8},{25,17},{2,18},{3,... | collective-permute-start | bytes 344072 | tf_op jit(solution)/shard_map/ppermute | solution.py:352
  33.7 1.3 %collective-permute-start.7 = (bf16[18,32,128]{2,1,0:T(8,128)(2,1)S(1)}, bf16[18,32,128]{2,1,0:T(8,128)(2,1)S(1)}, u32[]{:S(2)}, u32[]{:S(2)}) collective-permute-start(bf16[18,32,128]{2,1,0:T(8,128)(2,1)S(1)} %pad_maximum_fusion.1), channel_id=1, source_target_pairs={{2,0},{4,2},{6,4},{3,1},{5,3},{7,5},{10,8},{12,10},{14,12},{11,9},... | collective-permute-start | bytes 442376 | tf_op jit(solution)/shard_map/ppermute | solution.py:362
  35.0 3.0 %collective-permute-done.5 = bf16[1,448,128]{2,1,0:T(8,128)(2,1)S(1)} collective-permute-done((bf16[1,448,128]{2,1,0:T(8,128)(2,1)S(1)}, bf16[1,448,128]{2,1,0:T(8,128)(2,1)S(1)}, u32[]{:S(2)}, u32[]{:S(2)}) %collective-permute-start.5) | collective-permute-done | bytes 114720 | tf_op jit(solution)/shard_map/ppermute | solution.py:352
  38.1 1.5 %collective-permute-start.6 = (bf16[448,128]{1,0:T(8,128)(2,1)S(1)}, bf16[448,128]{1,0:T(8,128)(2,1)S(1)}, u32[]{:S(2)}, u32[]{:S(2)}) collective-permute-start(bf16[448,128]{1,0:T(8,128)(2,1)S(1)} %fusion.2), channel_id=1, source_target_pairs={{0,2},{1,5},{2,0},{3,7},{4,6},{5,1},{6,4},{7,3},{8,10},{9,13},{10,... | collective-permute-start | bytes 344072 | tf_op jit(solution)/shard_map/ppermute | solution.py:352
  39.6 1.2 %collective-permute-done.7.after = bf16[18,32,128]{2,1,0:T(8,128)(2,1)S(1)} collective-permute-done((bf16[18,32,128]{2,1,0:T(8,128)(2,1)S(1)}, bf16[18,32,128]{2,1,0:T(8,128)(2,1)S(1)}, u32[]{:S(2)}, u32[]{:S(2)}) %collective-permute-start.7) | collective-permute-done | bytes 147488 | tf_op jit(solution)/shard_map/ppermute | solution.py:362
  40.8 1.7 %input_gradient_last.1 = bf16[8,8,32,128]{3,2,1,0:T(8,128)(2,1)} custom-call(bf16[8,8,32,128]{3,2,1,0:T(8,128)(2,1)} %get-tuple-element.35.grad_in, bf16[2,10,32,384]{3,2,1,0:T(8,128)(2,1)S(1)} %get-tuple-element.36.last, bf16[18,32,128]{2,1,0:T(8,128)(2,1)S(1)} %collective-permute-done.7.after, ...), custom_call_target="tpu_custom_call", output_to_operand_aliasing={{}: (0, {})} | custom-call | flops 905969664 | bytes 4194304 | tf_op jit(solution)/shard_map/input_gradient_last/pallas_call | solution.py:403
  42.5 0.4 collective-permute-done.6
  43.0 1.6 %collective-permute-start.8 = (bf16[448,128]{1,0:T(8,128)(2,1)S(1)}, bf16[448,128]{1,0:T(8,128)(2,1)S(1)}, u32[]{:S(2)}, u32[]{:S(2)}) collective-permute-start(bf16[448,128]{1,0:T(8,128)(2,1)S(1)} %add_convert_fusion.2), channel_id=1, source_target_pairs={{0,4},{1,3},{2,6},{3,1},{4,0},{5,7},{6,2},{7,5},{8,12},{9,11},{10,... | collective-permute-start | bytes 344072 | tf_op jit(solution)/shard_map/ppermute | solution.py:352
  44.5 3.3 %collective-permute-done.8 = bf16[448,128]{1,0:T(8,128)(2,1)S(1)} collective-permute-done((bf16[448,128]{1,0:T(8,128)(2,1)S(1)}, bf16[448,128]{1,0:T(8,128)(2,1)S(1)}, u32[]{:S(2)}, u32[]{:S(2)}) %collective-permute-start.8) | collective-permute-done | bytes 114720 | tf_op jit(solution)/shard_map/ppermute | solution.py:352
  47.9 0.1 collective-permute-start.9
  48.0 1.3 %collective-permute-done.9 = bf16[448,128]{1,0:T(8,128)(2,1)S(1)} collective-permute-done((bf16[448,128]{1,0:T(8,128)(2,1)S(1)}, bf16[448,128]{1,0:T(8,128)(2,1)S(1)}, u32[]{:S(2)}, u32[]{:S(2)}) %collective-permute-start.9) | collective-permute-done | bytes 114720 | tf_op jit(solution)/shard_map/ppermute | solution.py:366
  49.3 0.8 %slice_multiply_fusion = f32[864,128]{1,0:T(8,128)} fusion(f32[896,128]{1,0:T(8,128)S(1)} %fusion.1), kind=kLoop, calls=%fused_computation.4 | loop fusion | flops 110592 | bytes 884736 | tf_op jit(solution)/shard_map/mul | solution.py:565
  50.1 0.6 %multiply_bitcast_fusion = f32[32]{0:T(128)} fusion(f32[1,128]{1,0:T(1,128)S(1)} %slice.50, s32[]{:T(128)S(6)} %select_n.20), kind=kLoop, calls=%fused_computation.14 | loop fusion | flops 32 | bytes 260 | tf_op jit(solution)/shard_map/mul | solution.py:565
  (24 shorter events, 0.3 us)
Async XLA Ops:
  1.5 1.4 %collective-permute-start = (bf16[8,32,128]{2,1,0:T(8,128)(2,1)S(1)}, bf16[8,32,128]{2,1,0:T(8,128)(2,1)S(1)}, u32[]{:S(2)}, u32[]{:S(2)}) collective-permute-start(bf16[8,32,128]{2,1,0:T(8,128)(2,1)S(1)} %dynamic-slice_bitcast_fusion), channel_id=1, source_target_pairs={{0,1},{1,0},{2,3},{3,2},{4,5},{5,4},{6,7},{7,6},{8,9},{9,8},{10,11... | collective-permute-start | bytes 196616 | tf_op jit(solution)/shard_map/ppermute | solution.py:366
  2.9 12.6 %collective-permute-start.1 = (bf16[18,32,128]{2,1,0:T(8,128)(2,1)S(1)}, bf16[18,32,128]{2,1,0:T(8,128)(2,1)S(1)}, u32[]{:S(2)}, u32[]{:S(2)}) collective-permute-start(bf16[18,32,128]{2,1,0:T(8,128)(2,1)S(1)} %pad_maximum_fusion), channel_id=1, source_target_pairs={{0,2},{2,4},{4,6},{1,3},{3,5},{5,7},{8,10},{10,12},{12,14},{9,11},... | collective-permute-start | bytes 442376 | tf_op jit(solution)/shard_map/ppermute | solution.py:362
  7.6 1.0 %copy-start = (bf16[1,8,8,32,128]{4,3,2,1,0:T(8,128)(2,1)S(1)}, bf16[1,8,8,32,128]{4,3,2,1,0:T(8,128)(2,1)}, u32[]{:S(2)}) copy-start(bf16[1,8,8,32,128]{4,3,2,1,0:T(8,128)(2,1)} %param.7) | copy-start | bytes 1572868
  8.7 1.0 %copy-start.2 = (bf16[1,8,8,32,128]{4,3,2,1,0:T(8,128)(2,1)S(1)}, bf16[1,8,8,32,128]{4,3,2,1,0:T(8,128)(2,1)}, u32[]{:S(2)}) copy-start(bf16[1,8,8,32,128]{4,3,2,1,0:T(8,128)(2,1)} %param.4) | copy-start | bytes 1572868
  9.7 1.2 %copy-start.3 = (bf16[3456,128]{1,0:T(8,128)(2,1)S(1)}, bf16[3456,128]{1,0:T(8,128)(2,1)}, u32[]{:S(2)}) copy-start(bf16[3456,128]{1,0:T(8,128)(2,1)} %kernel.3) | copy-start | bytes 2654212
  10.9 0.7 %copy-start.5 = (f32[128]{0:T(128)S(1)}, f32[128]{0:T(128)}, u32[]{:S(2)}) copy-start(f32[128]{0:T(128)} %param.6) | copy-start | bytes 1540
  11.5 4.0 %copy-start.1 = (bf16[1,8,8,32,128]{4,3,2,1,0:T(8,128)(2,1)S(1)}, bf16[1,8,8,32,128]{4,3,2,1,0:T(8,128)(2,1)}, u32[]{:S(2)}) copy-start(bf16[1,8,8,32,128]{4,3,2,1,0:T(8,128)(2,1)} %param.7) | copy-start | bytes 1572868
  11.5 4.0 %copy-start.6 = (f32[128]{0:T(128)S(1)}, f32[128]{0:T(128)}, u32[]{:S(2)}) copy-start(f32[128]{0:T(128)} %param.6) | copy-start | bytes 1540
  21.2 3.8 %copy-start.4 = (bf16[3456,128]{1,0:T(8,128)(2,1)S(1)}, bf16[3456,128]{1,0:T(8,128)(2,1)}, u32[]{:S(2)}) copy-start(bf16[3456,128]{1,0:T(8,128)(2,1)} %kernel.3) | copy-start | bytes 2654212
  21.2 2.0 %collective-permute-start.2 = (bf16[4,448,128]{2,1,0:T(8,128)(2,1)S(1)}, bf16[4,448,128]{2,1,0:T(8,128)(2,1)S(1)}, u32[]{:S(2)}, u32[]{:S(2)}) collective-permute-start(bf16[4,448,128]{2,1,0:T(8,128)(2,1)S(1)} %slice_bitcast_fusion), channel_id=1, source_target_pairs={{0,1},{1,0},{2,3},{3,2},{4,5},{5,4},{6,7},{7,6},{8,9},{9,8},{10,11... | collective-permute-start | bytes 1376264 | tf_op jit(solution)/shard_map/ppermute | solution.py:366
  21.3 1.9 %collective-permute-start.4 = (bf16[8,32,128]{2,1,0:T(8,128)(2,1)S(1)}, bf16[8,32,128]{2,1,0:T(8,128)(2,1)S(1)}, u32[]{:S(2)}, u32[]{:S(2)}) collective-permute-start(bf16[8,32,128]{2,1,0:T(8,128)(2,1)S(1)} %get-tuple-element.32), channel_id=1, source_target_pairs={{0,1},{1,0},{2,3},{3,2},{4,5},{5,4},{6,7},{7,6},{8,9},{9,8},{10,11... | collective-permute-start | bytes 196616 | tf_op jit(solution)/shard_map/ppermute | solution.py:366
  23.4 8.5 %collective-permute-start.3 = (bf16[2,448,128]{2,1,0:T(8,128)(2,1)S(1)}, bf16[2,448,128]{2,1,0:T(8,128)(2,1)S(1)}, u32[]{:S(2)}, u32[]{:S(2)}) collective-permute-start(bf16[2,448,128]{2,1,0:T(8,128)(2,1)S(1)} %slice.47), channel_id=1, source_target_pairs={{0,8},{1,17},{8,0},{9,25},{16,24},{17,1},{24,16},{25,9},{2,10},{3,... | collective-permute-start | bytes 688136 | tf_op jit(solution)/shard_map/ppermute | solution.py:352
  31.9 6.1 %collective-permute-start.5 = (bf16[1,448,128]{2,1,0:T(8,128)(2,1)S(1)}, bf16[1,448,128]{2,1,0:T(8,128)(2,1)S(1)}, u32[]{:S(2)}, u32[]{:S(2)}) collective-permute-start(bf16[1,448,128]{2,1,0:T(8,128)(2,1)S(1)} %slice.41), channel_id=1, source_target_pairs={{0,16},{1,9},{8,24},{9,1},{16,0},{17,25},{24,8},{25,17},{2,18},{3,... | collective-permute-start | bytes 344072 | tf_op jit(solution)/shard_map/ppermute | solution.py:352
  33.7 7.0 %collective-permute-start.7 = (bf16[18,32,128]{2,1,0:T(8,128)(2,1)S(1)}, bf16[18,32,128]{2,1,0:T(8,128)(2,1)S(1)}, u32[]{:S(2)}, u32[]{:S(2)}) collective-permute-start(bf16[18,32,128]{2,1,0:T(8,128)(2,1)S(1)} %pad_maximum_fusion.1), channel_id=1, source_target_pairs={{2,0},{4,2},{6,4},{3,1},{5,3},{7,5},{10,8},{12,10},{14,12},{11,9},... | collective-permute-start | bytes 442376 | tf_op jit(solution)/shard_map/ppermute | solution.py:362
  38.1 4.9 %collective-permute-start.6 = (bf16[448,128]{1,0:T(8,128)(2,1)S(1)}, bf16[448,128]{1,0:T(8,128)(2,1)S(1)}, u32[]{:S(2)}, u32[]{:S(2)}) collective-permute-start(bf16[448,128]{1,0:T(8,128)(2,1)S(1)} %fusion.2), channel_id=1, source_target_pairs={{0,2},{1,5},{2,0},{3,7},{4,6},{5,1},{6,4},{7,3},{8,10},{9,13},{10,... | collective-permute-start | bytes 344072 | tf_op jit(solution)/shard_map/ppermute | solution.py:352
  43.0 4.9 %collective-permute-start.8 = (bf16[448,128]{1,0:T(8,128)(2,1)S(1)}, bf16[448,128]{1,0:T(8,128)(2,1)S(1)}, u32[]{:S(2)}, u32[]{:S(2)}) collective-permute-start(bf16[448,128]{1,0:T(8,128)(2,1)S(1)} %add_convert_fusion.2), channel_id=1, source_target_pairs={{0,4},{1,3},{2,6},{3,1},{4,0},{5,7},{6,2},{7,5},{8,12},{9,11},{10,... | collective-permute-start | bytes 344072 | tf_op jit(solution)/shard_map/ppermute | solution.py:352
  47.9 1.4 %collective-permute-start.9 = (bf16[448,128]{1,0:T(8,128)(2,1)S(1)}, bf16[448,128]{1,0:T(8,128)(2,1)S(1)}, u32[]{:S(2)}, u32[]{:S(2)}) collective-permute-start(bf16[448,128]{1,0:T(8,128)(2,1)S(1)} %add_convert_fusion.1), channel_id=1, source_target_pairs={{0,1},{1,0},{2,3},{3,2},{4,5},{5,4},{6,7},{7,6},{8,9},{9,8},{10,11... | collective-permute-start | bytes 344072 | tf_op jit(solution)/shard_map/ppermute | solution.py:366

commit v3 on v2

--- a/solution.py
+++ b/solution.py
@@ -328,6 +328,37 @@
     copy.wait()
 
 
+def border_kernel(x, edge, tail, copied):
+    frames, height = x.shape[:2]
+    row = jnp.where(lax.axis_index("tile") == 0, height - 1, 0)
+    copies = [
+        pltpu.make_async_copy(x.at[:, row], edge, copied.at[0]),
+        pltpu.make_async_copy(x.at[frames - 2 : frames], tail, copied.at[1]),
+    ]
+    for copy in copies:
+        copy.start()
+    for copy in copies:
+        copy.wait()
+
+
+def closing_kernel(own, other, weight, bias, *, scale):
+    tile = lax.axis_index("tile")
+    half, channels = own.shape
+    rest = weight.shape[0] - half
+    mine, theirs = own[...].astype(F32) * scale, other[...].astype(F32) * scale
+    first = jnp.where(tile == 0, mine, theirs)
+    second = jnp.where(tile == 0, theirs, mine)
+    weight[0:half] = first
+    weight[half:] = second[0:rest]
+    line = second[rest : rest + 1]
+    share = bias.shape[1]
+    spot = lax.axis_index("dp") * share
+    picked = jnp.zeros((1, share), F32)
+    for j in range(channels // share):
+        picked = jnp.where(spot == j * share, line[:, j * share : (j + 1) * share], picked)
+    bias[...] = picked
+
+
 def bits_of(count):
     return count.bit_length() - 1
 
@@ -376,15 +407,6 @@
     half = -(-(share + 1) // 32) * 16
     arranged = share % 32 == 0
 
-    row = jnp.where(tile == 0, height - 1, 0)
-    edge = swapped(lax.dynamic_index_in_dim(x, row, 1, False))
-    before = passed_along(
-        jnp.concatenate(
-            [x[frames - 2 :].reshape(2 * height, breadth, channels), edge[frames - 2 :]], axis=0
-        ),
-        "tm",
-        1,
-    )
     area = height * breadth
     bias = conv_bias.reshape(1, channels)
     cells = jax.ShapeDtypeStruct(x.shape, BF16)
@@ -417,6 +439,24 @@
         )(*args)
 
     dma, vmem = pltpu.SemaphoreType.DMA, pltpu.VMEM
+    edge, tail = call(
+        border_kernel,
+        "border_rows",
+        2.0,
+        arrays((frames, breadth, channels), frames_shape(2)),
+        [dma((2,))],
+        (0,),
+        (),
+        (x,),
+    )
+    edge = swapped(edge)
+    before = passed_along(
+        jnp.concatenate(
+            [tail.reshape(2 * height, breadth, channels), edge[frames - 2 :]], axis=0
+        ),
+        "tm",
+        1,
+    )
     block_out, windows, taps, turned, later_grads, later_edge, total = call(
         interior_kernel,
         "forward_interior",
@@ -548,21 +588,20 @@
             total, grad_input = lax.optimization_barrier((total, grad_input))
         total = added(total, exchange(total, "tm", steps, (1 << k, 1 << (n - 1 - k))))
     other = swapped(total)
-    whole = jnp.where(
-        tile == 0,
-        jnp.concatenate([total, other], axis=0),
-        jnp.concatenate([other, total], axis=0),
-    ).astype(F32)
-
     positions = (
         clip_count * frames * height * breadth * shards * steps * lax.axis_size("tile")
     )
-    scale = 1.0 / math.sqrt(positions)
-    bias_share = channels // shards
-    bias_row = lax.dynamic_slice_in_dim(
-        whole[share], lax.axis_index("dp") * bias_share, bias_share, 0
-    )
-    return block_out[None], grad_input[None], whole[:share] * scale, bias_row * scale
+    weight, bias_grad = call(
+        functools.partial(closing_kernel, scale=1.0 / math.sqrt(positions)),
+        "scaled_weights",
+        0.01,
+        arrays((share, channels), (1, channels // shards), kind=F32),
+        [],
+        (),
+        (),
+        (total, other),
+    )
+    return block_out[None], grad_input[None], weight, bias_grad.reshape(channels // shards)
 
 
 def solution(mesh):

time: 51.4 us -> 47.8 us (0.930)
  local copies, waits for them, and re-layouts: 5.74 us -> 1.11 us
  starting transfers between devices: 13.6 us -> 15.5 us
  other arithmetic: 1.74 us -> 0.32 us
  Pallas kernels: 15.1 us -> 16.2 us
    unnamed x14 -> x8, local copies, waits for them, and re-layouts: 3.91 us -> 1.05 us
    ppermute x4, starting transfers between devices: 6.48 us -> 8.25 us  [exchange(): return lax.ppermute(block, (axis, 'tile'), route)]
    mul x2 -> x0, other arithmetic: 1.37 us -> none  [the longest x1 0.79 us: body(): whole[:share] * scale]
    pallas_call x4 -> x6, Pallas kernels: 15.1 us -> 16.2 us  [call(): pl.pallas_call(kernel_body, out_shape=shapes, in_specs=[there if i in far...]
    slice x2 -> x0, local copies, waits for them, and re-layouts: 0.92 us -> none  [the longest x1 0.91 us: body(): x[frames - 2:].reshape(2 * height, breadth, channels)]
    ppermute x4, waiting for transfers between devices: 2.71 us -> 3.62 us  [swapped(): return lax.ppermute(block, 'tile', [(0, 1), (1, 0)])]
    squeeze x1 -> x0, local copies, waits for them, and re-layouts: 0.85 us -> none  [body(): edge = swapped(lax.dynamic_index_in_dim(x, row, 1, False))]
    ppermute x4, waiting for transfers between devices: 9.87 us -> 9.28 us  [exchange(): return lax.ppermute(block, (axis, 'tile'), route)]
  transfers between devices with their start and end apart: 10 -> 10, of which waited for: 7 -> 8; matrix products, arithmetic and copies ran while one was open for 2% -> 0% of each run, Pallas kernels for 19% -> 20%
where the time goes in v3:
time: 47.8 us; the launch traced here: 47.6 us
  Pallas kernels  16.2 us (34%)
  starting transfers between devices  15.5 us (32%)
  waiting for transfers between devices  13.7 us (29%)
  local copies, waits for them, and re-layouts  1.11 us (2%)
  between operations  0.8 us (2%)
    pallas_call x6, Pallas kernels, call(): pl.pallas_call(kernel_body, out_shape=shapes, in_specs=[there if i in far...  16.2 us
    ppermute x4, waiting for transfers between devices, exchange(): return lax.ppermute(block, (axis, 'tile'), route)  9.28 us
    ppermute x4, starting transfers between devices, exchange(): return lax.ppermute(block, (axis, 'tile'), route)  8.25 us
    ppermute x2, starting transfers between devices, passed_along(): return lax.ppermute(block, axis, route)  6.04 us
    ppermute x4, waiting for transfers between devices, swapped(): return lax.ppermute(block, 'tile', [(0, 1), (1, 0)])  3.62 us
    ppermute x4, starting transfers between devices, swapped(): return lax.ppermute(block, 'tile', [(0, 1), (1, 0)])  1.16 us
    unnamed x8, local copies, waits for them, and re-layouts  1.05 us
  transfers between devices with their start and end apart: 10, of which 8 were waited for; matrix products, arithmetic and copies ran while one was open for 0% of the time, Pallas kernels for 20%

profile of v3, /device:TPU:0, one launch (start us, length us, event | category | flops | bytes accessed | tf_op | source)
XLA Modules:
  0.0 47.6 jit_solution(209843943664940016)
XLA Ops:
  0.6 0.0 copy-start.2
  0.6 1.0 %copy-done.2 = bf16[1,8,8,32,128]{4,3,2,1,0:T(8,128)(2,1)S(1)} copy-done((bf16[1,8,8,32,128]{4,3,2,1,0:T(8,128)(2,1)S(1)}, bf16[1,8,8,32,128]{4,3,2,1,0:T(8,128)(2,1)}, u32[]{:S(2)}) %copy-start.2) | copy-done | bytes 524312
  1.7 0.2 border_rows.1
  1.9 0.5 %collective-permute-start = (bf16[8,32,128]{2,1,0:T(8,128)(2,1)S(1)}, bf16[8,32,128]{2,1,0:T(8,128)(2,1)S(1)}, u32[]{:S(2)}, u32[]{:S(2)}) collective-permute-start(bf16[8,32,128]{2,1,0:T(8,128)(2,1)S(1)} %get-tuple-element.26), channel_id=1, source_target_pairs={{0,1},{1,0},{2,3},{3,2},{4,5},{5,4},{6,7},{7,6},{8,9},{9,8},{10,11... | collective-permute-start | bytes 196616 | tf_op jit(solution)/shard_map/ppermute | solution.py:397
  2.4 0.9 %collective-permute-done.edge = bf16[8,32,128]{2,1,0:T(8,128)(2,1)S(1)} collective-permute-done((bf16[8,32,128]{2,1,0:T(8,128)(2,1)S(1)}, bf16[8,32,128]{2,1,0:T(8,128)(2,1)S(1)}, u32[]{:S(2)}, u32[]{:S(2)}) %collective-permute-start) | collective-permute-done | bytes 65568 | tf_op jit(solution)/shard_map/ppermute | solution.py:397
  3.3 4.8 %collective-permute-start.1 = (bf16[18,32,128]{2,1,0:T(8,128)(2,1)S(1)}, bf16[18,32,128]{2,1,0:T(8,128)(2,1)S(1)}, u32[]{:S(2)}, u32[]{:S(2)}) collective-permute-start(bf16[18,32,128]{2,1,0:T(8,128)(2,1)S(1)} %pad_maximum_fusion), channel_id=1, source_target_pairs={{0,2},{2,4},{4,6},{1,3},{3,5},{5,7},{8,10},{10,12},{12,14},{9,11},... | collective-permute-start | bytes 442376 | tf_op jit(solution)/shard_map/ppermute | solution.py:393
  8.1 0.0 copy-done
  8.1 0.0 copy-done.1
  8.1 3.9 %forward_interior.1 = (bf16[8,8,32,128]{3,2,1,0:T(8,128)(2,1)}, bf16[8,10,32,384]{3,2,1,0:T(8,128)(2,1)S(1)}, bf16[4608,256]{1,0:T(8,128)(2,1)S(1)}, bf16[256,76...) custom-call(bf16[8,8,32,128]{3,2,1,0:T(8,128)(2,1)S(1)} %bitcast.22,, ...), custom_call_target="tpu_custom_call" | custom-call | flops 2717908992 | bytes 4194304 | tf_op jit(solution)/shard_map/forward_interior/pallas_call | solution.py:425
  12.1 0.0 collective-permute-done.1.before
  12.1 5.6 %first_frames_and_weights.1 = (bf16[8,8,32,128]{3,2,1,0:T(8,128)(2,1)}, bf16[2,8,32,128]{3,2,1,0:T(8,128)(2,1)S(1)}, bf16[8,32,128]{2,1,0:T(8,128)(2,1)S(1)}, bf16[2,4,448,128]{3,2,1,0:T(8,128)(2,1)S(1)}) custom-call(bf16[8,8,32,128]{3,2,1,0:T(8,128)(2,1)} %get-tuple-element.27.block_in, ...), custom_call_target="tpu_custom_call", output_to_operand_aliasing={{0}: (0, {})} | custom-call | flops 4529848320 | bytes 4194304 | tf_op jit(solution)/shard_map/first_frames_and_weights/pallas_call | solution.py:425
  17.7 0.1 collective-permute-start.2
  17.8 0.5 %collective-permute-start.4 = (bf16[8,32,128]{2,1,0:T(8,128)(2,1)S(1)}, bf16[8,32,128]{2,1,0:T(8,128)(2,1)S(1)}, u32[]{:S(2)}, u32[]{:S(2)}) collective-permute-start(bf16[8,32,128]{2,1,0:T(8,128)(2,1)S(1)} %get-tuple-element.38), channel_id=1, source_target_pairs={{0,1},{1,0},{2,3},{3,2},{4,5},{5,4},{6,7},{7,6},{8,9},{9,8},{10,11... | collective-permute-start | bytes 196616 | tf_op jit(solution)/shard_map/ppermute | solution.py:397
  18.3 1.4 %collective-permute-done.4.edge = bf16[8,32,128]{2,1,0:T(8,128)(2,1)S(1)} collective-permute-done((bf16[8,32,128]{2,1,0:T(8,128)(2,1)S(1)}, bf16[8,32,128]{2,1,0:T(8,128)(2,1)S(1)}, u32[]{:S(2)}, u32[]{:S(2)}) %collective-permute-start.4) | collective-permute-done | bytes 65568 | tf_op jit(solution)/shard_map/ppermute | solution.py:397
  19.7 0.0 collective-permute-done.2
  19.7 0.1 fusion
  19.9 1.6 %collective-permute-start.3 = (bf16[2,448,128]{2,1,0:T(8,128)(2,1)S(1)}, bf16[2,448,128]{2,1,0:T(8,128)(2,1)S(1)}, u32[]{:S(2)}, u32[]{:S(2)}) collective-permute-start(bf16[2,448,128]{2,1,0:T(8,128)(2,1)S(1)} %slice.34), channel_id=1, source_target_pairs={{0,8},{1,17},{8,0},{9,25},{16,24},{17,1},{24,16},{25,9},{2,10},{3,... | collective-permute-start | bytes 688136 | tf_op jit(solution)/shard_map/ppermute | solution.py:383
  21.5 3.7 %input_gradient_interior.1 = (bf16[8,8,32,128]{3,2,1,0:T(8,128)(2,1)}, bf16[2,10,32,384]{3,2,1,0:T(8,128)(2,1)S(1)}, bf16[256,4608]{1,0:T(8,128)(2,1)S(1)}) custom-call(bf16[2,8,32,128]{3,2,1,0:T(8,128)(2,1)S(1)} %get-tuple-element.36.early, bf16[6,8,32,128]{3,2,1,0:T(8,128)(2,1)S(1)} %get-tuple-element.37.g, ...), custom_call_target="tpu_custom_call" | custom-call | flops 2717908992 | bytes 4194304 | tf_op jit(solution)/shard_map/input_gradient_interior/pallas_call | solution.py:425
  25.2 3.1 %collective-permute-done.3 = bf16[2,448,128]{2,1,0:T(8,128)(2,1)S(1)} collective-permute-done((bf16[2,448,128]{2,1,0:T(8,128)(2,1)S(1)}, bf16[2,448,128]{2,1,0:T(8,128)(2,1)S(1)}, u32[]{:S(2)}, u32[]{:S(2)}) %collective-permute-start.3) | collective-permute-done | bytes 229408 | tf_op jit(solution)/shard_map/ppermute | solution.py:383
  28.3 0.1 add_convert_fusion
  28.4 1.8 %collective-permute-start.5 = (bf16[1,448,128]{2,1,0:T(8,128)(2,1)S(1)}, bf16[1,448,128]{2,1,0:T(8,128)(2,1)S(1)}, u32[]{:S(2)}, u32[]{:S(2)}) collective-permute-start(bf16[1,448,128]{2,1,0:T(8,128)(2,1)S(1)} %slice.30), channel_id=1, source_target_pairs={{0,16},{1,9},{8,24},{9,1},{16,0},{17,25},{24,8},{25,17},{2,18},{3,... | collective-permute-start | bytes 344072 | tf_op jit(solution)/shard_map/ppermute | solution.py:383
  30.2 1.3 %collective-permute-start.7 = (bf16[18,32,128]{2,1,0:T(8,128)(2,1)S(1)}, bf16[18,32,128]{2,1,0:T(8,128)(2,1)S(1)}, u32[]{:S(2)}, u32[]{:S(2)}) collective-permute-start(bf16[18,32,128]{2,1,0:T(8,128)(2,1)S(1)} %pad_maximum_fusion.1), channel_id=1, source_target_pairs={{2,0},{4,2},{6,4},{3,1},{5,3},{7,5},{10,8},{12,10},{14,12},{11,9},... | collective-permute-start | bytes 442376 | tf_op jit(solution)/shard_map/ppermute | solution.py:393
  31.5 3.0 %collective-permute-done.5 = bf16[1,448,128]{2,1,0:T(8,128)(2,1)S(1)} collective-permute-done((bf16[1,448,128]{2,1,0:T(8,128)(2,1)S(1)}, bf16[1,448,128]{2,1,0:T(8,128)(2,1)S(1)}, u32[]{:S(2)}, u32[]{:S(2)}) %collective-permute-start.5) | collective-permute-done | bytes 114720 | tf_op jit(solution)/shard_map/ppermute | solution.py:383
  34.6 1.9 %collective-permute-start.6 = (bf16[448,128]{1,0:T(8,128)(2,1)S(1)}, bf16[448,128]{1,0:T(8,128)(2,1)S(1)}, u32[]{:S(2)}, u32[]{:S(2)}) collective-permute-start(bf16[448,128]{1,0:T(8,128)(2,1)S(1)} %fusion.1), channel_id=1, source_target_pairs={{0,2},{1,5},{2,0},{3,7},{4,6},{5,1},{6,4},{7,3},{8,10},{9,13},{10,... | collective-permute-start | bytes 344072 | tf_op jit(solution)/shard_map/ppermute | solution.py:383
  36.5 0.8 %collective-permute-done.7.after = bf16[18,32,128]{2,1,0:T(8,128)(2,1)S(1)} collective-permute-done((bf16[18,32,128]{2,1,0:T(8,128)(2,1)S(1)}, bf16[18,32,128]{2,1,0:T(8,128)(2,1)S(1)}, u32[]{:S(2)}, u32[]{:S(2)}) %collective-permute-start.7) | collective-permute-done | bytes 147488 | tf_op jit(solution)/shard_map/ppermute | solution.py:393
  37.3 1.7 %input_gradient_last.1 = bf16[8,8,32,128]{3,2,1,0:T(8,128)(2,1)} custom-call(bf16[8,8,32,128]{3,2,1,0:T(8,128)(2,1)} %get-tuple-element.41.grad_in, bf16[2,10,32,384]{3,2,1,0:T(8,128)(2,1)S(1)} %get-tuple-element.42.last, bf16[18,32,128]{2,1,0:T(8,128)(2,1)S(1)} %collective-permute-done.7.after, ...), custom_call_target="tpu_custom_call", output_to_operand_aliasing={{}: (0, {})} | custom-call | flops 905969664 | bytes 4194304 | tf_op jit(solution)/shard_map/input_gradient_last/pallas_call | solution.py:425
  39.0 0.4 collective-permute-done.6
  39.5 2.9 %collective-permute-start.8 = (bf16[448,128]{1,0:T(8,128)(2,1)S(1)}, bf16[448,128]{1,0:T(8,128)(2,1)S(1)}, u32[]{:S(2)}, u32[]{:S(2)}) collective-permute-start(bf16[448,128]{1,0:T(8,128)(2,1)S(1)} %add_convert_fusion.2), channel_id=1, source_target_pairs={{0,4},{1,3},{2,6},{3,1},{4,0},{5,7},{6,2},{7,5},{8,12},{9,11},{10,... | collective-permute-start | bytes 344072 | tf_op jit(solution)/shard_map/ppermute | solution.py:383
  42.4 2.8 %collective-permute-done.8 = bf16[448,128]{1,0:T(8,128)(2,1)S(1)} collective-permute-done((bf16[448,128]{1,0:T(8,128)(2,1)S(1)}, bf16[448,128]{1,0:T(8,128)(2,1)S(1)}, u32[]{:S(2)}, u32[]{:S(2)}) %collective-permute-start.8) | collective-permute-done | bytes 114720 | tf_op jit(solution)/shard_map/ppermute | solution.py:383
  45.2 0.1 collective-permute-start.9
  45.2 1.3 %collective-permute-done.9.other = bf16[448,128]{1,0:T(8,128)(2,1)S(1)} collective-permute-done((bf16[448,128]{1,0:T(8,128)(2,1)S(1)}, bf16[448,128]{1,0:T(8,128)(2,1)S(1)}, u32[]{:S(2)}, u32[]{:S(2)}) %collective-permute-start.9) | collective-permute-done | bytes 114720 | tf_op jit(solution)/shard_map/ppermute | solution.py:397
  46.6 1.0 %scaled_weights.1 = (f32[864,128]{1,0:T(8,128)}, f32[1,32]{1,0:T(1,128)}) custom-call(bf16[448,128]{1,0:T(8,128)(2,1)S(1)} %add_convert_fusion.1.own, bf16[448,128]{1,0:T(8,128)(2,1)S(1)} %collective-permute-done.9.other), custom_call_target="tpu_custom_call" | custom-call | flops 36238784 | bytes 4194304 | tf_op jit(solution)/shard_map/scaled_weights/pallas_call | solution.py:425
  (14 shorter events, 0.2 us)
Async XLA Ops:
  0.6 1.0 %copy-start.2 = (bf16[1,8,8,32,128]{4,3,2,1,0:T(8,128)(2,1)S(1)}, bf16[1,8,8,32,128]{4,3,2,1,0:T(8,128)(2,1)}, u32[]{:S(2)}) copy-start(bf16[1,8,8,32,128]{4,3,2,1,0:T(8,128)(2,1)} %param.4) | copy-start | bytes 1572868
  1.7 6.4 %copy-start = (bf16[1,8,8,32,128]{4,3,2,1,0:T(8,128)(2,1)S(1)}, bf16[1,8,8,32,128]{4,3,2,1,0:T(8,128)(2,1)}, u32[]{:S(2)}) copy-start(bf16[1,8,8,32,128]{4,3,2,1,0:T(8,128)(2,1)} %param.7) | copy-start | bytes 1572868
  1.7 6.4 %copy-start.1 = (bf16[3456,128]{1,0:T(8,128)(2,1)S(1)}, bf16[3456,128]{1,0:T(8,128)(2,1)}, u32[]{:S(2)}) copy-start(bf16[3456,128]{1,0:T(8,128)(2,1)} %kernel.3) | copy-start | bytes 2654212
  1.7 6.4 %copy-start.3 = (f32[128]{0:T(128)S(1)}, f32[128]{0:T(128)}, u32[]{:S(2)}) copy-start(f32[128]{0:T(128)} %param.6) | copy-start | bytes 1540
  1.9 1.4 %collective-permute-start = (bf16[8,32,128]{2,1,0:T(8,128)(2,1)S(1)}, bf16[8,32,128]{2,1,0:T(8,128)(2,1)S(1)}, u32[]{:S(2)}, u32[]{:S(2)}) collective-permute-start(bf16[8,32,128]{2,1,0:T(8,128)(2,1)S(1)} %get-tuple-element.26), channel_id=1, source_target_pairs={{0,1},{1,0},{2,3},{3,2},{4,5},{5,4},{6,7},{7,6},{8,9},{9,8},{10,11... | collective-permute-start | bytes 196616 | tf_op jit(solution)/shard_map/ppermute | solution.py:397
  3.3 8.7 %collective-permute-start.1 = (bf16[18,32,128]{2,1,0:T(8,128)(2,1)S(1)}, bf16[18,32,128]{2,1,0:T(8,128)(2,1)S(1)}, u32[]{:S(2)}, u32[]{:S(2)}) collective-permute-start(bf16[18,32,128]{2,1,0:T(8,128)(2,1)S(1)} %pad_maximum_fusion), channel_id=1, source_target_pairs={{0,2},{2,4},{4,6},{1,3},{3,5},{5,7},{8,10},{10,12},{12,14},{9,11},... | collective-permute-start | bytes 442376 | tf_op jit(solution)/shard_map/ppermute | solution.py:393
  17.7 2.0 %collective-permute-start.2 = (bf16[4,448,128]{2,1,0:T(8,128)(2,1)S(1)}, bf16[4,448,128]{2,1,0:T(8,128)(2,1)S(1)}, u32[]{:S(2)}, u32[]{:S(2)}) collective-permute-start(bf16[4,448,128]{2,1,0:T(8,128)(2,1)S(1)} %slice_bitcast_fusion), channel_id=1, source_target_pairs={{0,1},{1,0},{2,3},{3,2},{4,5},{5,4},{6,7},{7,6},{8,9},{9,8},{10,11... | collective-permute-start | bytes 1376264 | tf_op jit(solution)/shard_map/ppermute | solution.py:397
  17.8 1.9 %collective-permute-start.4 = (bf16[8,32,128]{2,1,0:T(8,128)(2,1)S(1)}, bf16[8,32,128]{2,1,0:T(8,128)(2,1)S(1)}, u32[]{:S(2)}, u32[]{:S(2)}) collective-permute-start(bf16[8,32,128]{2,1,0:T(8,128)(2,1)S(1)} %get-tuple-element.38), channel_id=1, source_target_pairs={{0,1},{1,0},{2,3},{3,2},{4,5},{5,4},{6,7},{7,6},{8,9},{9,8},{10,11... | collective-permute-start | bytes 196616 | tf_op jit(solution)/shard_map/ppermute | solution.py:397
  19.9 8.5 %collective-permute-start.3 = (bf16[2,448,128]{2,1,0:T(8,128)(2,1)S(1)}, bf16[2,448,128]{2,1,0:T(8,128)(2,1)S(1)}, u32[]{:S(2)}, u32[]{:S(2)}) collective-permute-start(bf16[2,448,128]{2,1,0:T(8,128)(2,1)S(1)} %slice.34), channel_id=1, source_target_pairs={{0,8},{1,17},{8,0},{9,25},{16,24},{17,1},{24,16},{25,9},{2,10},{3,... | collective-permute-start | bytes 688136 | tf_op jit(solution)/shard_map/ppermute | solution.py:383
  28.4 6.1 %collective-permute-start.5 = (bf16[1,448,128]{2,1,0:T(8,128)(2,1)S(1)}, bf16[1,448,128]{2,1,0:T(8,128)(2,1)S(1)}, u32[]{:S(2)}, u32[]{:S(2)}) collective-permute-start(bf16[1,448,128]{2,1,0:T(8,128)(2,1)S(1)} %slice.30), channel_id=1, source_target_pairs={{0,16},{1,9},{8,24},{9,1},{16,0},{17,25},{24,8},{25,17},{2,18},{3,... | collective-permute-start | bytes 344072 | tf_op jit(solution)/shard_map/ppermute | solution.py:383
  30.2 7.0 %collective-permute-start.7 = (bf16[18,32,128]{2,1,0:T(8,128)(2,1)S(1)}, bf16[18,32,128]{2,1,0:T(8,128)(2,1)S(1)}, u32[]{:S(2)}, u32[]{:S(2)}) collective-permute-start(bf16[18,32,128]{2,1,0:T(8,128)(2,1)S(1)} %pad_maximum_fusion.1), channel_id=1, source_target_pairs={{2,0},{4,2},{6,4},{3,1},{5,3},{7,5},{10,8},{12,10},{14,12},{11,9},... | collective-permute-start | bytes 442376 | tf_op jit(solution)/shard_map/ppermute | solution.py:393
  34.6 4.9 %collective-permute-start.6 = (bf16[448,128]{1,0:T(8,128)(2,1)S(1)}, bf16[448,128]{1,0:T(8,128)(2,1)S(1)}, u32[]{:S(2)}, u32[]{:S(2)}) collective-permute-start(bf16[448,128]{1,0:T(8,128)(2,1)S(1)} %fusion.1), channel_id=1, source_target_pairs={{0,2},{1,5},{2,0},{3,7},{4,6},{5,1},{6,4},{7,3},{8,10},{9,13},{10,... | collective-permute-start | bytes 344072 | tf_op jit(solution)/shard_map/ppermute | solution.py:383
  39.5 5.7 %collective-permute-start.8 = (bf16[448,128]{1,0:T(8,128)(2,1)S(1)}, bf16[448,128]{1,0:T(8,128)(2,1)S(1)}, u32[]{:S(2)}, u32[]{:S(2)}) collective-permute-start(bf16[448,128]{1,0:T(8,128)(2,1)S(1)} %add_convert_fusion.2), channel_id=1, source_target_pairs={{0,4},{1,3},{2,6},{3,1},{4,0},{5,7},{6,2},{7,5},{8,12},{9,11},{10,... | collective-permute-start | bytes 344072 | tf_op jit(solution)/shard_map/ppermute | solution.py:383
  45.2 1.4 %collective-permute-start.9 = (bf16[448,128]{1,0:T(8,128)(2,1)S(1)}, bf16[448,128]{1,0:T(8,128)(2,1)S(1)}, u32[]{:S(2)}, u32[]{:S(2)}) collective-permute-start(bf16[448,128]{1,0:T(8,128)(2,1)S(1)} %add_convert_fusion.1.own), channel_id=1, source_target_pairs={{0,1},{1,0},{2,3},{3,2},{4,5},{5,4},{6,7},{7,6},{8,9},{9,8},{10,11... | collective-permute-start | bytes 344072 | tf_op jit(solution)/shard_map/ppermute | solution.py:397

commit v4 on v3

--- a/solution.py
+++ b/solution.py
@@ -34,17 +34,13 @@
         windows[frame, height + 1, :, lanes] = jnp.where(tile == 0, rim, none)
 
 
-def window_rows(pieces, frame, b, height):
-    for first, ref in pieces:
-        if first <= frame < first + ref.shape[0]:
-            block = ref[frame - first, b : b + height]
-            return block.reshape(-1, block.shape[-1])
-
-
-def window_block(pieces, first, height):
-    return jnp.concatenate(
-        [window_rows(pieces, first + f, b, height) for f in range(4) for b in range(3)], axis=1
-    )
+def window_block(frames):
+    blocks = []
+    for frame in frames:
+        height = frame.shape[0] - 2
+        for b in range(3):
+            blocks.append(frame[b : b + height].reshape(-1, frame.shape[-1]))
+    return jnp.concatenate(blocks, axis=1)
 
 
 def activate(pre, source, upstream):
@@ -54,12 +50,10 @@
     return result, grad
 
 
-def forward_pair(pieces, p, taps, bias, x_pair, upstream, height):
+def forward_pair(frames, taps, bias, x_pair, upstream):
     channels = bias.shape[1]
     both = jnp.concatenate([bias[...], bias[...]], axis=1)
-    pre = both + jnp.dot(
-        window_block(pieces, 2 * p, height), taps[...], preferred_element_type=F32
-    )
+    pre = both + jnp.dot(window_block(frames), taps[...], preferred_element_type=F32)
     return [
         activate(
             pre[:, s * channels : (s + 1) * channels],
@@ -101,41 +95,44 @@
     taps[3 * rows :, 0:channels] = jnp.zeros((rows, channels), BF16)
     taps[0:rows, channels:] = jnp.zeros((rows, channels), BF16)
     taps[rows:, channels:] = kernel[...]
-    for f in range(frames):
+    @pl.loop(0, frames)
+    def _(f):
         fill_windows(windows, f, x[f], edge[f], tile)
+
     bias_copy.wait()
     up_copy.wait()
-    summed = jnp.zeros((1, channels), F32)
-    copies = []
-    for p in range(1, frames // 2):
-        grads = []
+    total[...] = jnp.zeros((1, channels), F32)
+
+    def leave(p):
+        return pltpu.make_async_copy(
+            result.at[pl.ds(2 * p, 2)], block_out.at[pl.ds(2 * p + 2, 2)], leaving
+        )
+
+    @pl.loop(0, frames // 2 - 1, unroll=True)
+    def _(p):
         outs = forward_pair(
-            [(2, windows)],
-            p,
+            [windows[2 * p + f] for f in range(4)],
             taps,
             bias_here,
-            [x[2 * p], x[2 * p + 1]],
-            [upstream[2 * p - 2], upstream[2 * p - 1]],
-            height,
+            [x[2 * p + 2], x[2 * p + 3]],
+            [upstream[2 * p], upstream[2 * p + 1]],
         )
+        summed = jnp.zeros((1, channels), F32)
         for s in range(2):
-            t = 2 * p + s - 2
+            t = 2 * p + s
             result[t] = outs[s][0].reshape(height, breadth, channels)
             grad = outs[s][1]
-            grads.append(grad)
             summed = summed + jnp.sum(grad.astype(F32), axis=0, keepdims=True)
             cube = grad.reshape(height, breadth, channels)
             grad_pre[t] = cube
             edge_out[t] = jnp.where(tile == 0, cube[height - 1], cube[0])
-        turned[:, (p - 1) * area : p * area] = jnp.concatenate(grads, axis=1).T
-        copy = pltpu.make_async_copy(
-            result.at[2 * p - 2 : 2 * p], block_out.at[2 * p : 2 * p + 2], leaving.at[p - 1]
-        )
-        copy.start()
-        copies.append(copy)
-    total[...] = summed
-    for copy in copies:
-        copy.wait()
+        turned[p] = jnp.concatenate([outs[0][1], outs[1][1]], axis=1).T
+        total[...] += summed
+        leave(p).start()
+
+    @pl.loop(0, frames // 2 - 1)
+    def _(p):
+        leave(p).wait()
 
 
 def first_frames_kernel(
@@ -168,10 +165,13 @@
         fill_windows(early, f, before[f * height : (f + 1) * height], before[2 * height + f], tile)
     bias_copy.wait()
     up_copy.wait()
-    pieces = [(0, early), (2, windows)]
     summed = total[...]
     firsts = forward_pair(
-        pieces, 0, taps, bias_here, [x[0], x[1]], [upstream[0], upstream[1]], height
+        [early[0], early[1], windows[0], windows[1]],
+        taps,
+        bias_here,
+        [x[0], x[1]],
+        [upstream[0], upstream[1]],
     )
     for s in range(2):
         result[s] = firsts[s][0].reshape(height, breadth, channels)
@@ -182,71 +182,81 @@
     edge_out[2:frames] = edge_in[...]
     copy = pltpu.make_async_copy(result, block_out.at[0:2], leaving)
     copy.start()
+    pairs = frames // 2
+    pairs = frames // 2
     grads = jnp.concatenate(
-        [jnp.concatenate([firsts[0][1], firsts[1][1]], axis=1).T, turned[...]], axis=1
-    )
-    sums = [[None] * 9 for _ in range(3)]
-    for b in range(3):
-        for f in range(4):
+        [
+            part
+            for s in range(2)
+            for part in [firsts[s][1].T]
+            + [turned[p, s * channels : (s + 1) * channels] for p in range(pairs - 1)]
+        ],
+        axis=1,
+    )
+
+    def tap_row(b, write):
+        for a in range(3):
             source = jnp.concatenate(
-                [window_rows(pieces, 2 * p + f, b, height) for p in range(frames // 2)], axis=0
+                [
+                    (early if t + a < 2 else windows)[
+                        t + a - (0 if t + a < 2 else 2), pl.ds(b, height)
+                    ].reshape(area, 3 * channels)
+                    for s in range(2)
+                    for t in range(s, frames, 2)
+                ],
+                axis=0,
             )
-            low = 0 if f < 3 else channels
-            high = 2 * channels if f > 0 else channels
-            product = jnp.dot(grads[low:high], source, preferred_element_type=F32)
+            product = jnp.dot(grads, source, preferred_element_type=F32).astype(BF16)
             for e in range(3):
-                for s in range(2):
-                    a = f - s
-                    if 0 <= a < 3:
-                        piece = product[
-                            s * channels - low : (s + 1) * channels - low,
-                            e * channels : (e + 1) * channels,
-                        ]
-                        at = b * 3 + e
-                        sums[a][at] = piece if sums[a][at] is None else sums[a][at] + piece
-    if not arranged:
-        for k in range(27):
-            outs[0][k] = sums[k // 9][k % 9].T.astype(BF16)
-        outs[1][...] = summed
+                write((a * 3 + b) * 3 + e, product[:, e * channels : (e + 1) * channels].T)
+
+    step = 32
+    per_tap = channels // step
+    if arranged:
+        (parts,) = outs
+        count, half = parts.shape[1], parts.shape[2]
+        me = lax.axis_index("dp")
+        per, per_half = 27 * per_tap // count, half // step
+    else:
+        weights, bias_sum = outs
+
+    def put(j, at, rows):
+        h = at // per_half
+        place = place_of(me, j, count, h)
+        spot = (at - h * per_half) * step
+        if not isinstance(spot, int):
+            spot = pl.multiple_of(spot, step)
+        parts[tile ^ h, place, pl.ds(spot, step)] = rows
+
+    def tap_rows(b):
+        def write(k, block):
+            for i in range(per_tap):
+                r = k * per_tap + i
+                rows = block[i * step : (i + 1) * step]
+                if arranged:
+                    put(r // per, r % per, rows)
+                else:
+                    weights[r] = rows
+
+        tap_row(b, write)
+
+    if arranged:
+        pl.loop(0, 3)(tap_rows)
+    else:
+        for b in range(3):
+            tap_rows(b)
+        bias_sum[...] = summed
         copy.wait()
         return
-    (parts,) = outs
-    count, half = parts.shape[1], parts.shape[2]
-    share = 27 * channels // count
-    me = lax.axis_index("dp")
-
-    def put(j, start, rows):
-        done = 0
-        while done < rows.shape[0]:
-            h = (start + done) // half
-            stop = min(rows.shape[0], (h + 1) * half - start)
-            at = start + done - h * half
-            place = place_of(me, j, count, h)
-            parts[tile ^ h, place, at : at + stop - done] = rows[done:stop]
-            done = stop
-
-    for k in range(27):
-        block = sums[k // 9][k % 9].astype(BF16).T
-        at = k * channels
-        end = at + channels
-        while at < end:
-            j = at // share
-            stop = min(end, (j + 1) * share)
-            put(j, at - j * share, block[at - k * channels : stop - k * channels])
-            at = stop
-    pad = 2 * half - share
-    line = jnp.concatenate([summed, jnp.zeros((pad - 1, channels), F32)], axis=0).astype(BF16)
+    line = jnp.concatenate([summed, jnp.zeros((step - 1, channels), F32)], axis=0).astype(BF16)
     for j in range(count):
-        put(j, share, line)
+        put(j, per, line)
     copy.wait()
 
 
-def back_pair(pieces, p, taps, upstream, height):
+def back_pair(frames, taps, upstream):
     back = lax.dot_general(
-        window_block(pieces, 2 * p, height),
-        taps[...],
-        (((1,), (1,)), ((), ())),
-        preferred_element_type=F32,
+        window_block(frames), taps[...], (((1,), (1,)), ((), ())), preferred_element_type=F32
     )
     channels = back.shape[1] // 2
     return [
@@ -277,31 +287,35 @@
                         taps[where] = kernel[k : k + channels]
                     else:
                         taps[where] = jnp.zeros((channels, channels), BF16)
-    for f in range(frames):
-        cells = early[f] if f < 2 else g[f - 2]
-        if f < frames - 2:
-            fill_windows(windows, f, cells, edge[f], tile)
-        else:
-            fill_windows(last, f - (frames - 2), cells, edge[f], tile)
+    for f in range(2):
+        fill_windows(windows, f, early[f], edge[f], tile)
+
+    @pl.loop(2, frames)
+    def _(f):
+        fill_windows(windows, f, g[f - 2], edge[f], tile)
+
+    last[...] = windows[frames - 2 : frames]
     up_copy.wait()
-    copies = []
-    for p in range(frames // 2 - 1):
+
+    def leave(p):
+        return pltpu.make_async_copy(
+            result.at[pl.ds(2 * p, 2)], grad_input.at[pl.ds(2 * p, 2)], leaving
+        )
+
+    @pl.loop(0, frames // 2 - 1)
+    def _(p):
         pair = back_pair(
-            [(0, windows), (frames - 2, last)],
-            p,
+            [windows[2 * p + f] for f in range(4)],
             taps,
             [upstream[2 * p], upstream[2 * p + 1]],
-            height,
         )
         for s in range(2):
             result[2 * p + s] = pair[s]
-        copy = pltpu.make_async_copy(
-            result.at[2 * p : 2 * p + 2], grad_input.at[2 * p : 2 * p + 2], leaving.at[p]
-        )
-        copy.start()
-        copies.append(copy)
-    for copy in copies:
-        copy.wait()
+        leave(p).start()
+
+    @pl.loop(0, frames // 2 - 1)
+    def _(p):
+        leave(p).wait()
 
 
 def back_last_kernel(
@@ -315,11 +329,7 @@
         fill_windows(windows, f, after[f * height : (f + 1) * height], after[2 * height + f], tile)
     up_copy.wait()
     pair = back_pair(
-        [(frames - 2, last), (frames, windows)],
-        frames // 2 - 1,
-        taps,
-        [upstream[0], upstream[1]],
-        height,
+        [last[0], last[1], windows[0], windows[1]], taps, [upstream[0], upstream[1]]
     )
     for s in range(2):
         result[s] = pair[s]
@@ -465,7 +475,7 @@
         + arrays(
             windows_shape(frames),
             (36 * channels, 2 * channels),
-            (2 * channels, (frames // 2 - 1) * area),
+            (frames // 2 - 1, 2 * channels, area),
             frames_shape(frames - 2),
             (frames - 2, breadth, channels),
         )
@@ -475,7 +485,7 @@
             vmem(frames_shape(frames - 2), BF16),
             vmem(frames_shape(frames - 2), BF16),
             dma((2,)),
-            dma((frames // 2 - 1,)),
+            dma,
         ],
         (3, 4),
         (0,),
@@ -484,7 +494,7 @@
     if arranged:
         partial = arrays((2, shards, half, channels))
     else:
-        partial = arrays((27, channels, channels)) + arrays((1, channels), kind=F32)
+        partial = arrays((27 * channels // 32, 32, channels)) + arrays((1, channels), kind=F32)
     block_out, early_grads, grad_edge, *parts = call(
         functools.partial(first_frames_kernel, arranged=arranged),
         "first_frames_and_weights",
@@ -533,37 +543,47 @@
 
     total = added(kept, swapped(sent))
     edge = swapped(grad_edge)
-    after = passed_along(
-        jnp.concatenate(
-            [early_grads.reshape(2 * height, breadth, channels), edge[:2]], axis=0
-        ),
-        "tm",
-        -1,
-    )
+    edge, total = lax.optimization_barrier((edge, total))
     grad_input, last, taps = call(
         back_interior_kernel,
         "input_gradient_interior",
         0.75,
         [cells] + arrays(windows_shape(2), (2 * channels, 36 * channels)),
         [
-            vmem(windows_shape(frames - 2), BF16),
+            vmem(windows_shape(frames), BF16),
             vmem(frames_shape(frames - 2), BF16),
             vmem(frames_shape(frames - 2), BF16),
             dma,
-            dma((frames // 2 - 1,)),
+            dma,
         ],
         (4,),
         (0,),
         (early_grads, later_grads, edge, kernel, upstream),
     )
-    n = bits_of(shards)
-    for k in range(n):
-        if k == n - 1:
-            total, grad_input = lax.optimization_barrier((total, grad_input))
-        middle = total.shape[0] // 2
-        total = added(
-            total[:middle], exchange(total[middle:], "dp", shards, (1 << k, 1 << (n - 1 - k)))
-        )
+    first_edge, last = lax.optimization_barrier((edge[:2], last))
+    after = passed_along(
+        jnp.concatenate(
+            [early_grads.reshape(2 * height, breadth, channels), first_edge], axis=0
+        ),
+        "tm",
+        -1,
+    )
+    if shards == 4:
+        apart = {1: (2, 1), 2: (1, 2), 3: (3, 3)}
+        parts = [exchange(total[k], "dp", shards, apart[k]) for k in (3, 1, 2)]
+        total = total[0].astype(F32)
+        for part in parts:
+            total = total + part.astype(F32)
+        total = total.astype(BF16)
+    else:
+        n = bits_of(shards)
+        for k in range(n):
+            middle = total.shape[0] // 2
+            total = added(
+                total[:middle], exchange(total[middle:], "dp", shards, (1 << k, 1 << (n - 1 - k)))
+            )
+        total = total[0]
+    total, grad_input = lax.optimization_barrier((total, grad_input))
     (grad_input,) = call(
         back_last_kernel,
         "input_gradient_last",
@@ -581,12 +601,11 @@
         (grad_input, last, after, taps, upstream),
         {0: 0},
     )
-    total = total[0]
-    n = bits_of(steps)
-    for k in range(n):
-        if k == n - 1:
-            total, grad_input = lax.optimization_barrier((total, grad_input))
-        total = added(total, exchange(total, "tm", steps, (1 << k, 1 << (n - 1 - k))))
+    got = {k: exchange(total, "tm", steps, (k, k if k == 3 else 3 - k)) for k in (3, 2, 1)}
+    total = (
+        (total.astype(F32) + got[1].astype(F32)) + (got[2].astype(F32) + got[3].astype(F32))
+    ).astype(BF16)
+    total, grad_input = lax.optimization_barrier((total, grad_input))
     other = swapped(total)
     positions = (
         clip_count * frames * height * breadth * shards * steps * lax.axis_size("tile")

time: 47.8 us -> 44.3 us (0.927)
  waiting for transfers between devices: 13.7 us -> 10.4 us
  Pallas kernels: 16.2 us -> 15.6 us
    ppermute x4 -> x6, waiting for transfers between devices: 9.28 us -> 6.9 us  [exchange(): return lax.ppermute(block, (axis, 'tile'), route)]
    ppermute x2, waiting for transfers between devices: 0.77 us -> 0.01 us  [passed_along(): return lax.ppermute(block, axis, route)]
    pallas_call x6, Pallas kernels: 16.2 us -> 15.6 us  [call(): pl.pallas_call(kernel_body, out_shape=shapes, in_specs=[there if i in far...]
    ppermute x4 -> x6, starting transfers between devices: 8.25 us -> 8.73 us  [exchange(): return lax.ppermute(block, (axis, 'tile'), route)]
  transfers between devices with their start and end apart: 10 -> 12, of which waited for: 8 -> 7; matrix products, arithmetic and copies ran while one was open for 0% -> 0% of each run, Pallas kernels for 20% -> 22%
where the time goes in v4:
time: 44.3 us; the launch traced here: 44.1 us
  starting transfers between devices  15.9 us (36%)
  Pallas kernels  15.6 us (35%)
  waiting for transfers between devices  10.4 us (23%)
  local copies, waits for them, and re-layouts  1.11 us (3%)
  between operations  0.81 us (2%)
    pallas_call x6, Pallas kernels, call(): pl.pallas_call(kernel_body, out_shape=shapes, in_specs=[there if i in far...  15.6 us
    ppermute x6, starting transfers between devices, exchange(): return lax.ppermute(block, (axis, 'tile'), route)  8.73 us
    ppermute x6, waiting for transfers between devices, exchange(): return lax.ppermute(block, (axis, 'tile'), route)  6.9 us
    ppermute x2, starting transfers between devices, passed_along(): return lax.ppermute(block, axis, route)  6.04 us
    ppermute x4, waiting for transfers between devices, swapped(): return lax.ppermute(block, 'tile', [(0, 1), (1, 0)])  3.52 us
    ppermute x4, starting transfers between devices, swapped(): return lax.ppermute(block, 'tile', [(0, 1), (1, 0)])  1.16 us
    unnamed x8, local copies, waits for them, and re-layouts  1.05 us
  transfers between devices with their start and end apart: 12, of which 7 were waited for; matrix products, arithmetic and copies ran while one was open for 0% of the time, Pallas kernels for 22%

profile of v4, /device:TPU:0, one launch (start us, length us, event | category | flops | bytes accessed | tf_op | source)
XLA Modules:
  0.0 44.1 jit_solution(2590158049834088508)
XLA Ops:
  0.6 1.0 %copy-done.2 = bf16[1,8,8,32,128]{4,3,2,1,0:T(8,128)(2,1)S(1)} copy-done((bf16[1,8,8,32,128]{4,3,2,1,0:T(8,128)(2,1)S(1)}, bf16[1,8,8,32,128]{4,3,2,1,0:T(8,128)(2,1)}, u32[]{:S(2)}) %copy-start.2) | copy-done | bytes 524312
  1.7 0.2 border_rows.1
  1.9 0.5 %collective-permute-start = (bf16[8,32,128]{2,1,0:T(8,128)(2,1)S(1)}, bf16[8,32,128]{2,1,0:T(8,128)(2,1)S(1)}, u32[]{:S(2)}, u32[]{:S(2)}) collective-permute-start(bf16[8,32,128]{2,1,0:T(8,128)(2,1)S(1)} %get-tuple-element.30), channel_id=1, source_target_pairs={{0,1},{1,0},{2,3},{3,2},{4,5},{5,4},{6,7},{7,6},{8,9},{9,8},{10,11... | collective-permute-start | bytes 196616 | tf_op jit(solution)/shard_map/ppermute | solution.py:407
  2.4 0.9 %collective-permute-done.edge = bf16[8,32,128]{2,1,0:T(8,128)(2,1)S(1)} collective-permute-done((bf16[8,32,128]{2,1,0:T(8,128)(2,1)S(1)}, bf16[8,32,128]{2,1,0:T(8,128)(2,1)S(1)}, u32[]{:S(2)}, u32[]{:S(2)}) %collective-permute-start) | collective-permute-done | bytes 65568 | tf_op jit(solution)/shard_map/ppermute | solution.py:407
  3.3 4.8 %collective-permute-start.1 = (bf16[18,32,128]{2,1,0:T(8,128)(2,1)S(1)}, bf16[18,32,128]{2,1,0:T(8,128)(2,1)S(1)}, u32[]{:S(2)}, u32[]{:S(2)}) collective-permute-start(bf16[18,32,128]{2,1,0:T(8,128)(2,1)S(1)} %pad_maximum_fusion), channel_id=1, source_target_pairs={{0,2},{2,4},{4,6},{1,3},{3,5},{5,7},{8,10},{10,12},{12,14},{9,11},... | collective-permute-start | bytes 442376 | tf_op jit(solution)/shard_map/ppermute | solution.py:403
  8.1 4.0 %forward_interior.1 = (bf16[8,8,32,128]{3,2,1,0:T(8,128)(2,1)}, bf16[8,10,32,384]{3,2,1,0:T(8,128)(2,1)S(1)}, bf16[4608,256]{1,0:T(8,128)(2,1)S(1)}, bf16[3,256,...) custom-call(bf16[8,8,32,128]{3,2,1,0:T(8,128)(2,1)S(1)} %bitcast.29,, ...), custom_call_target="tpu_custom_call" | custom-call | flops 2717908992 | bytes 4194304 | tf_op jit(solution)/shard_map/forward_interior/pallas_call | solution.py:435
  12.1 0.0 collective-permute-done.1.before
  12.1 4.5 %first_frames_and_weights.1 = (bf16[8,8,32,128]{3,2,1,0:T(8,128)(2,1)}, bf16[2,8,32,128]{3,2,1,0:T(8,128)(2,1)S(1)}, bf16[8,32,128]{2,1,0:T(8,128)(2,1)S(1)}, bf16[2,4,448,128]{3,2,1,0:T(8,128)(2,1)S(1)}) custom-call(bf16[8,8,32,128]{3,2,1,0:T(8,128)(2,1)} %get-tuple-element.31.block_in, ...), custom_call_target="tpu_custom_call", output_to_operand_aliasing={{0}: (0, {})} | custom-call | flops 4529848320 | bytes 4194304 | tf_op jit(solution)/shard_map/first_frames_and_weights/pallas_call | solution.py:435
  16.6 0.1 collective-permute-start.3
  16.7 0.5 %collective-permute-start.2 = (bf16[8,32,128]{2,1,0:T(8,128)(2,1)S(1)}, bf16[8,32,128]{2,1,0:T(8,128)(2,1)S(1)}, u32[]{:S(2)}, u32[]{:S(2)}) collective-permute-start(bf16[8,32,128]{2,1,0:T(8,128)(2,1)S(1)} %get-tuple-element.39), channel_id=1, source_target_pairs={{0,1},{1,0},{2,3},{3,2},{4,5},{5,4},{6,7},{7,6},{8,9},{9,8},{10,11... | collective-permute-start | bytes 196616 | tf_op jit(solution)/shard_map/ppermute | solution.py:407
  17.2 1.3 %collective-permute-done.3 = bf16[4,448,128]{2,1,0:T(8,128)(2,1)S(1)} collective-permute-done((bf16[4,448,128]{2,1,0:T(8,128)(2,1)S(1)}, bf16[4,448,128]{2,1,0:T(8,128)(2,1)S(1)}, u32[]{:S(2)}, u32[]{:S(2)}) %collective-permute-start.3) | collective-permute-done | bytes 458784 | tf_op jit(solution)/shard_map/ppermute | solution.py:407
  18.5 0.1 fusion
  18.7 0.0 collective-permute-done.2.edge
  18.7 3.7 %collective-permute-start.4 = (bf16[448,128]{1,0:T(8,128)(2,1)S(1)}, bf16[448,128]{1,0:T(8,128)(2,1)S(1)}, u32[]{:S(2)}, u32[]{:S(2)}) collective-permute-start(bf16[448,128]{1,0:T(8,128)(2,1)S(1)} %get-tuple-element.56), channel_id=1, source_target_pairs={{0,24},{1,25},{8,16},{9,17},{16,8},{17,9},{24,0},{25,1},{2,26},{3,... | collective-permute-start | bytes 344072 | tf_op jit(solution)/shard_map/ppermute | solution.py:393
  22.4 0.0 collective-permute-start.6
  22.4 0.8 %collective-permute-start.5 = (bf16[448,128]{1,0:T(8,128)(2,1)S(1)}, bf16[448,128]{1,0:T(8,128)(2,1)S(1)}, u32[]{:S(2)}, u32[]{:S(2)}) collective-permute-start(bf16[448,128]{1,0:T(8,128)(2,1)S(1)} %get-tuple-element.58), channel_id=1, source_target_pairs={{0,16},{1,9},{8,24},{9,1},{16,0},{17,25},{24,8},{25,17},{2,18},{3,... | collective-permute-start | bytes 344072 | tf_op jit(solution)/shard_map/ppermute | solution.py:393
  23.2 4.1 %input_gradient_interior.1 = (bf16[8,8,32,128]{3,2,1,0:T(8,128)(2,1)}, bf16[2,10,32,384]{3,2,1,0:T(8,128)(2,1)S(1)}, bf16[256,4608]{1,0:T(8,128)(2,1)S(1)}) custom-call(bf16[2,8,32,128]{3,2,1,0:T(8,128)(2,1)S(1)} %get-tuple-element.42.early, bf16[6,8,32,128]{3,2,1,0:T(8,128)(2,1)S(1)} %get-tuple-element.43.g, ...), custom_call_target="tpu_custom_call" | custom-call | flops 2717908992 | bytes 4194304 | tf_op jit(solution)/shard_map/input_gradient_interior/pallas_call | solution.py:435
  27.3 1.3 %collective-permute-start.10 = (bf16[18,32,128]{2,1,0:T(8,128)(2,1)S(1)}, bf16[18,32,128]{2,1,0:T(8,128)(2,1)S(1)}, u32[]{:S(2)}, u32[]{:S(2)}) collective-permute-start(bf16[18,32,128]{2,1,0:T(8,128)(2,1)S(1)} %pad_maximum_fusion.1), channel_id=1, source_target_pairs={{2,0},{4,2},{6,4},{3,1},{5,3},{7,5},{10,8},{12,10},{14,12},{11,9},... | collective-permute-start | bytes 442376 | tf_op jit(solution)/shard_map/ppermute | solution.py:403
  28.6 0.0 collective-permute-done.4
  28.6 0.3 collective-permute-done.6
  28.9 3.4 %collective-permute-done.5 = bf16[448,128]{1,0:T(8,128)(2,1)S(1)} collective-permute-done((bf16[448,128]{1,0:T(8,128)(2,1)S(1)}, bf16[448,128]{1,0:T(8,128)(2,1)S(1)}, u32[]{:S(2)}, u32[]{:S(2)}) %collective-permute-start.5) | collective-permute-done | bytes 114720 | tf_op jit(solution)/shard_map/ppermute | solution.py:393
  32.3 0.1 fusion.3
  32.4 2.8 %collective-permute-start.9 = (bf16[448,128]{1,0:T(8,128)(2,1)S(1)}, bf16[448,128]{1,0:T(8,128)(2,1)S(1)}, u32[]{:S(2)}, u32[]{:S(2)}) collective-permute-start(bf16[448,128]{1,0:T(8,128)(2,1)S(1)} %fusion.3), channel_id=1, source_target_pairs={{0,6},{1,7},{2,4},{3,5},{4,2},{5,3},{6,0},{7,1},{8,14},{9,15},{10,... | collective-permute-start | bytes 344072 | tf_op jit(solution)/shard_map/ppermute | solution.py:393
  35.3 0.5 %collective-permute-start.8 = (bf16[448,128]{1,0:T(8,128)(2,1)S(1)}, bf16[448,128]{1,0:T(8,128)(2,1)S(1)}, u32[]{:S(2)}, u32[]{:S(2)}) collective-permute-start(bf16[448,128]{1,0:T(8,128)(2,1)S(1)} %fusion.3), channel_id=1, source_target_pairs={{0,4},{1,3},{2,6},{3,1},{4,0},{5,7},{6,2},{7,5},{8,12},{9,11},{10,... | collective-permute-start | bytes 344072 | tf_op jit(solution)/shard_map/ppermute | solution.py:393
  35.8 0.9 %collective-permute-start.7 = (bf16[448,128]{1,0:T(8,128)(2,1)S(1)}, bf16[448,128]{1,0:T(8,128)(2,1)S(1)}, u32[]{:S(2)}, u32[]{:S(2)}) collective-permute-start(bf16[448,128]{1,0:T(8,128)(2,1)S(1)} %fusion.3), channel_id=1, source_target_pairs={{0,2},{1,5},{2,0},{3,7},{4,6},{5,1},{6,4},{7,3},{8,10},{9,13},{10,... | collective-permute-start | bytes 344072 | tf_op jit(solution)/shard_map/ppermute | solution.py:393
  36.7 1.7 %input_gradient_last.1 = bf16[8,8,32,128]{3,2,1,0:T(8,128)(2,1)} custom-call(bf16[8,8,32,128]{3,2,1,0:T(8,128)(2,1)} %get-tuple-element.47.grad_in, bf16[2,10,32,384]{3,2,1,0:T(8,128)(2,1)S(1)} %get-tuple-element.49.last, bf16[18,32,128]{2,1,0:T(8,128)(2,1)S(1)} %collective-permute-done.10.after, ...), custom_call_target="tpu_custom_call", output_to_operand_aliasing={{}: (0, {})} | custom-call | flops 905969664 | bytes 4194304 | tf_op jit(solution)/shard_map/input_gradient_last/pallas_call | solution.py:435
  38.5 1.9 %collective-permute-done.9 = bf16[448,128]{1,0:T(8,128)(2,1)S(1)} collective-permute-done((bf16[448,128]{1,0:T(8,128)(2,1)S(1)}, bf16[448,128]{1,0:T(8,128)(2,1)S(1)}, u32[]{:S(2)}, u32[]{:S(2)}) %collective-permute-start.9) | collective-permute-done | bytes 114720 | tf_op jit(solution)/shard_map/ppermute | solution.py:393
  40.4 1.2 %collective-permute-done.8 = bf16[448,128]{1,0:T(8,128)(2,1)S(1)} collective-permute-done((bf16[448,128]{1,0:T(8,128)(2,1)S(1)}, bf16[448,128]{1,0:T(8,128)(2,1)S(1)}, u32[]{:S(2)}, u32[]{:S(2)}) %collective-permute-start.8) | collective-permute-done | bytes 114720 | tf_op jit(solution)/shard_map/ppermute | solution.py:393
  41.6 0.1 add_convert_fusion.own
  41.7 0.1 collective-permute-start.11
  41.8 1.3 %collective-permute-done.11.other = bf16[448,128]{1,0:T(8,128)(2,1)S(1)} collective-permute-done((bf16[448,128]{1,0:T(8,128)(2,1)S(1)}, bf16[448,128]{1,0:T(8,128)(2,1)S(1)}, u32[]{:S(2)}, u32[]{:S(2)}) %collective-permute-start.11) | collective-permute-done | bytes 114720 | tf_op jit(solution)/shard_map/ppermute | solution.py:407
  43.1 1.0 %scaled_weights.1 = (f32[864,128]{1,0:T(8,128)}, f32[1,32]{1,0:T(1,128)}) custom-call(bf16[448,128]{1,0:T(8,128)(2,1)S(1)} %add_convert_fusion.own, bf16[448,128]{1,0:T(8,128)(2,1)S(1)} %collective-permute-done.11.other), custom_call_target="tpu_custom_call" | custom-call | flops 36238784 | bytes 4194304 | tf_op jit(solution)/shard_map/scaled_weights/pallas_call | solution.py:435
  (15 shorter events, 0.1 us)
Async XLA Ops:
  0.6 1.0 %copy-start.2 = (bf16[1,8,8,32,128]{4,3,2,1,0:T(8,128)(2,1)S(1)}, bf16[1,8,8,32,128]{4,3,2,1,0:T(8,128)(2,1)}, u32[]{:S(2)}) copy-start(bf16[1,8,8,32,128]{4,3,2,1,0:T(8,128)(2,1)} %param.4) | copy-start | bytes 1572868
  1.7 6.4 %copy-start = (bf16[1,8,8,32,128]{4,3,2,1,0:T(8,128)(2,1)S(1)}, bf16[1,8,8,32,128]{4,3,2,1,0:T(8,128)(2,1)}, u32[]{:S(2)}) copy-start(bf16[1,8,8,32,128]{4,3,2,1,0:T(8,128)(2,1)} %param.7) | copy-start | bytes 1572868
  1.7 6.4 %copy-start.1 = (bf16[3456,128]{1,0:T(8,128)(2,1)S(1)}, bf16[3456,128]{1,0:T(8,128)(2,1)}, u32[]{:S(2)}) copy-start(bf16[3456,128]{1,0:T(8,128)(2,1)} %kernel.3) | copy-start | bytes 2654212
  1.7 6.4 %copy-start.3 = (f32[128]{0:T(128)S(1)}, f32[128]{0:T(128)}, u32[]{:S(2)}) copy-start(f32[128]{0:T(128)} %param.6) | copy-start | bytes 1540
  1.9 1.4 %collective-permute-start = (bf16[8,32,128]{2,1,0:T(8,128)(2,1)S(1)}, bf16[8,32,128]{2,1,0:T(8,128)(2,1)S(1)}, u32[]{:S(2)}, u32[]{:S(2)}) collective-permute-start(bf16[8,32,128]{2,1,0:T(8,128)(2,1)S(1)} %get-tuple-element.30), channel_id=1, source_target_pairs={{0,1},{1,0},{2,3},{3,2},{4,5},{5,4},{6,7},{7,6},{8,9},{9,8},{10,11... | collective-permute-start | bytes 196616 | tf_op jit(solution)/shard_map/ppermute | solution.py:407
  3.3 8.8 %collective-permute-start.1 = (bf16[18,32,128]{2,1,0:T(8,128)(2,1)S(1)}, bf16[18,32,128]{2,1,0:T(8,128)(2,1)S(1)}, u32[]{:S(2)}, u32[]{:S(2)}) collective-permute-start(bf16[18,32,128]{2,1,0:T(8,128)(2,1)S(1)} %pad_maximum_fusion), channel_id=1, source_target_pairs={{0,2},{2,4},{4,6},{1,3},{3,5},{5,7},{8,10},{10,12},{12,14},{9,11},... | collective-permute-start | bytes 442376 | tf_op jit(solution)/shard_map/ppermute | solution.py:403
  16.6 1.9 %collective-permute-start.3 = (bf16[4,448,128]{2,1,0:T(8,128)(2,1)S(1)}, bf16[4,448,128]{2,1,0:T(8,128)(2,1)S(1)}, u32[]{:S(2)}, u32[]{:S(2)}) collective-permute-start(bf16[4,448,128]{2,1,0:T(8,128)(2,1)S(1)} %slice_bitcast_fusion), channel_id=1, source_target_pairs={{0,1},{1,0},{2,3},{3,2},{4,5},{5,4},{6,7},{7,6},{8,9},{9,8},{10,11... | collective-permute-start | bytes 1376264 | tf_op jit(solution)/shard_map/ppermute | solution.py:407
  16.7 1.9 %collective-permute-start.2 = (bf16[8,32,128]{2,1,0:T(8,128)(2,1)S(1)}, bf16[8,32,128]{2,1,0:T(8,128)(2,1)S(1)}, u32[]{:S(2)}, u32[]{:S(2)}) collective-permute-start(bf16[8,32,128]{2,1,0:T(8,128)(2,1)S(1)} %get-tuple-element.39), channel_id=1, source_target_pairs={{0,1},{1,0},{2,3},{3,2},{4,5},{5,4},{6,7},{7,6},{8,9},{9,8},{10,11... | collective-permute-start | bytes 196616 | tf_op jit(solution)/shard_map/ppermute | solution.py:407
  18.7 9.9 %collective-permute-start.4 = (bf16[448,128]{1,0:T(8,128)(2,1)S(1)}, bf16[448,128]{1,0:T(8,128)(2,1)S(1)}, u32[]{:S(2)}, u32[]{:S(2)}) collective-permute-start(bf16[448,128]{1,0:T(8,128)(2,1)S(1)} %get-tuple-element.56), channel_id=1, source_target_pairs={{0,24},{1,25},{8,16},{9,17},{16,8},{17,9},{24,0},{25,1},{2,26},{3,... | collective-permute-start | bytes 344072 | tf_op jit(solution)/shard_map/ppermute | solution.py:393
  22.4 6.5 %collective-permute-start.6 = (bf16[448,128]{1,0:T(8,128)(2,1)S(1)}, bf16[448,128]{1,0:T(8,128)(2,1)S(1)}, u32[]{:S(2)}, u32[]{:S(2)}) collective-permute-start(bf16[448,128]{1,0:T(8,128)(2,1)S(1)} %get-tuple-element.57), channel_id=1, source_target_pairs={{0,8},{1,17},{8,0},{9,25},{16,24},{17,1},{24,16},{25,9},{2,10},{3,... | collective-permute-start | bytes 344072 | tf_op jit(solution)/shard_map/ppermute | solution.py:393
  22.4 10.0 %collective-permute-start.5 = (bf16[448,128]{1,0:T(8,128)(2,1)S(1)}, bf16[448,128]{1,0:T(8,128)(2,1)S(1)}, u32[]{:S(2)}, u32[]{:S(2)}) collective-permute-start(bf16[448,128]{1,0:T(8,128)(2,1)S(1)} %get-tuple-element.58), channel_id=1, source_target_pairs={{0,16},{1,9},{8,24},{9,1},{16,0},{17,25},{24,8},{25,17},{2,18},{3,... | collective-permute-start | bytes 344072 | tf_op jit(solution)/shard_map/ppermute | solution.py:393
  27.3 9.4 %collective-permute-start.10 = (bf16[18,32,128]{2,1,0:T(8,128)(2,1)S(1)}, bf16[18,32,128]{2,1,0:T(8,128)(2,1)S(1)}, u32[]{:S(2)}, u32[]{:S(2)}) collective-permute-start(bf16[18,32,128]{2,1,0:T(8,128)(2,1)S(1)} %pad_maximum_fusion.1), channel_id=1, source_target_pairs={{2,0},{4,2},{6,4},{3,1},{5,3},{7,5},{10,8},{12,10},{14,12},{11,9},... | collective-permute-start | bytes 442376 | tf_op jit(solution)/shard_map/ppermute | solution.py:403
  32.4 8.0 %collective-permute-start.9 = (bf16[448,128]{1,0:T(8,128)(2,1)S(1)}, bf16[448,128]{1,0:T(8,128)(2,1)S(1)}, u32[]{:S(2)}, u32[]{:S(2)}) collective-permute-start(bf16[448,128]{1,0:T(8,128)(2,1)S(1)} %fusion.3), channel_id=1, source_target_pairs={{0,6},{1,7},{2,4},{3,5},{4,2},{5,3},{6,0},{7,1},{8,14},{9,15},{10,... | collective-permute-start | bytes 344072 | tf_op jit(solution)/shard_map/ppermute | solution.py:393
  35.3 6.4 %collective-permute-start.8 = (bf16[448,128]{1,0:T(8,128)(2,1)S(1)}, bf16[448,128]{1,0:T(8,128)(2,1)S(1)}, u32[]{:S(2)}, u32[]{:S(2)}) collective-permute-start(bf16[448,128]{1,0:T(8,128)(2,1)S(1)} %fusion.3), channel_id=1, source_target_pairs={{0,4},{1,3},{2,6},{3,1},{4,0},{5,7},{6,2},{7,5},{8,12},{9,11},{10,... | collective-permute-start | bytes 344072 | tf_op jit(solution)/shard_map/ppermute | solution.py:393
  35.8 5.9 %collective-permute-start.7 = (bf16[448,128]{1,0:T(8,128)(2,1)S(1)}, bf16[448,128]{1,0:T(8,128)(2,1)S(1)}, u32[]{:S(2)}, u32[]{:S(2)}) collective-permute-start(bf16[448,128]{1,0:T(8,128)(2,1)S(1)} %fusion.3), channel_id=1, source_target_pairs={{0,2},{1,5},{2,0},{3,7},{4,6},{5,1},{6,4},{7,3},{8,10},{9,13},{10,... | collective-permute-start | bytes 344072 | tf_op jit(solution)/shard_map/ppermute | solution.py:393
  41.7 1.4 %collective-permute-start.11 = (bf16[448,128]{1,0:T(8,128)(2,1)S(1)}, bf16[448,128]{1,0:T(8,128)(2,1)S(1)}, u32[]{:S(2)}, u32[]{:S(2)}) collective-permute-start(bf16[448,128]{1,0:T(8,128)(2,1)S(1)} %add_convert_fusion.own), channel_id=1, source_target_pairs={{0,1},{1,0},{2,3},{3,2},{4,5},{5,4},{6,7},{7,6},{8,9},{9,8},{10,11... | collective-permute-start | bytes 344072 | tf_op jit(solution)/shard_map/ppermute | solution.py:407

commit v5 on v4

--- a/solution.py
+++ b/solution.py
@@ -135,27 +135,87 @@
         leave(p).wait()
 
 
-def first_frames_kernel(
-    block_in,
-    x,
-    edge,
-    before,
-    bias,
-    cotangent,
-    windows,
-    taps,
-    turned,
-    edge_in,
-    total,
-    block_out,
-    grad_pre,
-    edge_out,
-    *rest,
-    arranged,
+STEP = 32
+GROUP = 12
+HALVES = (
+    (
+        (*range(0, 12), 24, 25),
+        (*range(36, 48), 27, 28),
+        (*range(60, 74),),
+        (*range(84, 96), 81, 82),
+    ),
+    (
+        (*range(12, 24), 26),
+        (*range(29, 36), *range(48, 54)),
+        (*range(54, 60), *range(74, 81)),
+        (*range(96, 108), 83),
+    ),
+)
+LEAVING = (0x866421, 0x765320)
+STAYING = (0x7530, 0x8841)
+COUNTS = {LEAVING: (6, 3), STAYING: (4, 4)}
+
+
+def runs_of(steps):
+    runs = []
+    for position, step in enumerate(steps):
+        if runs and step == runs[-1][1] + runs[-1][2] and step % GROUP:
+            runs[-1][2] += 1
+        else:
+            runs.append([position, step, 1])
+    return runs
+
+
+def place_half(target, half, blocks, total, me):
+    for j, steps in enumerate(HALVES[half]):
+        spot = me ^ j
+        for position, step, count in runs_of(steps):
+            g, at = step // GROUP, step % GROUP * STEP
+            target[spot, position * STEP : (position + count) * STEP] = blocks(
+                g, at, at + count * STEP
+            )
+        if half == 1:
+            line = jnp.concatenate(
+                [total, jnp.zeros((STEP - 1, total.shape[1]), F32)], axis=0
+            ).astype(BF16)
+            target[spot, len(steps) * STEP : (len(steps) + 1) * STEP] = line
+
+
+def group_loop(codes, front, windows, grads, blocks, tile):
+    channels = grads.shape[0]
+    frames = windows.shape[0]
+    height = windows.shape[1] - 2
+    code = jnp.where(tile == 0, codes[0], codes[1])
+    count, together = COUNTS[codes]
+
+    @pl.loop(0, count // together)
+    def _(i):
+        for k in range(together):
+            g = lax.shift_right_logical(code, 4 * (together * i + k)) & 15
+            a, b = g // 3, g % 3
+            source = jnp.concatenate(
+                [
+                    (
+                        front[t + a, pl.ds(b, height)]
+                        if t < 2
+                        else windows[t - 2 + a, pl.ds(b, height)]
+                    ).reshape(-1, 3 * channels)
+                    for s in range(2)
+                    for t in range(s, frames, 2)
+                ],
+                axis=0,
+            )
+            product = jnp.dot(grads[...], source, preferred_element_type=F32).astype(BF16)
+            for e in range(3):
+                lanes = slice(e * channels, (e + 1) * channels)
+                blocks[g, lanes] = product[:, lanes].T
+
+
+def first_frames(
+    x, before, bias, cotangent, windows, taps, turned, edge_in, total, block_out, grad_pre, edge_out,
+    early, bias_here, upstream, result, arriving, leaving,
 ):
-    outs, (early, bias_here, upstream, result, arriving, leaving) = rest[:-6], rest[-6:]
     frames, height, breadth, channels = x.shape
-    area = height * breadth
     tile = lax.axis_index("tile")
     bias_copy = pltpu.make_async_copy(bias, bias_here, arriving.at[0])
     up_copy = pltpu.make_async_copy(cotangent.at[0:2], upstream, arriving.at[1])
@@ -182,25 +242,76 @@
     edge_out[2:frames] = edge_in[...]
     copy = pltpu.make_async_copy(result, block_out.at[0:2], leaving)
     copy.start()
-    pairs = frames // 2
-    pairs = frames // 2
     grads = jnp.concatenate(
         [
             part
             for s in range(2)
             for part in [firsts[s][1].T]
-            + [turned[p, s * channels : (s + 1) * channels] for p in range(pairs - 1)]
+            + [turned[p, s * channels : (s + 1) * channels] for p in range(frames // 2 - 1)]
         ],
         axis=1,
     )
-
-    def tap_row(b, write):
+    return grads, summed, copy
+
+
+def leaving_half_kernel(
+    block_in, x, before, bias, cotangent, windows, taps, turned, edge_in, total,
+    block_out, grad_pre, edge_out, sent, blocks, front, grads, total_out,
+    bias_here, upstream, result, arriving, leaving,
+):
+    tile = lax.axis_index("tile")
+    me = lax.axis_index("dp")
+    front[2:4] = windows[0:2]
+    values, summed, copy = first_frames(
+        x, before, bias, cotangent, windows, taps, turned, edge_in, total, block_out, grad_pre, edge_out,
+        front, bias_here, upstream, result, arriving, leaving,
+    )
+    grads[...] = values
+    total_out[...] = summed
+    group_loop(LEAVING, front, windows, grads, blocks, tile)
+    for own in range(2):
+
+        @pl.when(tile == own)
+        def _():
+            place_half(sent, 1 - own, lambda g, low, high: blocks[g, low:high], summed, me)
+
+    copy.wait()
+
+
+def staying_half_kernel(blocks_in, front, windows, grads, total, kept, blocks):
+    tile = lax.axis_index("tile")
+    me = lax.axis_index("dp")
+    group_loop(STAYING, front, windows, grads, blocks, tile)
+    for own in range(2):
+        mine = [STAYING[own] >> 4 * i & 15 for i in range(COUNTS[STAYING][0])]
+
+        @pl.when(tile == own)
+        def _():
+            place_half(
+                kept,
+                own,
+                lambda g, low, high: (blocks if g in mine else blocks_in)[g, low:high],
+                total[...],
+                me,
+            )
+
+
+def whole_weights_kernel(
+    block_in, x, before, bias, cotangent, windows, taps, turned, edge_in, total,
+    block_out, grad_pre, edge_out, weights, bias_sum,
+    early, bias_here, upstream, result, arriving, leaving,
+):
+    frames, height, breadth, channels = x.shape
+    grads, summed, copy = first_frames(
+        x, before, bias, cotangent, windows, taps, turned, edge_in, total, block_out, grad_pre, edge_out,
+        early, bias_here, upstream, result, arriving, leaving,
+    )
+    for b in range(3):
         for a in range(3):
             source = jnp.concatenate(
                 [
-                    (early if t + a < 2 else windows)[
-                        t + a - (0 if t + a < 2 else 2), pl.ds(b, height)
-                    ].reshape(area, 3 * channels)
+                    (early[t + a, b : b + height] if t + a < 2 else windows[t + a - 2, b : b + height])
+                    .reshape(-1, 3 * channels)
                     for s in range(2)
                     for t in range(s, frames, 2)
                 ],
@@ -208,49 +319,8 @@
             )
             product = jnp.dot(grads, source, preferred_element_type=F32).astype(BF16)
             for e in range(3):
-                write((a * 3 + b) * 3 + e, product[:, e * channels : (e + 1) * channels].T)
-
-    step = 32
-    per_tap = channels // step
-    if arranged:
-        (parts,) = outs
-        count, half = parts.shape[1], parts.shape[2]
-        me = lax.axis_index("dp")
-        per, per_half = 27 * per_tap // count, half // step
-    else:
-        weights, bias_sum = outs
-
-    def put(j, at, rows):
-        h = at // per_half
-        place = place_of(me, j, count, h)
-        spot = (at - h * per_half) * step
-        if not isinstance(spot, int):
-            spot = pl.multiple_of(spot, step)
-        parts[tile ^ h, place, pl.ds(spot, step)] = rows
-
-    def tap_rows(b):
-        def write(k, block):
-            for i in range(per_tap):
-                r = k * per_tap + i
-                rows = block[i * step : (i + 1) * step]
-                if arranged:
-                    put(r // per, r % per, rows)
-                else:
-                    weights[r] = rows
-
-        tap_row(b, write)
-
-    if arranged:
-        pl.loop(0, 3)(tap_rows)
-    else:
-        for b in range(3):
-            tap_rows(b)
-        bias_sum[...] = summed
-        copy.wait()
-        return
-    line = jnp.concatenate([summed, jnp.zeros((step - 1, channels), F32)], axis=0).astype(BF16)
-    for j in range(count):
-        put(j, per, line)
+                weights[(a * 3 + b) * 3 + e] = product[:, e * channels : (e + 1) * channels].T
+    bias_sum[...] = summed
     copy.wait()
 
 
@@ -351,21 +421,35 @@
         copy.wait()
 
 
-def closing_kernel(own, other, weight, bias, *, scale):
+def closing_kernel(own, other, weight, bias, *, scale, arranged):
     tile = lax.axis_index("tile")
+    me = lax.axis_index("dp")
     half, channels = own.shape
-    rest = weight.shape[0] - half
     mine, theirs = own[...].astype(F32) * scale, other[...].astype(F32) * scale
-    first = jnp.where(tile == 0, mine, theirs)
-    second = jnp.where(tile == 0, theirs, mine)
-    weight[0:half] = first
-    weight[half:] = second[0:rest]
-    line = second[rest : rest + 1]
+    halves = jnp.where(tile == 0, mine, theirs), jnp.where(tile == 0, theirs, mine)
+    if arranged:
+        per = weight.shape[0] // STEP
+        at = (len(HALVES[1][0]) * STEP) % half
+        for j in range(len(HALVES[0])):
+
+            @pl.when(me == j)
+            def _():
+                for h in range(2):
+                    for position, step, count in runs_of(HALVES[h][j]):
+                        q = (step - j * per) * STEP
+                        weight[q : q + count * STEP] = halves[h][
+                            position * STEP : (position + count) * STEP
+                        ]
+
+    else:
+        at = weight.shape[0] - half
+        weight[0:half] = halves[0]
+        weight[half:] = halves[1][0:at]
+    line = halves[1][at : at + 1]
     share = bias.shape[1]
-    spot = lax.axis_index("dp") * share
     picked = jnp.zeros((1, share), F32)
     for j in range(channels // share):
-        picked = jnp.where(spot == j * share, line[:, j * share : (j + 1) * share], picked)
+        picked = jnp.where(me == j, line[:, j * share : (j + 1) * share], picked)
     bias[...] = picked
 
 
@@ -415,7 +499,7 @@
     steps = lax.axis_size("tm")
     share = 27 * channels // shards
     half = -(-(share + 1) // 32) * 16
-    arranged = share % 32 == 0
+    arranged = shards == 4 and channels == 128
 
     area = height * breadth
     bias = conv_bias.reshape(1, channels)
@@ -491,45 +575,58 @@
         (0,),
         (x, edge, kernel, bias, upstream),
     )
+    front_scratch = [
+        vmem((1, channels), F32),
+        vmem(frames_shape(2), BF16),
+        vmem(frames_shape(2), BF16),
+        dma((2,)),
+        dma,
+    ]
+    firsts = [cells] + arrays(frames_shape(2), (frames, breadth, channels))
+    operands = (
+        block_out, x, before, bias, upstream, windows, taps, turned, later_edge, total,
+    )
     if arranged:
-        partial = arrays((2, shards, half, channels))
+        groups = arrays((9, 3 * channels, channels))
+        block_out, early_grads, grad_edge, sent, blocks, front, grads, total = call(
+            leaving_half_kernel,
+            "first_frames_and_leaving_half",
+            0.8,
+            firsts
+            + arrays((shards, half, channels))
+            + groups
+            + arrays(windows_shape(4), (channels, frames * area))
+            + arrays((1, channels), kind=F32),
+            front_scratch,
+            (0, 3, 4),
+            (0,),
+            operands,
+            {0: 0},
+        )
+        (kept,) = call(
+            staying_half_kernel,
+            "staying_half",
+            0.45,
+            arrays((shards, half, channels)),
+            [vmem((9, 3 * channels, channels), BF16)],
+            (),
+            (),
+            (blocks, front, windows, grads, total),
+        )
     else:
-        partial = arrays((27 * channels // 32, 32, channels)) + arrays((1, channels), kind=F32)
-    block_out, early_grads, grad_edge, *parts = call(
-        functools.partial(first_frames_kernel, arranged=arranged),
-        "first_frames_and_weights",
-        1.25,
-        [cells] + arrays(frames_shape(2), (frames, breadth, channels)) + partial,
-        [
-            vmem(windows_shape(2), BF16),
-            vmem((1, channels), F32),
-            vmem(frames_shape(2), BF16),
-            vmem(frames_shape(2), BF16),
-            dma((2,)),
-            dma,
-        ],
-        (0, 4, 5),
-        (0,),
-        (
-            block_out,
-            x,
-            edge,
-            before,
-            bias,
-            upstream,
-            windows,
-            taps,
-            turned,
-            later_edge,
-            total,
-        ),
-        {0: 0},
-    )
-    if arranged:
-        kept, sent = parts[0][0], parts[0][1]
-    else:
-        weight = parts[0].reshape(shards, share, channels)
-        line = jnp.broadcast_to(parts[1].astype(BF16)[None], (shards, 1, channels))
+        block_out, early_grads, grad_edge, weight, line = call(
+            whole_weights_kernel,
+            "first_frames_and_weights",
+            1.25,
+            firsts + arrays((27, channels, channels)) + arrays((1, channels), kind=F32),
+            [vmem(windows_shape(2), BF16)] + front_scratch,
+            (0, 3, 4),
+            (0,),
+            operands,
+            {0: 0},
+        )
+        weight = weight.reshape(shards, share, channels)
+        line = jnp.broadcast_to(line.astype(BF16)[None], (shards, 1, channels))
         pad = jnp.zeros((shards, 2 * half - share - 1, channels), BF16)
         whole = jnp.concatenate([weight, line, pad], axis=1)
         me = lax.axis_index("dp")
@@ -568,9 +665,8 @@
         "tm",
         -1,
     )
-    if shards == 4:
-        apart = {1: (2, 1), 2: (1, 2), 3: (3, 3)}
-        parts = [exchange(total[k], "dp", shards, apart[k]) for k in (3, 1, 2)]
+    if arranged:
+        parts = [exchange(total[k], "dp", shards, (k, k)) for k in (3, 1, 2)]
         total = total[0].astype(F32)
         for part in parts:
             total = total + part.astype(F32)
@@ -611,7 +707,7 @@
         clip_count * frames * height * breadth * shards * steps * lax.axis_size("tile")
     )
     weight, bias_grad = call(
-        functools.partial(closing_kernel, scale=1.0 / math.sqrt(positions)),
+        functools.partial(closing_kernel, scale=1.0 / math.sqrt(positions), arranged=arranged),
         "scaled_weights",
         0.01,
         arrays((share, channels), (1, channels // shards), kind=F32),

time: 44.3 us -> 43.3 us (0.977)
  waiting for transfers between devices: 10.4 us -> 9.03 us
    ppermute x4, waiting for transfers between devices: 3.52 us -> 2.22 us  [swapped(): return lax.ppermute(block, 'tile', [(0, 1), (1, 0)])]
    pallas_call x6 -> x7, Pallas kernels: 15.6 us -> 16 us  [call(): pl.pallas_call(kernel_body, out_shape=shapes, in_specs=[there if i in far...]
  transfers between devices with their start and end apart: 12 -> 12, of which waited for: 7 -> 5; matrix products, arithmetic and copies ran while one was open for 0% -> 0% of each run, Pallas kernels for 22% -> 26%
where the time goes in v5:
time: 43.3 us; the launch traced here: 43.1 us
  Pallas kernels  16 us (37%)
  starting transfers between devices  15.9 us (37%)
  waiting for transfers between devices  9.03 us (21%)
  local copies, waits for them, and re-layouts  1.08 us (2%)
  between operations  0.83 us (2%)
    pallas_call x7, Pallas kernels, call(): pl.pallas_call(kernel_body, out_shape=shapes, in_specs=[there if i in far...  16 us
    ppermute x6, starting transfers between devices, exchange(): return lax.ppermute(block, (axis, 'tile'), route)  8.71 us
    ppermute x6, waiting for transfers between devices, exchange(): return lax.ppermute(block, (axis, 'tile'), route)  6.8 us
    ppermute x2, starting transfers between devices, passed_along(): return lax.ppermute(block, axis, route)  6.04 us
    ppermute x4, waiting for transfers between devices, swapped(): return lax.ppermute(block, 'tile', [(0, 1), (1, 0)])  2.22 us
    ppermute x4, starting transfers between devices, swapped(): return lax.ppermute(block, 'tile', [(0, 1), (1, 0)])  1.16 us
    unnamed x8, local copies, waits for them, and re-layouts  1.05 us
  transfers between devices with their start and end apart: 12, of which 5 were waited for; matrix products, arithmetic and copies ran while one was open for 0% of the time, Pallas kernels for 26%

profile of v5, /device:TPU:0, one launch (start us, length us, event | category | flops | bytes accessed | tf_op | source)
XLA Modules:
  0.0 43.1 jit_solution(16542203747688536137)
XLA Ops:
  0.6 1.0 %copy-done.2 = bf16[1,8,8,32,128]{4,3,2,1,0:T(8,128)(2,1)S(1)} copy-done((bf16[1,8,8,32,128]{4,3,2,1,0:T(8,128)(2,1)S(1)}, bf16[1,8,8,32,128]{4,3,2,1,0:T(8,128)(2,1)}, u32[]{:S(2)}) %copy-start.2) | copy-done | bytes 524312
  1.7 0.2 border_rows.1
  1.9 0.5 %collective-permute-start = (bf16[8,32,128]{2,1,0:T(8,128)(2,1)S(1)}, bf16[8,32,128]{2,1,0:T(8,128)(2,1)S(1)}, u32[]{:S(2)}, u32[]{:S(2)}) collective-permute-start(bf16[8,32,128]{2,1,0:T(8,128)(2,1)S(1)} %get-tuple-element.34), channel_id=1, source_target_pairs={{0,1},{1,0},{2,3},{3,2},{4,5},{5,4},{6,7},{7,6},{8,9},{9,8},{10,11... | collective-permute-start | bytes 196616 | tf_op jit(solution)/shard_map/ppermute | solution.py:491
  2.4 0.9 %collective-permute-done.edge = bf16[8,32,128]{2,1,0:T(8,128)(2,1)S(1)} collective-permute-done((bf16[8,32,128]{2,1,0:T(8,128)(2,1)S(1)}, bf16[8,32,128]{2,1,0:T(8,128)(2,1)S(1)}, u32[]{:S(2)}, u32[]{:S(2)}) %collective-permute-start) | collective-permute-done | bytes 65568 | tf_op jit(solution)/shard_map/ppermute | solution.py:491
  3.3 4.8 %collective-permute-start.1 = (bf16[18,32,128]{2,1,0:T(8,128)(2,1)S(1)}, bf16[18,32,128]{2,1,0:T(8,128)(2,1)S(1)}, u32[]{:S(2)}, u32[]{:S(2)}) collective-permute-start(bf16[18,32,128]{2,1,0:T(8,128)(2,1)S(1)} %pad_maximum_fusion), channel_id=1, source_target_pairs={{0,2},{2,4},{4,6},{1,3},{3,5},{5,7},{8,10},{10,12},{12,14},{9,11},... | collective-permute-start | bytes 442376 | tf_op jit(solution)/shard_map/ppermute | solution.py:487
  8.1 4.0 %forward_interior.1 = (bf16[8,8,32,128]{3,2,1,0:T(8,128)(2,1)}, bf16[8,10,32,384]{3,2,1,0:T(8,128)(2,1)S(1)}, bf16[4608,256]{1,0:T(8,128)(2,1)S(1)}, bf16[3,256,...) custom-call(bf16[8,8,32,128]{3,2,1,0:T(8,128)(2,1)S(1)} %bitcast.24,, ...), custom_call_target="tpu_custom_call" | custom-call | flops 2717908992 | bytes 4194304 | tf_op jit(solution)/shard_map/forward_interior/pallas_call | solution.py:519
  12.1 0.0 collective-permute-done.1.before
  12.2 3.6 %first_frames_and_leaving_half.1 = (bf16[8,8,32,128]{3,2,1,0:T(8,128)(2,1)}, bf16[2,8,32,128]{3,2,1,0:T(8,128)(2,1)S(1)}, bf16[8,32,128]{2,1,0:T(8,128)(2,1)S(1)...) custom-call(bf16[8,8,32,128]{3,2,1,0:T(8,128)(2,1)} %get-tuple-eleme, ...), custom_call_target="tpu_custom_call", output_to_operand_aliasing={{0}: (0, {})} | custom-call | flops 2899102976 | bytes 4194304 | tf_op jit(solution)/shard_map/first_frames_and_leaving_half/pallas_call | solution.py:519
  15.7 0.1 collective-permute-start.3
  15.8 0.5 %collective-permute-start.2 = (bf16[8,32,128]{2,1,0:T(8,128)(2,1)S(1)}, bf16[8,32,128]{2,1,0:T(8,128)(2,1)S(1)}, u32[]{:S(2)}, u32[]{:S(2)}) collective-permute-start(bf16[8,32,128]{2,1,0:T(8,128)(2,1)S(1)} %get-tuple-element.43), channel_id=1, source_target_pairs={{0,1},{1,0},{2,3},{3,2},{4,5},{5,4},{6,7},{7,6},{8,9},{9,8},{10,11... | collective-permute-start | bytes 196616 | tf_op jit(solution)/shard_map/ppermute | solution.py:491
  16.3 1.4 %staying_half.1 = bf16[4,448,128]{2,1,0:T(8,128)(2,1)S(1)} custom-call(bf16[9,384,128]{2,1,0:T(8,128)(2,1)S(1)} %get-tuple-element.44.blocks_in, bf16[4,10,32,384]{3,2,1,0:T(8,128)(2,1)S(1)} %get-tuple-element.45.front, bf16[8,10,32,384]{3,2,1,0:T(8,128)(2,1)S(1)} %get-tuple-element.37.windows, bf16[128,2048]{1,0:T(8,128)(2,1)S(1)} %get-tuple-element.46.grads, ...), custom_call_target="tpu_custom_call" | custom-call | flops 1630745344 | bytes 4194304 | tf_op jit(solution)/shard_map/staying_half/pallas_call | solution.py:519
  17.7 0.1 add_convert_fusion
  17.9 0.0 collective-permute-done.2.edge
  17.9 3.7 %collective-permute-start.4 = (bf16[448,128]{1,0:T(8,128)(2,1)S(1)}, bf16[448,128]{1,0:T(8,128)(2,1)S(1)}, u32[]{:S(2)}, u32[]{:S(2)}) collective-permute-start(bf16[448,128]{1,0:T(8,128)(2,1)S(1)} %get-tuple-element.64), channel_id=1, source_target_pairs={{0,24},{1,25},{8,16},{9,17},{16,8},{17,9},{24,0},{25,1},{2,26},{3,... | collective-permute-start | bytes 344072 | tf_op jit(solution)/shard_map/ppermute | solution.py:477
  21.6 0.0 collective-permute-start.6
  21.6 0.8 %collective-permute-start.5 = (bf16[448,128]{1,0:T(8,128)(2,1)S(1)}, bf16[448,128]{1,0:T(8,128)(2,1)S(1)}, u32[]{:S(2)}, u32[]{:S(2)}) collective-permute-start(bf16[448,128]{1,0:T(8,128)(2,1)S(1)} %get-tuple-element.66), channel_id=1, source_target_pairs={{0,8},{1,9},{8,0},{9,1},{16,24},{17,25},{24,16},{25,17},{2,10},{3,... | collective-permute-start | bytes 344072 | tf_op jit(solution)/shard_map/ppermute | solution.py:477
  22.4 4.1 %input_gradient_interior.1 = (bf16[8,8,32,128]{3,2,1,0:T(8,128)(2,1)}, bf16[2,10,32,384]{3,2,1,0:T(8,128)(2,1)S(1)}, bf16[256,4608]{1,0:T(8,128)(2,1)S(1)}) custom-call(bf16[2,8,32,128]{3,2,1,0:T(8,128)(2,1)S(1)} %get-tuple-element.50.early, bf16[6,8,32,128]{3,2,1,0:T(8,128)(2,1)S(1)} %get-tuple-element.51.g, ...), custom_call_target="tpu_custom_call" | custom-call | flops 2717908992 | bytes 4194304 | tf_op jit(solution)/shard_map/input_gradient_interior/pallas_call | solution.py:519
  26.6 1.3 %collective-permute-start.10 = (bf16[18,32,128]{2,1,0:T(8,128)(2,1)S(1)}, bf16[18,32,128]{2,1,0:T(8,128)(2,1)S(1)}, u32[]{:S(2)}, u32[]{:S(2)}) collective-permute-start(bf16[18,32,128]{2,1,0:T(8,128)(2,1)S(1)} %pad_maximum_fusion.1), channel_id=1, source_target_pairs={{2,0},{4,2},{6,4},{3,1},{5,3},{7,5},{10,8},{12,10},{14,12},{11,9},... | collective-permute-start | bytes 442376 | tf_op jit(solution)/shard_map/ppermute | solution.py:487
  27.9 0.0 collective-permute-done.4
  27.9 3.6 %collective-permute-done.6 = bf16[448,128]{1,0:T(8,128)(2,1)S(1)} collective-permute-done((bf16[448,128]{1,0:T(8,128)(2,1)S(1)}, bf16[448,128]{1,0:T(8,128)(2,1)S(1)}, u32[]{:S(2)}, u32[]{:S(2)}) %collective-permute-start.6) | collective-permute-done | bytes 114720 | tf_op jit(solution)/shard_map/ppermute | solution.py:477
  31.5 0.1 fusion.2
  31.6 2.8 %collective-permute-start.9 = (bf16[448,128]{1,0:T(8,128)(2,1)S(1)}, bf16[448,128]{1,0:T(8,128)(2,1)S(1)}, u32[]{:S(2)}, u32[]{:S(2)}) collective-permute-start(bf16[448,128]{1,0:T(8,128)(2,1)S(1)} %fusion.2), channel_id=1, source_target_pairs={{0,6},{1,7},{2,4},{3,5},{4,2},{5,3},{6,0},{7,1},{8,14},{9,15},{10,... | collective-permute-start | bytes 344072 | tf_op jit(solution)/shard_map/ppermute | solution.py:477
  34.4 0.5 %collective-permute-start.8 = (bf16[448,128]{1,0:T(8,128)(2,1)S(1)}, bf16[448,128]{1,0:T(8,128)(2,1)S(1)}, u32[]{:S(2)}, u32[]{:S(2)}) collective-permute-start(bf16[448,128]{1,0:T(8,128)(2,1)S(1)} %fusion.2), channel_id=1, source_target_pairs={{0,4},{1,3},{2,6},{3,1},{4,0},{5,7},{6,2},{7,5},{8,12},{9,11},{10,... | collective-permute-start | bytes 344072 | tf_op jit(solution)/shard_map/ppermute | solution.py:477
  34.9 0.9 %collective-permute-start.7 = (bf16[448,128]{1,0:T(8,128)(2,1)S(1)}, bf16[448,128]{1,0:T(8,128)(2,1)S(1)}, u32[]{:S(2)}, u32[]{:S(2)}) collective-permute-start(bf16[448,128]{1,0:T(8,128)(2,1)S(1)} %fusion.2), channel_id=1, source_target_pairs={{0,2},{1,5},{2,0},{3,7},{4,6},{5,1},{6,4},{7,3},{8,10},{9,13},{10,... | collective-permute-start | bytes 344072 | tf_op jit(solution)/shard_map/ppermute | solution.py:477
  35.8 1.7 %input_gradient_last.1 = bf16[8,8,32,128]{3,2,1,0:T(8,128)(2,1)} custom-call(bf16[8,8,32,128]{3,2,1,0:T(8,128)(2,1)} %get-tuple-element.55.grad_in, bf16[2,10,32,384]{3,2,1,0:T(8,128)(2,1)S(1)} %get-tuple-element.57.last, bf16[18,32,128]{2,1,0:T(8,128)(2,1)S(1)} %collective-permute-done.10.after, ...), custom_call_target="tpu_custom_call", output_to_operand_aliasing={{}: (0, {})} | custom-call | flops 905969664 | bytes 4194304 | tf_op jit(solution)/shard_map/input_gradient_last/pallas_call | solution.py:519
  37.6 1.9 %collective-permute-done.9 = bf16[448,128]{1,0:T(8,128)(2,1)S(1)} collective-permute-done((bf16[448,128]{1,0:T(8,128)(2,1)S(1)}, bf16[448,128]{1,0:T(8,128)(2,1)S(1)}, u32[]{:S(2)}, u32[]{:S(2)}) %collective-permute-start.9) | collective-permute-done | bytes 114720 | tf_op jit(solution)/shard_map/ppermute | solution.py:477
  39.5 1.2 %collective-permute-done.8 = bf16[448,128]{1,0:T(8,128)(2,1)S(1)} collective-permute-done((bf16[448,128]{1,0:T(8,128)(2,1)S(1)}, bf16[448,128]{1,0:T(8,128)(2,1)S(1)}, u32[]{:S(2)}, u32[]{:S(2)}) %collective-permute-start.8) | collective-permute-done | bytes 114720 | tf_op jit(solution)/shard_map/ppermute | solution.py:477
  40.7 0.0 collective-permute-done.7
  40.8 0.1 add_convert_fusion.1.own
  40.8 0.1 collective-permute-start.11
  40.9 1.3 %collective-permute-done.11.other = bf16[448,128]{1,0:T(8,128)(2,1)S(1)} collective-permute-done((bf16[448,128]{1,0:T(8,128)(2,1)S(1)}, bf16[448,128]{1,0:T(8,128)(2,1)S(1)}, u32[]{:S(2)}, u32[]{:S(2)}) %collective-permute-start.11) | collective-permute-done | bytes 114720 | tf_op jit(solution)/shard_map/ppermute | solution.py:491
  42.2 0.9 %scaled_weights.1 = (f32[864,128]{1,0:T(8,128)}, f32[1,32]{1,0:T(1,128)}) custom-call(bf16[448,128]{1,0:T(8,128)(2,1)S(1)} %add_convert_fusion.1.own, bf16[448,128]{1,0:T(8,128)(2,1)S(1)} %collective-permute-done.11.other), custom_call_target="tpu_custom_call" | custom-call | flops 36238784 | bytes 4194304 | tf_op jit(solution)/shard_map/scaled_weights/pallas_call | solution.py:519
  (15 shorter events, 0.1 us)
Async XLA Ops:
  0.6 1.0 %copy-start.2 = (bf16[1,8,8,32,128]{4,3,2,1,0:T(8,128)(2,1)S(1)}, bf16[1,8,8,32,128]{4,3,2,1,0:T(8,128)(2,1)}, u32[]{:S(2)}) copy-start(bf16[1,8,8,32,128]{4,3,2,1,0:T(8,128)(2,1)} %param.4) | copy-start | bytes 1572868
  1.7 6.4 %copy-start = (bf16[1,8,8,32,128]{4,3,2,1,0:T(8,128)(2,1)S(1)}, bf16[1,8,8,32,128]{4,3,2,1,0:T(8,128)(2,1)}, u32[]{:S(2)}) copy-start(bf16[1,8,8,32,128]{4,3,2,1,0:T(8,128)(2,1)} %param.7) | copy-start | bytes 1572868
  1.7 6.4 %copy-start.1 = (bf16[3456,128]{1,0:T(8,128)(2,1)S(1)}, bf16[3456,128]{1,0:T(8,128)(2,1)}, u32[]{:S(2)}) copy-start(bf16[3456,128]{1,0:T(8,128)(2,1)} %kernel.3) | copy-start | bytes 2654212
  1.7 6.4 %copy-start.3 = (f32[128]{0:T(128)S(1)}, f32[128]{0:T(128)}, u32[]{:S(2)}) copy-start(f32[128]{0:T(128)} %param.6) | copy-start | bytes 1540
  1.9 1.4 %collective-permute-start = (bf16[8,32,128]{2,1,0:T(8,128)(2,1)S(1)}, bf16[8,32,128]{2,1,0:T(8,128)(2,1)S(1)}, u32[]{:S(2)}, u32[]{:S(2)}) collective-permute-start(bf16[8,32,128]{2,1,0:T(8,128)(2,1)S(1)} %get-tuple-element.34), channel_id=1, source_target_pairs={{0,1},{1,0},{2,3},{3,2},{4,5},{5,4},{6,7},{7,6},{8,9},{9,8},{10,11... | collective-permute-start | bytes 196616 | tf_op jit(solution)/shard_map/ppermute | solution.py:491
  3.3 8.8 %collective-permute-start.1 = (bf16[18,32,128]{2,1,0:T(8,128)(2,1)S(1)}, bf16[18,32,128]{2,1,0:T(8,128)(2,1)S(1)}, u32[]{:S(2)}, u32[]{:S(2)}) collective-permute-start(bf16[18,32,128]{2,1,0:T(8,128)(2,1)S(1)} %pad_maximum_fusion), channel_id=1, source_target_pairs={{0,2},{2,4},{4,6},{1,3},{3,5},{5,7},{8,10},{10,12},{12,14},{9,11},... | collective-permute-start | bytes 442376 | tf_op jit(solution)/shard_map/ppermute | solution.py:487
  15.7 2.0 %collective-permute-start.3 = (bf16[4,448,128]{2,1,0:T(8,128)(2,1)S(1)}, bf16[4,448,128]{2,1,0:T(8,128)(2,1)S(1)}, u32[]{:S(2)}, u32[]{:S(2)}) collective-permute-start(bf16[4,448,128]{2,1,0:T(8,128)(2,1)S(1)} %get-tuple-element.48), channel_id=1, source_target_pairs={{0,1},{1,0},{2,3},{3,2},{4,5},{5,4},{6,7},{7,6},{8,9},{9,8},{10,11... | collective-permute-start | bytes 1376264 | tf_op jit(solution)/shard_map/ppermute | solution.py:491
  15.8 2.1 %collective-permute-start.2 = (bf16[8,32,128]{2,1,0:T(8,128)(2,1)S(1)}, bf16[8,32,128]{2,1,0:T(8,128)(2,1)S(1)}, u32[]{:S(2)}, u32[]{:S(2)}) collective-permute-start(bf16[8,32,128]{2,1,0:T(8,128)(2,1)S(1)} %get-tuple-element.43), channel_id=1, source_target_pairs={{0,1},{1,0},{2,3},{3,2},{4,5},{5,4},{6,7},{7,6},{8,9},{9,8},{10,11... | collective-permute-start | bytes 196616 | tf_op jit(solution)/shard_map/ppermute | solution.py:491
  17.9 9.9 %collective-permute-start.4 = (bf16[448,128]{1,0:T(8,128)(2,1)S(1)}, bf16[448,128]{1,0:T(8,128)(2,1)S(1)}, u32[]{:S(2)}, u32[]{:S(2)}) collective-permute-start(bf16[448,128]{1,0:T(8,128)(2,1)S(1)} %get-tuple-element.64), channel_id=1, source_target_pairs={{0,24},{1,25},{8,16},{9,17},{16,8},{17,9},{24,0},{25,1},{2,26},{3,... | collective-permute-start | bytes 344072 | tf_op jit(solution)/shard_map/ppermute | solution.py:477
  21.6 9.9 %collective-permute-start.6 = (bf16[448,128]{1,0:T(8,128)(2,1)S(1)}, bf16[448,128]{1,0:T(8,128)(2,1)S(1)}, u32[]{:S(2)}, u32[]{:S(2)}) collective-permute-start(bf16[448,128]{1,0:T(8,128)(2,1)S(1)} %get-tuple-element.65), channel_id=1, source_target_pairs={{0,16},{1,17},{8,24},{9,25},{16,0},{17,1},{24,8},{25,9},{2,18},{3,... | collective-permute-start | bytes 344072 | tf_op jit(solution)/shard_map/ppermute | solution.py:477
  21.6 9.9 %collective-permute-start.5 = (bf16[448,128]{1,0:T(8,128)(2,1)S(1)}, bf16[448,128]{1,0:T(8,128)(2,1)S(1)}, u32[]{:S(2)}, u32[]{:S(2)}) collective-permute-start(bf16[448,128]{1,0:T(8,128)(2,1)S(1)} %get-tuple-element.66), channel_id=1, source_target_pairs={{0,8},{1,9},{8,0},{9,1},{16,24},{17,25},{24,16},{25,17},{2,10},{3,... | collective-permute-start | bytes 344072 | tf_op jit(solution)/shard_map/ppermute | solution.py:477
  26.6 9.3 %collective-permute-start.10 = (bf16[18,32,128]{2,1,0:T(8,128)(2,1)S(1)}, bf16[18,32,128]{2,1,0:T(8,128)(2,1)S(1)}, u32[]{:S(2)}, u32[]{:S(2)}) collective-permute-start(bf16[18,32,128]{2,1,0:T(8,128)(2,1)S(1)} %pad_maximum_fusion.1), channel_id=1, source_target_pairs={{2,0},{4,2},{6,4},{3,1},{5,3},{7,5},{10,8},{12,10},{14,12},{11,9},... | collective-permute-start | bytes 442376 | tf_op jit(solution)/shard_map/ppermute | solution.py:487
  31.6 8.0 %collective-permute-start.9 = (bf16[448,128]{1,0:T(8,128)(2,1)S(1)}, bf16[448,128]{1,0:T(8,128)(2,1)S(1)}, u32[]{:S(2)}, u32[]{:S(2)}) collective-permute-start(bf16[448,128]{1,0:T(8,128)(2,1)S(1)} %fusion.2), channel_id=1, source_target_pairs={{0,6},{1,7},{2,4},{3,5},{4,2},{5,3},{6,0},{7,1},{8,14},{9,15},{10,... | collective-permute-start | bytes 344072 | tf_op jit(solution)/shard_map/ppermute | solution.py:477
  34.4 6.3 %collective-permute-start.8 = (bf16[448,128]{1,0:T(8,128)(2,1)S(1)}, bf16[448,128]{1,0:T(8,128)(2,1)S(1)}, u32[]{:S(2)}, u32[]{:S(2)}) collective-permute-start(bf16[448,128]{1,0:T(8,128)(2,1)S(1)} %fusion.2), channel_id=1, source_target_pairs={{0,4},{1,3},{2,6},{3,1},{4,0},{5,7},{6,2},{7,5},{8,12},{9,11},{10,... | collective-permute-start | bytes 344072 | tf_op jit(solution)/shard_map/ppermute | solution.py:477
  34.9 5.8 %collective-permute-start.7 = (bf16[448,128]{1,0:T(8,128)(2,1)S(1)}, bf16[448,128]{1,0:T(8,128)(2,1)S(1)}, u32[]{:S(2)}, u32[]{:S(2)}) collective-permute-start(bf16[448,128]{1,0:T(8,128)(2,1)S(1)} %fusion.2), channel_id=1, source_target_pairs={{0,2},{1,5},{2,0},{3,7},{4,6},{5,1},{6,4},{7,3},{8,10},{9,13},{10,... | collective-permute-start | bytes 344072 | tf_op jit(solution)/shard_map/ppermute | solution.py:477
  40.8 1.4 %collective-permute-start.11 = (bf16[448,128]{1,0:T(8,128)(2,1)S(1)}, bf16[448,128]{1,0:T(8,128)(2,1)S(1)}, u32[]{:S(2)}, u32[]{:S(2)}) collective-permute-start(bf16[448,128]{1,0:T(8,128)(2,1)S(1)} %add_convert_fusion.1.own), channel_id=1, source_target_pairs={{0,1},{1,0},{2,3},{3,2},{4,5},{5,4},{6,7},{7,6},{8,9},{9,8},{10,11... | collective-permute-start | bytes 344072 | tf_op jit(solution)/shard_map/ppermute | solution.py:491

commit v6 on v5

--- a/solution.py
+++ b/solution.py
@@ -666,7 +666,7 @@
         -1,
     )
     if arranged:
-        parts = [exchange(total[k], "dp", shards, (k, k)) for k in (3, 1, 2)]
+        parts = [exchange(total[k], "dp", shards, (k, k)) for k in (2, 3, 1)]
         total = total[0].astype(F32)
         for part in parts:
             total = total + part.astype(F32)

time: 43.3 us -> 42.6 us (0.984)
  waiting for transfers between devices: 9.03 us -> 7.97 us
    ppermute x6, waiting for transfers between devices: 6.8 us -> 5.75 us  [exchange(): return lax.ppermute(block, (axis, 'tile'), route)]
  transfers between devices with their start and end apart: 12 -> 12, of which waited for: 5 -> 6; matrix products, arithmetic and copies ran while one was open for 0% -> 0% of each run, Pallas kernels for 26% -> 27%
where the time goes in v6:
time: 42.6 us; the launch traced here: 42 us
  Pallas kernels  16 us (38%)
  starting transfers between devices  15.9 us (37%)
  waiting for transfers between devices  7.97 us (19%)
  local copies, waits for them, and re-layouts  1.08 us (3%)
  between operations  0.82 us (2%)
    pallas_call x7, Pallas kernels, call(): pl.pallas_call(kernel_body, out_shape=shapes, in_specs=[there if i in far...  16 us
    ppermute x6, starting transfers between devices, exchange(): return lax.ppermute(block, (axis, 'tile'), route)  8.71 us
    ppermute x2, starting transfers between devices, passed_along(): return lax.ppermute(block, axis, route)  6.04 us
    ppermute x6, waiting for transfers between devices, exchange(): return lax.ppermute(block, (axis, 'tile'), route)  5.75 us
    ppermute x4, waiting for transfers between devices, swapped(): return lax.ppermute(block, 'tile', [(0, 1), (1, 0)])  2.22 us
    ppermute x4, starting transfers between devices, swapped(): return lax.ppermute(block, 'tile', [(0, 1), (1, 0)])  1.16 us
    unnamed x8, local copies, waits for them, and re-layouts  1.05 us
  transfers between devices with their start and end apart: 12, of which 6 were waited for; matrix products, arithmetic and copies ran while one was open for 0% of the time, Pallas kernels for 27%

profile of v6, /device:TPU:0, one launch (start us, length us, event | category | flops | bytes accessed | tf_op | source)
XLA Modules:
  0.0 42.0 jit_solution(6772379822737742067)
XLA Ops:
  0.6 1.0 %copy-done.2 = bf16[1,8,8,32,128]{4,3,2,1,0:T(8,128)(2,1)S(1)} copy-done((bf16[1,8,8,32,128]{4,3,2,1,0:T(8,128)(2,1)S(1)}, bf16[1,8,8,32,128]{4,3,2,1,0:T(8,128)(2,1)}, u32[]{:S(2)}) %copy-start.2) | copy-done | bytes 524312
  1.7 0.2 border_rows.1
  1.9 0.5 %collective-permute-start = (bf16[8,32,128]{2,1,0:T(8,128)(2,1)S(1)}, bf16[8,32,128]{2,1,0:T(8,128)(2,1)S(1)}, u32[]{:S(2)}, u32[]{:S(2)}) collective-permute-start(bf16[8,32,128]{2,1,0:T(8,128)(2,1)S(1)} %get-tuple-element.34), channel_id=1, source_target_pairs={{0,1},{1,0},{2,3},{3,2},{4,5},{5,4},{6,7},{7,6},{8,9},{9,8},{10,11... | collective-permute-start | bytes 196616 | tf_op jit(solution)/shard_map/ppermute | solution.py:491
  2.4 0.9 %collective-permute-done.edge = bf16[8,32,128]{2,1,0:T(8,128)(2,1)S(1)} collective-permute-done((bf16[8,32,128]{2,1,0:T(8,128)(2,1)S(1)}, bf16[8,32,128]{2,1,0:T(8,128)(2,1)S(1)}, u32[]{:S(2)}, u32[]{:S(2)}) %collective-permute-start) | collective-permute-done | bytes 65568 | tf_op jit(solution)/shard_map/ppermute | solution.py:491
  3.3 4.8 %collective-permute-start.1 = (bf16[18,32,128]{2,1,0:T(8,128)(2,1)S(1)}, bf16[18,32,128]{2,1,0:T(8,128)(2,1)S(1)}, u32[]{:S(2)}, u32[]{:S(2)}) collective-permute-start(bf16[18,32,128]{2,1,0:T(8,128)(2,1)S(1)} %pad_maximum_fusion), channel_id=1, source_target_pairs={{0,2},{2,4},{4,6},{1,3},{3,5},{5,7},{8,10},{10,12},{12,14},{9,11},... | collective-permute-start | bytes 442376 | tf_op jit(solution)/shard_map/ppermute | solution.py:487
  8.1 4.0 %forward_interior.1 = (bf16[8,8,32,128]{3,2,1,0:T(8,128)(2,1)}, bf16[8,10,32,384]{3,2,1,0:T(8,128)(2,1)S(1)}, bf16[4608,256]{1,0:T(8,128)(2,1)S(1)}, bf16[3,256,...) custom-call(bf16[8,8,32,128]{3,2,1,0:T(8,128)(2,1)S(1)} %bitcast.24,, ...), custom_call_target="tpu_custom_call" | custom-call | flops 2717908992 | bytes 4194304 | tf_op jit(solution)/shard_map/forward_interior/pallas_call | solution.py:519
  12.1 0.0 collective-permute-done.1.before
  12.2 3.6 %first_frames_and_leaving_half.1 = (bf16[8,8,32,128]{3,2,1,0:T(8,128)(2,1)}, bf16[2,8,32,128]{3,2,1,0:T(8,128)(2,1)S(1)}, bf16[8,32,128]{2,1,0:T(8,128)(2,1)S(1)...) custom-call(bf16[8,8,32,128]{3,2,1,0:T(8,128)(2,1)} %get-tuple-eleme, ...), custom_call_target="tpu_custom_call", output_to_operand_aliasing={{0}: (0, {})} | custom-call | flops 2899102976 | bytes 4194304 | tf_op jit(solution)/shard_map/first_frames_and_leaving_half/pallas_call | solution.py:519
  15.7 0.1 collective-permute-start.3
  15.8 0.5 %collective-permute-start.2 = (bf16[8,32,128]{2,1,0:T(8,128)(2,1)S(1)}, bf16[8,32,128]{2,1,0:T(8,128)(2,1)S(1)}, u32[]{:S(2)}, u32[]{:S(2)}) collective-permute-start(bf16[8,32,128]{2,1,0:T(8,128)(2,1)S(1)} %get-tuple-element.43), channel_id=1, source_target_pairs={{0,1},{1,0},{2,3},{3,2},{4,5},{5,4},{6,7},{7,6},{8,9},{9,8},{10,11... | collective-permute-start | bytes 196616 | tf_op jit(solution)/shard_map/ppermute | solution.py:491
  16.3 1.4 %staying_half.1 = bf16[4,448,128]{2,1,0:T(8,128)(2,1)S(1)} custom-call(bf16[9,384,128]{2,1,0:T(8,128)(2,1)S(1)} %get-tuple-element.44.blocks_in, bf16[4,10,32,384]{3,2,1,0:T(8,128)(2,1)S(1)} %get-tuple-element.45.front, bf16[8,10,32,384]{3,2,1,0:T(8,128)(2,1)S(1)} %get-tuple-element.37.windows, bf16[128,2048]{1,0:T(8,128)(2,1)S(1)} %get-tuple-element.46.grads, ...), custom_call_target="tpu_custom_call" | custom-call | flops 1630745344 | bytes 4194304 | tf_op jit(solution)/shard_map/staying_half/pallas_call | solution.py:519
  17.7 0.0 collective-permute-done.3
  17.7 0.1 add_convert_fusion
  17.9 2.6 %collective-permute-start.4 = (bf16[448,128]{1,0:T(8,128)(2,1)S(1)}, bf16[448,128]{1,0:T(8,128)(2,1)S(1)}, u32[]{:S(2)}, u32[]{:S(2)}) collective-permute-start(bf16[448,128]{1,0:T(8,128)(2,1)S(1)} %get-tuple-element.64), channel_id=1, source_target_pairs={{0,16},{1,17},{8,24},{9,25},{16,0},{17,1},{24,8},{25,9},{2,18},{3,... | collective-permute-start | bytes 344072 | tf_op jit(solution)/shard_map/ppermute | solution.py:477
  20.6 1.6 %collective-permute-start.6 = (bf16[448,128]{1,0:T(8,128)(2,1)S(1)}, bf16[448,128]{1,0:T(8,128)(2,1)S(1)}, u32[]{:S(2)}, u32[]{:S(2)}) collective-permute-start(bf16[448,128]{1,0:T(8,128)(2,1)S(1)} %get-tuple-element.65), channel_id=1, source_target_pairs={{0,8},{1,9},{8,0},{9,1},{16,24},{17,25},{24,16},{25,17},{2,10},{3,... | collective-permute-start | bytes 344072 | tf_op jit(solution)/shard_map/ppermute | solution.py:477
  22.1 0.2 collective-permute-start.5
  22.4 4.1 %input_gradient_interior.1 = (bf16[8,8,32,128]{3,2,1,0:T(8,128)(2,1)}, bf16[2,10,32,384]{3,2,1,0:T(8,128)(2,1)S(1)}, bf16[256,4608]{1,0:T(8,128)(2,1)S(1)}) custom-call(bf16[2,8,32,128]{3,2,1,0:T(8,128)(2,1)S(1)} %get-tuple-element.50.early, bf16[6,8,32,128]{3,2,1,0:T(8,128)(2,1)S(1)} %get-tuple-element.51.g, ...), custom_call_target="tpu_custom_call" | custom-call | flops 2717908992 | bytes 4194304 | tf_op jit(solution)/shard_map/input_gradient_interior/pallas_call | solution.py:519
  26.6 1.3 %collective-permute-start.10 = (bf16[18,32,128]{2,1,0:T(8,128)(2,1)S(1)}, bf16[18,32,128]{2,1,0:T(8,128)(2,1)S(1)}, u32[]{:S(2)}, u32[]{:S(2)}) collective-permute-start(bf16[18,32,128]{2,1,0:T(8,128)(2,1)S(1)} %pad_maximum_fusion.1), channel_id=1, source_target_pairs={{2,0},{4,2},{6,4},{3,1},{5,3},{7,5},{10,8},{12,10},{14,12},{11,9},... | collective-permute-start | bytes 442376 | tf_op jit(solution)/shard_map/ppermute | solution.py:487
  27.9 0.2 collective-permute-done.4
  28.0 0.0 collective-permute-done.6
  28.0 2.1 %collective-permute-done.5 = bf16[448,128]{1,0:T(8,128)(2,1)S(1)} collective-permute-done((bf16[448,128]{1,0:T(8,128)(2,1)S(1)}, bf16[448,128]{1,0:T(8,128)(2,1)S(1)}, u32[]{:S(2)}, u32[]{:S(2)}) %collective-permute-start.5) | collective-permute-done | bytes 114720 | tf_op jit(solution)/shard_map/ppermute | solution.py:477
  30.1 0.1 fusion.2
  30.2 2.8 %collective-permute-start.9 = (bf16[448,128]{1,0:T(8,128)(2,1)S(1)}, bf16[448,128]{1,0:T(8,128)(2,1)S(1)}, u32[]{:S(2)}, u32[]{:S(2)}) collective-permute-start(bf16[448,128]{1,0:T(8,128)(2,1)S(1)} %fusion.2), channel_id=1, source_target_pairs={{0,6},{1,7},{2,4},{3,5},{4,2},{5,3},{6,0},{7,1},{8,14},{9,15},{10,... | collective-permute-start | bytes 344072 | tf_op jit(solution)/shard_map/ppermute | solution.py:477
  33.0 0.5 %collective-permute-start.8 = (bf16[448,128]{1,0:T(8,128)(2,1)S(1)}, bf16[448,128]{1,0:T(8,128)(2,1)S(1)}, u32[]{:S(2)}, u32[]{:S(2)}) collective-permute-start(bf16[448,128]{1,0:T(8,128)(2,1)S(1)} %fusion.2), channel_id=1, source_target_pairs={{0,4},{1,3},{2,6},{3,1},{4,0},{5,7},{6,2},{7,5},{8,12},{9,11},{10,... | collective-permute-start | bytes 344072 | tf_op jit(solution)/shard_map/ppermute | solution.py:477
  33.5 0.9 %collective-permute-start.7 = (bf16[448,128]{1,0:T(8,128)(2,1)S(1)}, bf16[448,128]{1,0:T(8,128)(2,1)S(1)}, u32[]{:S(2)}, u32[]{:S(2)}) collective-permute-start(bf16[448,128]{1,0:T(8,128)(2,1)S(1)} %fusion.2), channel_id=1, source_target_pairs={{0,2},{1,5},{2,0},{3,7},{4,6},{5,1},{6,4},{7,3},{8,10},{9,13},{10,... | collective-permute-start | bytes 344072 | tf_op jit(solution)/shard_map/ppermute | solution.py:477
  34.4 1.7 %input_gradient_last.1 = bf16[8,8,32,128]{3,2,1,0:T(8,128)(2,1)} custom-call(bf16[8,8,32,128]{3,2,1,0:T(8,128)(2,1)} %get-tuple-element.55.grad_in, bf16[2,10,32,384]{3,2,1,0:T(8,128)(2,1)S(1)} %get-tuple-element.57.last, bf16[18,32,128]{2,1,0:T(8,128)(2,1)S(1)} %collective-permute-done.10.after, ...), custom_call_target="tpu_custom_call", output_to_operand_aliasing={{}: (0, {})} | custom-call | flops 905969664 | bytes 4194304 | tf_op jit(solution)/shard_map/input_gradient_last/pallas_call | solution.py:519
  36.2 3.3 %collective-permute-done.9 = bf16[448,128]{1,0:T(8,128)(2,1)S(1)} collective-permute-done((bf16[448,128]{1,0:T(8,128)(2,1)S(1)}, bf16[448,128]{1,0:T(8,128)(2,1)S(1)}, u32[]{:S(2)}, u32[]{:S(2)}) %collective-permute-start.9) | collective-permute-done | bytes 114720 | tf_op jit(solution)/shard_map/ppermute | solution.py:477
  39.5 0.2 collective-permute-done.8
  39.7 0.1 add_convert_fusion.1.own
  39.8 0.1 collective-permute-start.11
  39.8 1.3 %collective-permute-done.11.other = bf16[448,128]{1,0:T(8,128)(2,1)S(1)} collective-permute-done((bf16[448,128]{1,0:T(8,128)(2,1)S(1)}, bf16[448,128]{1,0:T(8,128)(2,1)S(1)}, u32[]{:S(2)}, u32[]{:S(2)}) %collective-permute-start.11) | collective-permute-done | bytes 114720 | tf_op jit(solution)/shard_map/ppermute | solution.py:491
  41.1 0.9 %scaled_weights.1 = (f32[864,128]{1,0:T(8,128)}, f32[1,32]{1,0:T(1,128)}) custom-call(bf16[448,128]{1,0:T(8,128)(2,1)S(1)} %add_convert_fusion.1.own, bf16[448,128]{1,0:T(8,128)(2,1)S(1)} %collective-permute-done.11.other), custom_call_target="tpu_custom_call" | custom-call | flops 36238784 | bytes 4194304 | tf_op jit(solution)/shard_map/scaled_weights/pallas_call | solution.py:519
  (15 shorter events, 0.1 us)
Async XLA Ops:
  0.6 1.0 %copy-start.2 = (bf16[1,8,8,32,128]{4,3,2,1,0:T(8,128)(2,1)S(1)}, bf16[1,8,8,32,128]{4,3,2,1,0:T(8,128)(2,1)}, u32[]{:S(2)}) copy-start(bf16[1,8,8,32,128]{4,3,2,1,0:T(8,128)(2,1)} %param.4) | copy-start | bytes 1572868
  1.7 6.4 %copy-start = (bf16[1,8,8,32,128]{4,3,2,1,0:T(8,128)(2,1)S(1)}, bf16[1,8,8,32,128]{4,3,2,1,0:T(8,128)(2,1)}, u32[]{:S(2)}) copy-start(bf16[1,8,8,32,128]{4,3,2,1,0:T(8,128)(2,1)} %param.7) | copy-start | bytes 1572868
  1.7 6.4 %copy-start.1 = (bf16[3456,128]{1,0:T(8,128)(2,1)S(1)}, bf16[3456,128]{1,0:T(8,128)(2,1)}, u32[]{:S(2)}) copy-start(bf16[3456,128]{1,0:T(8,128)(2,1)} %kernel.3) | copy-start | bytes 2654212
  1.7 6.4 %copy-start.3 = (f32[128]{0:T(128)S(1)}, f32[128]{0:T(128)}, u32[]{:S(2)}) copy-start(f32[128]{0:T(128)} %param.6) | copy-start | bytes 1540
  1.9 1.4 %collective-permute-start = (bf16[8,32,128]{2,1,0:T(8,128)(2,1)S(1)}, bf16[8,32,128]{2,1,0:T(8,128)(2,1)S(1)}, u32[]{:S(2)}, u32[]{:S(2)}) collective-permute-start(bf16[8,32,128]{2,1,0:T(8,128)(2,1)S(1)} %get-tuple-element.34), channel_id=1, source_target_pairs={{0,1},{1,0},{2,3},{3,2},{4,5},{5,4},{6,7},{7,6},{8,9},{9,8},{10,11... | collective-permute-start | bytes 196616 | tf_op jit(solution)/shard_map/ppermute | solution.py:491
  3.3 8.8 %collective-permute-start.1 = (bf16[18,32,128]{2,1,0:T(8,128)(2,1)S(1)}, bf16[18,32,128]{2,1,0:T(8,128)(2,1)S(1)}, u32[]{:S(2)}, u32[]{:S(2)}) collective-permute-start(bf16[18,32,128]{2,1,0:T(8,128)(2,1)S(1)} %pad_maximum_fusion), channel_id=1, source_target_pairs={{0,2},{2,4},{4,6},{1,3},{3,5},{5,7},{8,10},{10,12},{12,14},{9,11},... | collective-permute-start | bytes 442376 | tf_op jit(solution)/shard_map/ppermute | solution.py:487
  15.7 2.0 %collective-permute-start.3 = (bf16[4,448,128]{2,1,0:T(8,128)(2,1)S(1)}, bf16[4,448,128]{2,1,0:T(8,128)(2,1)S(1)}, u32[]{:S(2)}, u32[]{:S(2)}) collective-permute-start(bf16[4,448,128]{2,1,0:T(8,128)(2,1)S(1)} %get-tuple-element.48), channel_id=1, source_target_pairs={{0,1},{1,0},{2,3},{3,2},{4,5},{5,4},{6,7},{7,6},{8,9},{9,8},{10,11... | collective-permute-start | bytes 1376264 | tf_op jit(solution)/shard_map/ppermute | solution.py:491
  15.8 2.1 %collective-permute-start.2 = (bf16[8,32,128]{2,1,0:T(8,128)(2,1)S(1)}, bf16[8,32,128]{2,1,0:T(8,128)(2,1)S(1)}, u32[]{:S(2)}, u32[]{:S(2)}) collective-permute-start(bf16[8,32,128]{2,1,0:T(8,128)(2,1)S(1)} %get-tuple-element.43), channel_id=1, source_target_pairs={{0,1},{1,0},{2,3},{3,2},{4,5},{5,4},{6,7},{7,6},{8,9},{9,8},{10,11... | collective-permute-start | bytes 196616 | tf_op jit(solution)/shard_map/ppermute | solution.py:491
  17.9 10.1 %collective-permute-start.4 = (bf16[448,128]{1,0:T(8,128)(2,1)S(1)}, bf16[448,128]{1,0:T(8,128)(2,1)S(1)}, u32[]{:S(2)}, u32[]{:S(2)}) collective-permute-start(bf16[448,128]{1,0:T(8,128)(2,1)S(1)} %get-tuple-element.64), channel_id=1, source_target_pairs={{0,16},{1,17},{8,24},{9,25},{16,0},{17,1},{24,8},{25,9},{2,18},{3,... | collective-permute-start | bytes 344072 | tf_op jit(solution)/shard_map/ppermute | solution.py:477
  20.6 7.5 %collective-permute-start.6 = (bf16[448,128]{1,0:T(8,128)(2,1)S(1)}, bf16[448,128]{1,0:T(8,128)(2,1)S(1)}, u32[]{:S(2)}, u32[]{:S(2)}) collective-permute-start(bf16[448,128]{1,0:T(8,128)(2,1)S(1)} %get-tuple-element.65), channel_id=1, source_target_pairs={{0,8},{1,9},{8,0},{9,1},{16,24},{17,25},{24,16},{25,17},{2,10},{3,... | collective-permute-start | bytes 344072 | tf_op jit(solution)/shard_map/ppermute | solution.py:477
  22.1 8.0 %collective-permute-start.5 = (bf16[448,128]{1,0:T(8,128)(2,1)S(1)}, bf16[448,128]{1,0:T(8,128)(2,1)S(1)}, u32[]{:S(2)}, u32[]{:S(2)}) collective-permute-start(bf16[448,128]{1,0:T(8,128)(2,1)S(1)} %get-tuple-element.66), channel_id=1, source_target_pairs={{0,24},{1,25},{8,16},{9,17},{16,8},{17,9},{24,0},{25,1},{2,26},{3,... | collective-permute-start | bytes 344072 | tf_op jit(solution)/shard_map/ppermute | solution.py:477
  26.6 7.9 %collective-permute-start.10 = (bf16[18,32,128]{2,1,0:T(8,128)(2,1)S(1)}, bf16[18,32,128]{2,1,0:T(8,128)(2,1)S(1)}, u32[]{:S(2)}, u32[]{:S(2)}) collective-permute-start(bf16[18,32,128]{2,1,0:T(8,128)(2,1)S(1)} %pad_maximum_fusion.1), channel_id=1, source_target_pairs={{2,0},{4,2},{6,4},{3,1},{5,3},{7,5},{10,8},{12,10},{14,12},{11,9},... | collective-permute-start | bytes 442376 | tf_op jit(solution)/shard_map/ppermute | solution.py:487
  30.2 9.3 %collective-permute-start.9 = (bf16[448,128]{1,0:T(8,128)(2,1)S(1)}, bf16[448,128]{1,0:T(8,128)(2,1)S(1)}, u32[]{:S(2)}, u32[]{:S(2)}) collective-permute-start(bf16[448,128]{1,0:T(8,128)(2,1)S(1)} %fusion.2), channel_id=1, source_target_pairs={{0,6},{1,7},{2,4},{3,5},{4,2},{5,3},{6,0},{7,1},{8,14},{9,15},{10,... | collective-permute-start | bytes 344072 | tf_op jit(solution)/shard_map/ppermute | solution.py:477
  33.0 6.7 %collective-permute-start.8 = (bf16[448,128]{1,0:T(8,128)(2,1)S(1)}, bf16[448,128]{1,0:T(8,128)(2,1)S(1)}, u32[]{:S(2)}, u32[]{:S(2)}) collective-permute-start(bf16[448,128]{1,0:T(8,128)(2,1)S(1)} %fusion.2), channel_id=1, source_target_pairs={{0,4},{1,3},{2,6},{3,1},{4,0},{5,7},{6,2},{7,5},{8,12},{9,11},{10,... | collective-permute-start | bytes 344072 | tf_op jit(solution)/shard_map/ppermute | solution.py:477
  33.5 6.2 %collective-permute-start.7 = (bf16[448,128]{1,0:T(8,128)(2,1)S(1)}, bf16[448,128]{1,0:T(8,128)(2,1)S(1)}, u32[]{:S(2)}, u32[]{:S(2)}) collective-permute-start(bf16[448,128]{1,0:T(8,128)(2,1)S(1)} %fusion.2), channel_id=1, source_target_pairs={{0,2},{1,5},{2,0},{3,7},{4,6},{5,1},{6,4},{7,3},{8,10},{9,13},{10,... | collective-permute-start | bytes 344072 | tf_op jit(solution)/shard_map/ppermute | solution.py:477
  39.8 1.4 %collective-permute-start.11 = (bf16[448,128]{1,0:T(8,128)(2,1)S(1)}, bf16[448,128]{1,0:T(8,128)(2,1)S(1)}, u32[]{:S(2)}, u32[]{:S(2)}) collective-permute-start(bf16[448,128]{1,0:T(8,128)(2,1)S(1)} %add_convert_fusion.1.own), channel_id=1, source_target_pairs={{0,1},{1,0},{2,3},{3,2},{4,5},{5,4},{6,7},{7,6},{8,9},{9,8},{10,11... | collective-permute-start | bytes 344072 | tf_op jit(solution)/shard_map/ppermute | solution.py:491

commit v7 on v6

--- a/solution.py
+++ b/solution.py
@@ -50,10 +50,11 @@
     return result, grad
 
 
-def forward_pair(frames, taps, bias, x_pair, upstream):
+def forward_pair(frames, taps, bias, x_pair, upstream, begun=0.0):
     channels = bias.shape[1]
     both = jnp.concatenate([bias[...], bias[...]], axis=1)
-    pre = both + jnp.dot(window_block(frames), taps[...], preferred_element_type=F32)
+    count = 9 * channels * len(frames)
+    pre = both + begun + jnp.dot(window_block(frames), taps[0:count], preferred_element_type=F32)
     return [
         activate(
             pre[:, s * channels : (s + 1) * channels],
@@ -77,6 +78,7 @@
     grad_pre,
     edge_out,
     total,
+    begun,
     bias_here,
     upstream,
     result,
@@ -130,6 +132,10 @@
         total[...] += summed
         leave(p).start()
 
+    begun[...] = jnp.dot(
+        window_block([windows[0], windows[1]]), taps[2 * rows :], preferred_element_type=F32
+    )
+
     @pl.loop(0, frames // 2 - 1)
     def _(p):
         leave(p).wait()
@@ -151,9 +157,9 @@
         (*range(96, 108), 83),
     ),
 )
-LEAVING = (0x866421, 0x765320)
-STAYING = (0x7530, 0x8841)
-COUNTS = {LEAVING: (6, 3), STAYING: (4, 4)}
+LEAVING = (0x864210, 0x765320)
+STAYING = (0x753, 0x841)
+COUNTS = {LEAVING: (6, 3), STAYING: (3, 3)}
 
 
 def runs_of(steps):
@@ -212,7 +218,7 @@
 
 
 def first_frames(
-    x, before, bias, cotangent, windows, taps, turned, edge_in, total, block_out, grad_pre, edge_out,
+    x, before, bias, cotangent, windows, taps, turned, edge_in, total, begun, block_out, grad_pre, edge_out,
     early, bias_here, upstream, result, arriving, leaving,
 ):
     frames, height, breadth, channels = x.shape
@@ -227,11 +233,12 @@
     up_copy.wait()
     summed = total[...]
     firsts = forward_pair(
-        [early[0], early[1], windows[0], windows[1]],
+        [early[0], early[1]],
         taps,
         bias_here,
         [x[0], x[1]],
         [upstream[0], upstream[1]],
+        begun[...],
     )
     for s in range(2):
         result[s] = firsts[s][0].reshape(height, breadth, channels)
@@ -255,7 +262,7 @@
 
 
 def leaving_half_kernel(
-    block_in, x, before, bias, cotangent, windows, taps, turned, edge_in, total,
+    block_in, x, before, bias, cotangent, windows, taps, turned, edge_in, total, begun,
     block_out, grad_pre, edge_out, sent, blocks, front, grads, total_out,
     bias_here, upstream, result, arriving, leaving,
 ):
@@ -263,7 +270,7 @@
     me = lax.axis_index("dp")
     front[2:4] = windows[0:2]
     values, summed, copy = first_frames(
-        x, before, bias, cotangent, windows, taps, turned, edge_in, total, block_out, grad_pre, edge_out,
+        x, before, bias, cotangent, windows, taps, turned, edge_in, total, begun, block_out, grad_pre, edge_out,
         front, bias_here, upstream, result, arriving, leaving,
     )
     grads[...] = values
@@ -297,13 +304,13 @@
 
 
 def whole_weights_kernel(
-    block_in, x, before, bias, cotangent, windows, taps, turned, edge_in, total,
+    block_in, x, before, bias, cotangent, windows, taps, turned, edge_in, total, begun,
     block_out, grad_pre, edge_out, weights, bias_sum,
     early, bias_here, upstream, result, arriving, leaving,
 ):
     frames, height, breadth, channels = x.shape
     grads, summed, copy = first_frames(
-        x, before, bias, cotangent, windows, taps, turned, edge_in, total, block_out, grad_pre, edge_out,
+        x, before, bias, cotangent, windows, taps, turned, edge_in, total, begun, block_out, grad_pre, edge_out,
         early, bias_here, upstream, result, arriving, leaving,
     )
     for b in range(3):
@@ -551,7 +558,7 @@
         "tm",
         1,
     )
-    block_out, windows, taps, turned, later_grads, later_edge, total = call(
+    block_out, windows, taps, turned, later_grads, later_edge, total, begun = call(
         interior_kernel,
         "forward_interior",
         0.75,
@@ -563,7 +570,7 @@
             frames_shape(frames - 2),
             (frames - 2, breadth, channels),
         )
-        + arrays((1, channels), kind=F32),
+        + arrays((1, channels), (area, 2 * channels), kind=F32),
         [
             vmem((1, channels), F32),
             vmem(frames_shape(frames - 2), BF16),
@@ -584,7 +591,7 @@
     ]
     firsts = [cells] + arrays(frames_shape(2), (frames, breadth, channels))
     operands = (
-        block_out, x, before, bias, upstream, windows, taps, turned, later_edge, total,
+        block_out, x, before, bias, upstream, windows, taps, turned, later_edge, total, begun,
     )
     if arranged:
         groups = arrays((9, 3 * channels, channels))

time: 42.6 us -> 42.3 us (level)
  Pallas kernels: 16 us -> 15.5 us
    pallas_call x7, Pallas kernels: 16 us -> 15.5 us  [call(): pl.pallas_call(kernel_body, out_shape=shapes, in_specs=[there if i in far...]
where the time goes in v7:
time: 42.3 us; the launch traced here: 41.7 us
  starting transfers between devices  15.7 us (37%)
  Pallas kernels  15.5 us (37%)
  waiting for transfers between devices  8.28 us (20%)
  local copies, waits for them, and re-layouts  1.08 us (3%)
  between operations  0.81 us (2%)
    pallas_call x7, Pallas kernels, call(): pl.pallas_call(kernel_body, out_shape=shapes, in_specs=[there if i in far...  15.5 us
    ppermute x6, starting transfers between devices, exchange(): return lax.ppermute(block, (axis, 'tile'), route)  8.55 us
    ppermute x2, starting transfers between devices, passed_along(): return lax.ppermute(block, axis, route)  6.04 us
    ppermute x6, waiting for transfers between devices, exchange(): return lax.ppermute(block, (axis, 'tile'), route)  5.87 us
    ppermute x4, waiting for transfers between devices, swapped(): return lax.ppermute(block, 'tile', [(0, 1), (1, 0)])  2.41 us
    ppermute x4, starting transfers between devices, swapped(): return lax.ppermute(block, 'tile', [(0, 1), (1, 0)])  1.16 us
    unnamed x8, local copies, waits for them, and re-layouts  1.05 us
  transfers between devices with their start and end apart: 12, of which 6 were waited for; matrix products, arithmetic and copies ran while one was open for 0% of the time, Pallas kernels for 27%

profile of v7, /device:TPU:0, one launch (start us, length us, event | category | flops | bytes accessed | tf_op | source)
XLA Modules:
  0.0 41.7 jit_solution(11750050517366800054)
XLA Ops:
  0.6 1.0 %copy-done.2 = bf16[1,8,8,32,128]{4,3,2,1,0:T(8,128)(2,1)S(1)} copy-done((bf16[1,8,8,32,128]{4,3,2,1,0:T(8,128)(2,1)S(1)}, bf16[1,8,8,32,128]{4,3,2,1,0:T(8,128)(2,1)}, u32[]{:S(2)}) %copy-start.2) | copy-done | bytes 524312
  1.7 0.2 border_rows.1
  1.9 0.5 %collective-permute-start = (bf16[8,32,128]{2,1,0:T(8,128)(2,1)S(1)}, bf16[8,32,128]{2,1,0:T(8,128)(2,1)S(1)}, u32[]{:S(2)}, u32[]{:S(2)}) collective-permute-start(bf16[8,32,128]{2,1,0:T(8,128)(2,1)S(1)} %get-tuple-element.35), channel_id=1, source_target_pairs={{0,1},{1,0},{2,3},{3,2},{4,5},{5,4},{6,7},{7,6},{8,9},{9,8},{10,11... | collective-permute-start | bytes 196616 | tf_op jit(solution)/shard_map/ppermute | solution.py:498
  2.4 0.9 %collective-permute-done.edge = bf16[8,32,128]{2,1,0:T(8,128)(2,1)S(1)} collective-permute-done((bf16[8,32,128]{2,1,0:T(8,128)(2,1)S(1)}, bf16[8,32,128]{2,1,0:T(8,128)(2,1)S(1)}, u32[]{:S(2)}, u32[]{:S(2)}) %collective-permute-start) | collective-permute-done | bytes 65568 | tf_op jit(solution)/shard_map/ppermute | solution.py:498
  3.3 4.8 %collective-permute-start.1 = (bf16[18,32,128]{2,1,0:T(8,128)(2,1)S(1)}, bf16[18,32,128]{2,1,0:T(8,128)(2,1)S(1)}, u32[]{:S(2)}, u32[]{:S(2)}) collective-permute-start(bf16[18,32,128]{2,1,0:T(8,128)(2,1)S(1)} %pad_maximum_fusion), channel_id=1, source_target_pairs={{0,2},{2,4},{4,6},{1,3},{3,5},{5,7},{8,10},{10,12},{12,14},{9,11},... | collective-permute-start | bytes 442376 | tf_op jit(solution)/shard_map/ppermute | solution.py:494
  8.1 4.2 %forward_interior.1 = (bf16[8,8,32,128]{3,2,1,0:T(8,128)(2,1)}, bf16[8,10,32,384]{3,2,1,0:T(8,128)(2,1)S(1)}, bf16[4608,256]{1,0:T(8,128)(2,1)S(1)}, bf16[3,256,...) custom-call(bf16[8,8,32,128]{3,2,1,0:T(8,128)(2,1)S(1)} %bitcast.24,, ...), custom_call_target="tpu_custom_call" | custom-call | flops 2717908992 | bytes 4194304 | tf_op jit(solution)/shard_map/forward_interior/pallas_call | solution.py:526
  12.3 0.0 collective-permute-done.1.before
  12.3 3.3 %first_frames_and_leaving_half.1 = (bf16[8,8,32,128]{3,2,1,0:T(8,128)(2,1)}, bf16[2,8,32,128]{3,2,1,0:T(8,128)(2,1)S(1)}, bf16[8,32,128]{2,1,0:T(8,128)(2,1)S(1)...) custom-call(bf16[8,8,32,128]{3,2,1,0:T(8,128)(2,1)} %get-tuple-eleme, ...), custom_call_target="tpu_custom_call", output_to_operand_aliasing={{0}: (0, {})} | custom-call | flops 2899102976 | bytes 4194304 | tf_op jit(solution)/shard_map/first_frames_and_leaving_half/pallas_call | solution.py:526
  15.6 0.1 collective-permute-start.3
  15.7 0.5 %collective-permute-start.2 = (bf16[8,32,128]{2,1,0:T(8,128)(2,1)S(1)}, bf16[8,32,128]{2,1,0:T(8,128)(2,1)S(1)}, u32[]{:S(2)}, u32[]{:S(2)}) collective-permute-start(bf16[8,32,128]{2,1,0:T(8,128)(2,1)S(1)} %get-tuple-element.45), channel_id=1, source_target_pairs={{0,1},{1,0},{2,3},{3,2},{4,5},{5,4},{6,7},{7,6},{8,9},{9,8},{10,11... | collective-permute-start | bytes 196616 | tf_op jit(solution)/shard_map/ppermute | solution.py:498
  16.2 1.1 %staying_half.1 = bf16[4,448,128]{2,1,0:T(8,128)(2,1)S(1)} custom-call(bf16[9,384,128]{2,1,0:T(8,128)(2,1)S(1)} %get-tuple-element.46.blocks_in, bf16[4,10,32,384]{3,2,1,0:T(8,128)(2,1)S(1)} %get-tuple-element.47.front, bf16[8,10,32,384]{3,2,1,0:T(8,128)(2,1)S(1)} %get-tuple-element.38.windows, bf16[128,2048]{1,0:T(8,128)(2,1)S(1)} %get-tuple-element.48.grads, ...), custom_call_target="tpu_custom_call" | custom-call | flops 1630745344 | bytes 4194304 | tf_op jit(solution)/shard_map/staying_half/pallas_call | solution.py:526
  17.3 0.2 collective-permute-done.3
  17.5 0.1 add_convert_fusion
  17.6 0.0 collective-permute-done.2.edge
  17.7 2.6 %collective-permute-start.4 = (bf16[448,128]{1,0:T(8,128)(2,1)S(1)}, bf16[448,128]{1,0:T(8,128)(2,1)S(1)}, u32[]{:S(2)}, u32[]{:S(2)}) collective-permute-start(bf16[448,128]{1,0:T(8,128)(2,1)S(1)} %get-tuple-element.66), channel_id=1, source_target_pairs={{0,16},{1,17},{8,24},{9,25},{16,0},{17,1},{24,8},{25,9},{2,18},{3,... | collective-permute-start | bytes 344072 | tf_op jit(solution)/shard_map/ppermute | solution.py:484
  20.3 1.6 %collective-permute-start.6 = (bf16[448,128]{1,0:T(8,128)(2,1)S(1)}, bf16[448,128]{1,0:T(8,128)(2,1)S(1)}, u32[]{:S(2)}, u32[]{:S(2)}) collective-permute-start(bf16[448,128]{1,0:T(8,128)(2,1)S(1)} %get-tuple-element.67), channel_id=1, source_target_pairs={{0,8},{1,9},{8,0},{9,1},{16,24},{17,25},{24,16},{25,17},{2,10},{3,... | collective-permute-start | bytes 344072 | tf_op jit(solution)/shard_map/ppermute | solution.py:484
  21.9 0.2 collective-permute-start.5
  22.1 4.1 %input_gradient_interior.1 = (bf16[8,8,32,128]{3,2,1,0:T(8,128)(2,1)}, bf16[2,10,32,384]{3,2,1,0:T(8,128)(2,1)S(1)}, bf16[256,4608]{1,0:T(8,128)(2,1)S(1)}) custom-call(bf16[2,8,32,128]{3,2,1,0:T(8,128)(2,1)S(1)} %get-tuple-element.52.early, bf16[6,8,32,128]{3,2,1,0:T(8,128)(2,1)S(1)} %get-tuple-element.53.g, ...), custom_call_target="tpu_custom_call" | custom-call | flops 2717908992 | bytes 4194304 | tf_op jit(solution)/shard_map/input_gradient_interior/pallas_call | solution.py:526
  26.3 1.3 %collective-permute-start.10 = (bf16[18,32,128]{2,1,0:T(8,128)(2,1)S(1)}, bf16[18,32,128]{2,1,0:T(8,128)(2,1)S(1)}, u32[]{:S(2)}, u32[]{:S(2)}) collective-permute-start(bf16[18,32,128]{2,1,0:T(8,128)(2,1)S(1)} %pad_maximum_fusion.1), channel_id=1, source_target_pairs={{2,0},{4,2},{6,4},{3,1},{5,3},{7,5},{10,8},{12,10},{14,12},{11,9},... | collective-permute-start | bytes 442376 | tf_op jit(solution)/shard_map/ppermute | solution.py:494
  27.6 0.0 collective-permute-done.4
  27.6 2.3 %collective-permute-done.5 = bf16[448,128]{1,0:T(8,128)(2,1)S(1)} collective-permute-done((bf16[448,128]{1,0:T(8,128)(2,1)S(1)}, bf16[448,128]{1,0:T(8,128)(2,1)S(1)}, u32[]{:S(2)}, u32[]{:S(2)}) %collective-permute-start.5) | collective-permute-done | bytes 114720 | tf_op jit(solution)/shard_map/ppermute | solution.py:484
  29.9 0.1 fusion.2
  30.0 2.7 %collective-permute-start.9 = (bf16[448,128]{1,0:T(8,128)(2,1)S(1)}, bf16[448,128]{1,0:T(8,128)(2,1)S(1)}, u32[]{:S(2)}, u32[]{:S(2)}) collective-permute-start(bf16[448,128]{1,0:T(8,128)(2,1)S(1)} %fusion.2), channel_id=1, source_target_pairs={{0,6},{1,7},{2,4},{3,5},{4,2},{5,3},{6,0},{7,1},{8,14},{9,15},{10,... | collective-permute-start | bytes 344072 | tf_op jit(solution)/shard_map/ppermute | solution.py:484
  32.6 0.5 %collective-permute-start.8 = (bf16[448,128]{1,0:T(8,128)(2,1)S(1)}, bf16[448,128]{1,0:T(8,128)(2,1)S(1)}, u32[]{:S(2)}, u32[]{:S(2)}) collective-permute-start(bf16[448,128]{1,0:T(8,128)(2,1)S(1)} %fusion.2), channel_id=1, source_target_pairs={{0,4},{1,3},{2,6},{3,1},{4,0},{5,7},{6,2},{7,5},{8,12},{9,11},{10,... | collective-permute-start | bytes 344072 | tf_op jit(solution)/shard_map/ppermute | solution.py:484
  33.1 0.9 %collective-permute-start.7 = (bf16[448,128]{1,0:T(8,128)(2,1)S(1)}, bf16[448,128]{1,0:T(8,128)(2,1)S(1)}, u32[]{:S(2)}, u32[]{:S(2)}) collective-permute-start(bf16[448,128]{1,0:T(8,128)(2,1)S(1)} %fusion.2), channel_id=1, source_target_pairs={{0,2},{1,5},{2,0},{3,7},{4,6},{5,1},{6,4},{7,3},{8,10},{9,13},{10,... | collective-permute-start | bytes 344072 | tf_op jit(solution)/shard_map/ppermute | solution.py:484
  34.1 1.7 %input_gradient_last.1 = bf16[8,8,32,128]{3,2,1,0:T(8,128)(2,1)} custom-call(bf16[8,8,32,128]{3,2,1,0:T(8,128)(2,1)} %get-tuple-element.57.grad_in, bf16[2,10,32,384]{3,2,1,0:T(8,128)(2,1)S(1)} %get-tuple-element.59.last, bf16[18,32,128]{2,1,0:T(8,128)(2,1)S(1)} %collective-permute-done.10.after, ...), custom_call_target="tpu_custom_call", output_to_operand_aliasing={{}: (0, {})} | custom-call | flops 905969664 | bytes 4194304 | tf_op jit(solution)/shard_map/input_gradient_last/pallas_call | solution.py:526
  35.8 3.3 %collective-permute-done.9 = bf16[448,128]{1,0:T(8,128)(2,1)S(1)} collective-permute-done((bf16[448,128]{1,0:T(8,128)(2,1)S(1)}, bf16[448,128]{1,0:T(8,128)(2,1)S(1)}, u32[]{:S(2)}, u32[]{:S(2)}) %collective-permute-start.9) | collective-permute-done | bytes 114720 | tf_op jit(solution)/shard_map/ppermute | solution.py:484
  39.1 0.3 collective-permute-done.8
  39.4 0.1 add_convert_fusion.1.own
  39.5 0.1 collective-permute-start.11
  39.5 1.3 %collective-permute-done.11.other = bf16[448,128]{1,0:T(8,128)(2,1)S(1)} collective-permute-done((bf16[448,128]{1,0:T(8,128)(2,1)S(1)}, bf16[448,128]{1,0:T(8,128)(2,1)S(1)}, u32[]{:S(2)}, u32[]{:S(2)}) %collective-permute-start.11) | collective-permute-done | bytes 114720 | tf_op jit(solution)/shard_map/ppermute | solution.py:498
  40.8 0.9 %scaled_weights.1 = (f32[864,128]{1,0:T(8,128)}, f32[1,32]{1,0:T(1,128)}) custom-call(bf16[448,128]{1,0:T(8,128)(2,1)S(1)} %add_convert_fusion.1.own, bf16[448,128]{1,0:T(8,128)(2,1)S(1)} %collective-permute-done.11.other), custom_call_target="tpu_custom_call" | custom-call | flops 36238784 | bytes 4194304 | tf_op jit(solution)/shard_map/scaled_weights/pallas_call | solution.py:526
  (15 shorter events, 0.1 us)
Async XLA Ops:
  0.6 1.0 %copy-start.2 = (bf16[1,8,8,32,128]{4,3,2,1,0:T(8,128)(2,1)S(1)}, bf16[1,8,8,32,128]{4,3,2,1,0:T(8,128)(2,1)}, u32[]{:S(2)}) copy-start(bf16[1,8,8,32,128]{4,3,2,1,0:T(8,128)(2,1)} %param.4) | copy-start | bytes 1572868
  1.7 6.4 %copy-start = (bf16[1,8,8,32,128]{4,3,2,1,0:T(8,128)(2,1)S(1)}, bf16[1,8,8,32,128]{4,3,2,1,0:T(8,128)(2,1)}, u32[]{:S(2)}) copy-start(bf16[1,8,8,32,128]{4,3,2,1,0:T(8,128)(2,1)} %param.7) | copy-start | bytes 1572868
  1.7 6.4 %copy-start.1 = (bf16[3456,128]{1,0:T(8,128)(2,1)S(1)}, bf16[3456,128]{1,0:T(8,128)(2,1)}, u32[]{:S(2)}) copy-start(bf16[3456,128]{1,0:T(8,128)(2,1)} %kernel.3) | copy-start | bytes 2654212
  1.7 6.4 %copy-start.3 = (f32[128]{0:T(128)S(1)}, f32[128]{0:T(128)}, u32[]{:S(2)}) copy-start(f32[128]{0:T(128)} %param.6) | copy-start | bytes 1540
  1.9 1.4 %collective-permute-start = (bf16[8,32,128]{2,1,0:T(8,128)(2,1)S(1)}, bf16[8,32,128]{2,1,0:T(8,128)(2,1)S(1)}, u32[]{:S(2)}, u32[]{:S(2)}) collective-permute-start(bf16[8,32,128]{2,1,0:T(8,128)(2,1)S(1)} %get-tuple-element.35), channel_id=1, source_target_pairs={{0,1},{1,0},{2,3},{3,2},{4,5},{5,4},{6,7},{7,6},{8,9},{9,8},{10,11... | collective-permute-start | bytes 196616 | tf_op jit(solution)/shard_map/ppermute | solution.py:498
  3.3 9.0 %collective-permute-start.1 = (bf16[18,32,128]{2,1,0:T(8,128)(2,1)S(1)}, bf16[18,32,128]{2,1,0:T(8,128)(2,1)S(1)}, u32[]{:S(2)}, u32[]{:S(2)}) collective-permute-start(bf16[18,32,128]{2,1,0:T(8,128)(2,1)S(1)} %pad_maximum_fusion), channel_id=1, source_target_pairs={{0,2},{2,4},{4,6},{1,3},{3,5},{5,7},{8,10},{10,12},{12,14},{9,11},... | collective-permute-start | bytes 442376 | tf_op jit(solution)/shard_map/ppermute | solution.py:494
  15.6 1.9 %collective-permute-start.3 = (bf16[4,448,128]{2,1,0:T(8,128)(2,1)S(1)}, bf16[4,448,128]{2,1,0:T(8,128)(2,1)S(1)}, u32[]{:S(2)}, u32[]{:S(2)}) collective-permute-start(bf16[4,448,128]{2,1,0:T(8,128)(2,1)S(1)} %get-tuple-element.50), channel_id=1, source_target_pairs={{0,1},{1,0},{2,3},{3,2},{4,5},{5,4},{6,7},{7,6},{8,9},{9,8},{10,11... | collective-permute-start | bytes 1376264 | tf_op jit(solution)/shard_map/ppermute | solution.py:498
  15.7 1.9 %collective-permute-start.2 = (bf16[8,32,128]{2,1,0:T(8,128)(2,1)S(1)}, bf16[8,32,128]{2,1,0:T(8,128)(2,1)S(1)}, u32[]{:S(2)}, u32[]{:S(2)}) collective-permute-start(bf16[8,32,128]{2,1,0:T(8,128)(2,1)S(1)} %get-tuple-element.45), channel_id=1, source_target_pairs={{0,1},{1,0},{2,3},{3,2},{4,5},{5,4},{6,7},{7,6},{8,9},{9,8},{10,11... | collective-permute-start | bytes 196616 | tf_op jit(solution)/shard_map/ppermute | solution.py:498
  17.7 10.0 %collective-permute-start.4 = (bf16[448,128]{1,0:T(8,128)(2,1)S(1)}, bf16[448,128]{1,0:T(8,128)(2,1)S(1)}, u32[]{:S(2)}, u32[]{:S(2)}) collective-permute-start(bf16[448,128]{1,0:T(8,128)(2,1)S(1)} %get-tuple-element.66), channel_id=1, source_target_pairs={{0,16},{1,17},{8,24},{9,25},{16,0},{17,1},{24,8},{25,9},{2,18},{3,... | collective-permute-start | bytes 344072 | tf_op jit(solution)/shard_map/ppermute | solution.py:484
  20.3 7.3 %collective-permute-start.6 = (bf16[448,128]{1,0:T(8,128)(2,1)S(1)}, bf16[448,128]{1,0:T(8,128)(2,1)S(1)}, u32[]{:S(2)}, u32[]{:S(2)}) collective-permute-start(bf16[448,128]{1,0:T(8,128)(2,1)S(1)} %get-tuple-element.67), channel_id=1, source_target_pairs={{0,8},{1,9},{8,0},{9,1},{16,24},{17,25},{24,16},{25,17},{2,10},{3,... | collective-permute-start | bytes 344072 | tf_op jit(solution)/shard_map/ppermute | solution.py:484
  21.9 8.0 %collective-permute-start.5 = (bf16[448,128]{1,0:T(8,128)(2,1)S(1)}, bf16[448,128]{1,0:T(8,128)(2,1)S(1)}, u32[]{:S(2)}, u32[]{:S(2)}) collective-permute-start(bf16[448,128]{1,0:T(8,128)(2,1)S(1)} %get-tuple-element.68), channel_id=1, source_target_pairs={{0,24},{1,25},{8,16},{9,17},{16,8},{17,9},{24,0},{25,1},{2,26},{3,... | collective-permute-start | bytes 344072 | tf_op jit(solution)/shard_map/ppermute | solution.py:484
  26.3 7.8 %collective-permute-start.10 = (bf16[18,32,128]{2,1,0:T(8,128)(2,1)S(1)}, bf16[18,32,128]{2,1,0:T(8,128)(2,1)S(1)}, u32[]{:S(2)}, u32[]{:S(2)}) collective-permute-start(bf16[18,32,128]{2,1,0:T(8,128)(2,1)S(1)} %pad_maximum_fusion.1), channel_id=1, source_target_pairs={{2,0},{4,2},{6,4},{3,1},{5,3},{7,5},{10,8},{12,10},{14,12},{11,9},... | collective-permute-start | bytes 442376 | tf_op jit(solution)/shard_map/ppermute | solution.py:494
  30.0 9.1 %collective-permute-start.9 = (bf16[448,128]{1,0:T(8,128)(2,1)S(1)}, bf16[448,128]{1,0:T(8,128)(2,1)S(1)}, u32[]{:S(2)}, u32[]{:S(2)}) collective-permute-start(bf16[448,128]{1,0:T(8,128)(2,1)S(1)} %fusion.2), channel_id=1, source_target_pairs={{0,6},{1,7},{2,4},{3,5},{4,2},{5,3},{6,0},{7,1},{8,14},{9,15},{10,... | collective-permute-start | bytes 344072 | tf_op jit(solution)/shard_map/ppermute | solution.py:484
  32.6 6.8 %collective-permute-start.8 = (bf16[448,128]{1,0:T(8,128)(2,1)S(1)}, bf16[448,128]{1,0:T(8,128)(2,1)S(1)}, u32[]{:S(2)}, u32[]{:S(2)}) collective-permute-start(bf16[448,128]{1,0:T(8,128)(2,1)S(1)} %fusion.2), channel_id=1, source_target_pairs={{0,4},{1,3},{2,6},{3,1},{4,0},{5,7},{6,2},{7,5},{8,12},{9,11},{10,... | collective-permute-start | bytes 344072 | tf_op jit(solution)/shard_map/ppermute | solution.py:484
  33.1 6.3 %collective-permute-start.7 = (bf16[448,128]{1,0:T(8,128)(2,1)S(1)}, bf16[448,128]{1,0:T(8,128)(2,1)S(1)}, u32[]{:S(2)}, u32[]{:S(2)}) collective-permute-start(bf16[448,128]{1,0:T(8,128)(2,1)S(1)} %fusion.2), channel_id=1, source_target_pairs={{0,2},{1,5},{2,0},{3,7},{4,6},{5,1},{6,4},{7,3},{8,10},{9,13},{10,... | collective-permute-start | bytes 344072 | tf_op jit(solution)/shard_map/ppermute | solution.py:484
  39.5 1.4 %collective-permute-start.11 = (bf16[448,128]{1,0:T(8,128)(2,1)S(1)}, bf16[448,128]{1,0:T(8,128)(2,1)S(1)}, u32[]{:S(2)}, u32[]{:S(2)}) collective-permute-start(bf16[448,128]{1,0:T(8,128)(2,1)S(1)} %add_convert_fusion.1.own), channel_id=1, source_target_pairs={{0,1},{1,0},{2,3},{3,2},{4,5},{5,4},{6,7},{7,6},{8,9},{9,8},{10,11... | collective-permute-start | bytes 344072 | tf_op jit(solution)/shard_map/ppermute | solution.py:498

commit v8 on v7

--- a/solution.py
+++ b/solution.py
@@ -415,17 +415,10 @@
     copy.wait()
 
 
-def border_kernel(x, edge, tail, copied):
-    frames, height = x.shape[:2]
-    row = jnp.where(lax.axis_index("tile") == 0, height - 1, 0)
-    copies = [
-        pltpu.make_async_copy(x.at[:, row], edge, copied.at[0]),
-        pltpu.make_async_copy(x.at[frames - 2 : frames], tail, copied.at[1]),
-    ]
-    for copy in copies:
-        copy.start()
-    for copy in copies:
-        copy.wait()
+def border_kernel(tail, edge, border):
+    count = tail.shape[0]
+    border[0:count] = tail[...]
+    border[count:] = edge[edge.shape[0] - 2 :]
 
 
 def closing_kernel(own, other, weight, bias, *, scale, arranged):
@@ -540,24 +533,19 @@
         )(*args)
 
     dma, vmem = pltpu.SemaphoreType.DMA, pltpu.VMEM
-    edge, tail = call(
+    row = jnp.where(tile == 0, height - 1, 0)
+    edge = swapped(lax.dynamic_index_in_dim(x, row, 1, False))
+    (border,) = call(
         border_kernel,
         "border_rows",
         2.0,
-        arrays((frames, breadth, channels), frames_shape(2)),
-        [dma((2,))],
-        (0,),
+        arrays((2 * height + 2, breadth, channels)),
+        [],
         (),
-        (x,),
-    )
-    edge = swapped(edge)
-    before = passed_along(
-        jnp.concatenate(
-            [tail.reshape(2 * height, breadth, channels), edge[frames - 2 :]], axis=0
-        ),
-        "tm",
-        1,
-    )
+        (),
+        (x[frames - 2 :].reshape(2 * height, breadth, channels), edge),
+    )
+    before = passed_along(border, "tm", 1)
     block_out, windows, taps, turned, later_grads, later_edge, total, begun = call(
         interior_kernel,
         "forward_interior",

time: 42.3 us -> 42 us (level)
  waiting for transfers between devices: 8.28 us -> 7.41 us
  local copies, waits for them, and re-layouts: 1.08 us -> 1.82 us
    unnamed x8, local copies, waits for them, and re-layouts: 1.05 us -> 0.03 us
    slice x1, local copies, waits for them, and re-layouts: 0.01 us -> 0.91 us  [body(): x[frames - 2:].reshape(2 * height, breadth, channels)]
    ppermute x4, waiting for transfers between devices: 2.41 us -> 1.51 us  [swapped(): return lax.ppermute(block, 'tile', [(0, 1), (1, 0)])]
    squeeze x0 -> x1, local copies, waits for them, and re-layouts: none -> 0.85 us  [body(): edge = swapped(lax.dynamic_index_in_dim(x, row, 1, False))]
  transfers between devices with their start and end apart: 12 -> 12, of which waited for: 6 -> 5; matrix products, arithmetic and copies ran while one was open for 0% -> 3% of each run, Pallas kernels for 27% -> 27%
where the time goes in v8:
time: 42 us; the launch traced here: 41.5 us
  starting transfers between devices  15.8 us (38%)
  Pallas kernels  15.3 us (36%)
  waiting for transfers between devices  7.41 us (18%)
  local copies, waits for them, and re-layouts  1.82 us (4%)
  between operations  0.85 us (2%)
    pallas_call x7, Pallas kernels, call(): pl.pallas_call(kernel_body, out_shape=shapes, in_specs=[there if i in far...  15.3 us
    ppermute x6, starting transfers between devices, exchange(): return lax.ppermute(block, (axis, 'tile'), route)  8.62 us
    ppermute x2, starting transfers between devices, passed_along(): return lax.ppermute(block, axis, route)  6.11 us
    ppermute x6, waiting for transfers between devices, exchange(): return lax.ppermute(block, (axis, 'tile'), route)  5.9 us
    ppermute x4, waiting for transfers between devices, swapped(): return lax.ppermute(block, 'tile', [(0, 1), (1, 0)])  1.51 us
    ppermute x4, starting transfers between devices, swapped(): return lax.ppermute(block, 'tile', [(0, 1), (1, 0)])  1.09 us
    slice x1, local copies, waits for them, and re-layouts, body(): x[frames - 2:].reshape(2 * height, breadth, channels)  0.91 us
    squeeze x1, local copies, waits for them, and re-layouts, body(): edge = swapped(lax.dynamic_index_in_dim(x, row, 1, False))  0.85 us
  transfers between devices with their start and end apart: 12, of which 5 were waited for; matrix products, arithmetic and copies ran while one was open for 3% of the time, Pallas kernels for 27%

profile of v8, /device:TPU:0, one launch (start us, length us, event | category | flops | bytes accessed | tf_op | source)
XLA Modules:
  0.0 41.5 jit_solution(13795319167159773513)
XLA Ops:
  0.6 0.9 %dynamic-slice_bitcast_fusion = bf16[8,32,128]{2,1,0:T(8,128)(2,1)S(1)} fusion(bf16[1,8,8,32,128]{4,3,2,1,0:T(8,128)(2,1)} %param.4, s32[]{:T(128)S(6)} %select_n.6), kind=kLoop, calls=%fused_computation.10 | loop fusion | bytes 131076 | tf_op jit(solution)/shard_map/jit(dynamic_index_in_dim)/squeeze | solution.py:537
  1.5 0.5 %collective-permute-start = (bf16[8,32,128]{2,1,0:T(8,128)(2,1)S(1)}, bf16[8,32,128]{2,1,0:T(8,128)(2,1)S(1)}, u32[]{:S(2)}, u32[]{:S(2)}) collective-permute-start(bf16[8,32,128]{2,1,0:T(8,128)(2,1)S(1)} %dynamic-slice_bitcast_fusion), channel_id=1, source_target_pairs={{0,1},{1,0},{2,3},{3,2},{4,5},{5,4},{6,7},{7,6},{8,9},{9,8},{10,11... | collective-permute-start | bytes 196616 | tf_op jit(solution)/shard_map/ppermute | solution.py:491
  1.9 0.9 %slice.19 = bf16[1,2,8,32,128]{4,3,2,1,0:T(8,128)(2,1)S(1)} slice(bf16[1,8,8,32,128]{4,3,2,1,0:T(8,128)(2,1)} %param.4), slice={[0:1], [6:8], [0:8], [0:32], [0:128]} | slice | bytes 262144 | tf_op jit(solution)/shard_map/slice | solution.py:546
  2.9 0.0 copy-start
  2.9 0.0 copy-start.1
  2.9 0.0 copy-start.3
  2.9 4.8 %collective-permute-start.1 = (bf16[18,32,128]{2,1,0:T(8,128)(2,1)S(1)}, bf16[18,32,128]{2,1,0:T(8,128)(2,1)S(1)}, u32[]{:S(2)}, u32[]{:S(2)}) collective-permute-start(bf16[18,32,128]{2,1,0:T(8,128)(2,1)S(1)} %border_rows.1), channel_id=1, source_target_pairs={{0,2},{2,4},{4,6},{1,3},{3,5},{5,7},{8,10},{10,12},{12,14},{9,11},... | collective-permute-start | bytes 442376 | tf_op jit(solution)/shard_map/ppermute | solution.py:487
  7.8 4.2 %forward_interior.1 = (bf16[8,8,32,128]{3,2,1,0:T(8,128)(2,1)}, bf16[8,10,32,384]{3,2,1,0:T(8,128)(2,1)S(1)}, bf16[4608,256]{1,0:T(8,128)(2,1)S(1)}, bf16[3,256,...) custom-call(bf16[8,8,32,128]{3,2,1,0:T(8,128)(2,1)S(1)} %bitcast.25,, ...), custom_call_target="tpu_custom_call" | custom-call | flops 2717908992 | bytes 4194304 | tf_op jit(solution)/shard_map/forward_interior/pallas_call | solution.py:519
  12.0 3.3 %first_frames_and_leaving_half.1 = (bf16[8,8,32,128]{3,2,1,0:T(8,128)(2,1)}, bf16[2,8,32,128]{3,2,1,0:T(8,128)(2,1)S(1)}, bf16[8,32,128]{2,1,0:T(8,128)(2,1)S(1)...) custom-call(bf16[8,8,32,128]{3,2,1,0:T(8,128)(2,1)} %get-tuple-eleme, ...), custom_call_target="tpu_custom_call", output_to_operand_aliasing={{0}: (0, {})} | custom-call | flops 2899102976 | bytes 4194304 | tf_op jit(solution)/shard_map/first_frames_and_leaving_half/pallas_call | solution.py:519
  15.3 0.1 collective-permute-start.3
  15.4 0.5 %collective-permute-start.2 = (bf16[8,32,128]{2,1,0:T(8,128)(2,1)S(1)}, bf16[8,32,128]{2,1,0:T(8,128)(2,1)S(1)}, u32[]{:S(2)}, u32[]{:S(2)}) collective-permute-start(bf16[8,32,128]{2,1,0:T(8,128)(2,1)S(1)} %get-tuple-element.41), channel_id=1, source_target_pairs={{0,1},{1,0},{2,3},{3,2},{4,5},{5,4},{6,7},{7,6},{8,9},{9,8},{10,11... | collective-permute-start | bytes 196616 | tf_op jit(solution)/shard_map/ppermute | solution.py:491
  15.8 1.1 %staying_half.1 = bf16[4,448,128]{2,1,0:T(8,128)(2,1)S(1)} custom-call(bf16[9,384,128]{2,1,0:T(8,128)(2,1)S(1)} %get-tuple-element.42.blocks_in, bf16[4,10,32,384]{3,2,1,0:T(8,128)(2,1)S(1)} %get-tuple-element.43.front, bf16[8,10,32,384]{3,2,1,0:T(8,128)(2,1)S(1)} %get-tuple-element.34.windows, bf16[128,2048]{1,0:T(8,128)(2,1)S(1)} %get-tuple-element.44.grads, ...), custom_call_target="tpu_custom_call" | custom-call | flops 1630745344 | bytes 4194304 | tf_op jit(solution)/shard_map/staying_half/pallas_call | solution.py:519
  17.0 0.2 collective-permute-done.3
  17.2 0.1 add_convert_fusion
  17.3 2.7 %collective-permute-start.4 = (bf16[448,128]{1,0:T(8,128)(2,1)S(1)}, bf16[448,128]{1,0:T(8,128)(2,1)S(1)}, u32[]{:S(2)}, u32[]{:S(2)}) collective-permute-start(bf16[448,128]{1,0:T(8,128)(2,1)S(1)} %get-tuple-element.62), channel_id=1, source_target_pairs={{0,16},{1,17},{8,24},{9,25},{16,0},{17,1},{24,8},{25,9},{2,18},{3,... | collective-permute-start | bytes 344072 | tf_op jit(solution)/shard_map/ppermute | solution.py:477
  20.0 1.6 %collective-permute-start.6 = (bf16[448,128]{1,0:T(8,128)(2,1)S(1)}, bf16[448,128]{1,0:T(8,128)(2,1)S(1)}, u32[]{:S(2)}, u32[]{:S(2)}) collective-permute-start(bf16[448,128]{1,0:T(8,128)(2,1)S(1)} %get-tuple-element.63), channel_id=1, source_target_pairs={{0,8},{1,9},{8,0},{9,1},{16,24},{17,25},{24,16},{25,17},{2,10},{3,... | collective-permute-start | bytes 344072 | tf_op jit(solution)/shard_map/ppermute | solution.py:477
  21.6 0.2 collective-permute-start.5
  21.8 4.1 %input_gradient_interior.1 = (bf16[8,8,32,128]{3,2,1,0:T(8,128)(2,1)}, bf16[2,10,32,384]{3,2,1,0:T(8,128)(2,1)S(1)}, bf16[256,4608]{1,0:T(8,128)(2,1)S(1)}) custom-call(bf16[2,8,32,128]{3,2,1,0:T(8,128)(2,1)S(1)} %get-tuple-element.48.early, bf16[6,8,32,128]{3,2,1,0:T(8,128)(2,1)S(1)} %get-tuple-element.49.g, ...), custom_call_target="tpu_custom_call" | custom-call | flops 2717908992 | bytes 4194304 | tf_op jit(solution)/shard_map/input_gradient_interior/pallas_call | solution.py:519
  26.0 1.3 %collective-permute-start.10 = (bf16[18,32,128]{2,1,0:T(8,128)(2,1)S(1)}, bf16[18,32,128]{2,1,0:T(8,128)(2,1)S(1)}, u32[]{:S(2)}, u32[]{:S(2)}) collective-permute-start(bf16[18,32,128]{2,1,0:T(8,128)(2,1)S(1)} %pad_maximum_fusion), channel_id=1, source_target_pairs={{2,0},{4,2},{6,4},{3,1},{5,3},{7,5},{10,8},{12,10},{14,12},{11,9},... | collective-permute-start | bytes 442376 | tf_op jit(solution)/shard_map/ppermute | solution.py:487
  27.3 0.0 collective-permute-done.4
  27.3 2.3 %collective-permute-done.5 = bf16[448,128]{1,0:T(8,128)(2,1)S(1)} collective-permute-done((bf16[448,128]{1,0:T(8,128)(2,1)S(1)}, bf16[448,128]{1,0:T(8,128)(2,1)S(1)}, u32[]{:S(2)}, u32[]{:S(2)}) %collective-permute-start.5) | collective-permute-done | bytes 114720 | tf_op jit(solution)/shard_map/ppermute | solution.py:477
  29.6 0.1 fusion.2
  29.6 2.7 %collective-permute-start.9 = (bf16[448,128]{1,0:T(8,128)(2,1)S(1)}, bf16[448,128]{1,0:T(8,128)(2,1)S(1)}, u32[]{:S(2)}, u32[]{:S(2)}) collective-permute-start(bf16[448,128]{1,0:T(8,128)(2,1)S(1)} %fusion.2), channel_id=1, source_target_pairs={{0,6},{1,7},{2,4},{3,5},{4,2},{5,3},{6,0},{7,1},{8,14},{9,15},{10,... | collective-permute-start | bytes 344072 | tf_op jit(solution)/shard_map/ppermute | solution.py:477
  32.4 0.5 %collective-permute-start.8 = (bf16[448,128]{1,0:T(8,128)(2,1)S(1)}, bf16[448,128]{1,0:T(8,128)(2,1)S(1)}, u32[]{:S(2)}, u32[]{:S(2)}) collective-permute-start(bf16[448,128]{1,0:T(8,128)(2,1)S(1)} %fusion.2), channel_id=1, source_target_pairs={{0,4},{1,3},{2,6},{3,1},{4,0},{5,7},{6,2},{7,5},{8,12},{9,11},{10,... | collective-permute-start | bytes 344072 | tf_op jit(solution)/shard_map/ppermute | solution.py:477
  32.9 0.9 %collective-permute-start.7 = (bf16[448,128]{1,0:T(8,128)(2,1)S(1)}, bf16[448,128]{1,0:T(8,128)(2,1)S(1)}, u32[]{:S(2)}, u32[]{:S(2)}) collective-permute-start(bf16[448,128]{1,0:T(8,128)(2,1)S(1)} %fusion.2), channel_id=1, source_target_pairs={{0,2},{1,5},{2,0},{3,7},{4,6},{5,1},{6,4},{7,3},{8,10},{9,13},{10,... | collective-permute-start | bytes 344072 | tf_op jit(solution)/shard_map/ppermute | solution.py:477
  33.8 1.7 %input_gradient_last.1 = bf16[8,8,32,128]{3,2,1,0:T(8,128)(2,1)} custom-call(bf16[8,8,32,128]{3,2,1,0:T(8,128)(2,1)} %get-tuple-element.53.grad_in, bf16[2,10,32,384]{3,2,1,0:T(8,128)(2,1)S(1)} %get-tuple-element.55.last, bf16[18,32,128]{2,1,0:T(8,128)(2,1)S(1)} %collective-permute-done.10.after, ...), custom_call_target="tpu_custom_call", output_to_operand_aliasing={{}: (0, {})} | custom-call | flops 905969664 | bytes 4194304 | tf_op jit(solution)/shard_map/input_gradient_last/pallas_call | solution.py:519
  35.6 3.3 %collective-permute-done.9 = bf16[448,128]{1,0:T(8,128)(2,1)S(1)} collective-permute-done((bf16[448,128]{1,0:T(8,128)(2,1)S(1)}, bf16[448,128]{1,0:T(8,128)(2,1)S(1)}, u32[]{:S(2)}, u32[]{:S(2)}) %collective-permute-start.9) | collective-permute-done | bytes 114720 | tf_op jit(solution)/shard_map/ppermute | solution.py:477
  38.9 0.3 collective-permute-done.8
  39.2 0.1 add_convert_fusion.1.own
  39.2 0.1 collective-permute-start.11
  39.3 1.3 %collective-permute-done.11.other = bf16[448,128]{1,0:T(8,128)(2,1)S(1)} collective-permute-done((bf16[448,128]{1,0:T(8,128)(2,1)S(1)}, bf16[448,128]{1,0:T(8,128)(2,1)S(1)}, u32[]{:S(2)}, u32[]{:S(2)}) %collective-permute-start.11) | collective-permute-done | bytes 114720 | tf_op jit(solution)/shard_map/ppermute | solution.py:491
  40.6 0.9 %scaled_weights.1 = (f32[864,128]{1,0:T(8,128)}, f32[1,32]{1,0:T(1,128)}) custom-call(bf16[448,128]{1,0:T(8,128)(2,1)S(1)} %add_convert_fusion.1.own, bf16[448,128]{1,0:T(8,128)(2,1)S(1)} %collective-permute-done.11.other), custom_call_target="tpu_custom_call" | custom-call | flops 36238784 | bytes 4194304 | tf_op jit(solution)/shard_map/scaled_weights/pallas_call | solution.py:519
  (15 shorter events, 0.1 us)
Async XLA Ops:
  1.5 1.4 %collective-permute-start = (bf16[8,32,128]{2,1,0:T(8,128)(2,1)S(1)}, bf16[8,32,128]{2,1,0:T(8,128)(2,1)S(1)}, u32[]{:S(2)}, u32[]{:S(2)}) collective-permute-start(bf16[8,32,128]{2,1,0:T(8,128)(2,1)S(1)} %dynamic-slice_bitcast_fusion), channel_id=1, source_target_pairs={{0,1},{1,0},{2,3},{3,2},{4,5},{5,4},{6,7},{7,6},{8,9},{9,8},{10,11... | collective-permute-start | bytes 196616 | tf_op jit(solution)/shard_map/ppermute | solution.py:491
  2.9 4.9 %copy-start = (bf16[1,8,8,32,128]{4,3,2,1,0:T(8,128)(2,1)S(1)}, bf16[1,8,8,32,128]{4,3,2,1,0:T(8,128)(2,1)}, u32[]{:S(2)}) copy-start(bf16[1,8,8,32,128]{4,3,2,1,0:T(8,128)(2,1)} %param.7) | copy-start | bytes 1572868
  2.9 4.9 %copy-start.1 = (bf16[1,8,8,32,128]{4,3,2,1,0:T(8,128)(2,1)S(1)}, bf16[1,8,8,32,128]{4,3,2,1,0:T(8,128)(2,1)}, u32[]{:S(2)}) copy-start(bf16[1,8,8,32,128]{4,3,2,1,0:T(8,128)(2,1)} %param.4) | copy-start | bytes 1572868
  2.9 4.9 %copy-start.2 = (bf16[3456,128]{1,0:T(8,128)(2,1)S(1)}, bf16[3456,128]{1,0:T(8,128)(2,1)}, u32[]{:S(2)}) copy-start(bf16[3456,128]{1,0:T(8,128)(2,1)} %kernel.3) | copy-start | bytes 2654212
  2.9 4.9 %copy-start.3 = (f32[128]{0:T(128)S(1)}, f32[128]{0:T(128)}, u32[]{:S(2)}) copy-start(f32[128]{0:T(128)} %param.6) | copy-start | bytes 1540
  2.9 9.0 %collective-permute-start.1 = (bf16[18,32,128]{2,1,0:T(8,128)(2,1)S(1)}, bf16[18,32,128]{2,1,0:T(8,128)(2,1)S(1)}, u32[]{:S(2)}, u32[]{:S(2)}) collective-permute-start(bf16[18,32,128]{2,1,0:T(8,128)(2,1)S(1)} %border_rows.1), channel_id=1, source_target_pairs={{0,2},{2,4},{4,6},{1,3},{3,5},{5,7},{8,10},{10,12},{12,14},{9,11},... | collective-permute-start | bytes 442376 | tf_op jit(solution)/shard_map/ppermute | solution.py:487
  15.3 1.9 %collective-permute-start.3 = (bf16[4,448,128]{2,1,0:T(8,128)(2,1)S(1)}, bf16[4,448,128]{2,1,0:T(8,128)(2,1)S(1)}, u32[]{:S(2)}, u32[]{:S(2)}) collective-permute-start(bf16[4,448,128]{2,1,0:T(8,128)(2,1)S(1)} %get-tuple-element.46), channel_id=1, source_target_pairs={{0,1},{1,0},{2,3},{3,2},{4,5},{5,4},{6,7},{7,6},{8,9},{9,8},{10,11... | collective-permute-start | bytes 1376264 | tf_op jit(solution)/shard_map/ppermute | solution.py:491
  15.4 1.9 %collective-permute-start.2 = (bf16[8,32,128]{2,1,0:T(8,128)(2,1)S(1)}, bf16[8,32,128]{2,1,0:T(8,128)(2,1)S(1)}, u32[]{:S(2)}, u32[]{:S(2)}) collective-permute-start(bf16[8,32,128]{2,1,0:T(8,128)(2,1)S(1)} %get-tuple-element.41), channel_id=1, source_target_pairs={{0,1},{1,0},{2,3},{3,2},{4,5},{5,4},{6,7},{7,6},{8,9},{9,8},{10,11... | collective-permute-start | bytes 196616 | tf_op jit(solution)/shard_map/ppermute | solution.py:491
  17.3 10.0 %collective-permute-start.4 = (bf16[448,128]{1,0:T(8,128)(2,1)S(1)}, bf16[448,128]{1,0:T(8,128)(2,1)S(1)}, u32[]{:S(2)}, u32[]{:S(2)}) collective-permute-start(bf16[448,128]{1,0:T(8,128)(2,1)S(1)} %get-tuple-element.62), channel_id=1, source_target_pairs={{0,16},{1,17},{8,24},{9,25},{16,0},{17,1},{24,8},{25,9},{2,18},{3,... | collective-permute-start | bytes 344072 | tf_op jit(solution)/shard_map/ppermute | solution.py:477
  20.0 7.3 %collective-permute-start.6 = (bf16[448,128]{1,0:T(8,128)(2,1)S(1)}, bf16[448,128]{1,0:T(8,128)(2,1)S(1)}, u32[]{:S(2)}, u32[]{:S(2)}) collective-permute-start(bf16[448,128]{1,0:T(8,128)(2,1)S(1)} %get-tuple-element.63), channel_id=1, source_target_pairs={{0,8},{1,9},{8,0},{9,1},{16,24},{17,25},{24,16},{25,17},{2,10},{3,... | collective-permute-start | bytes 344072 | tf_op jit(solution)/shard_map/ppermute | solution.py:477
  21.6 8.0 %collective-permute-start.5 = (bf16[448,128]{1,0:T(8,128)(2,1)S(1)}, bf16[448,128]{1,0:T(8,128)(2,1)S(1)}, u32[]{:S(2)}, u32[]{:S(2)}) collective-permute-start(bf16[448,128]{1,0:T(8,128)(2,1)S(1)} %get-tuple-element.64), channel_id=1, source_target_pairs={{0,24},{1,25},{8,16},{9,17},{16,8},{17,9},{24,0},{25,1},{2,26},{3,... | collective-permute-start | bytes 344072 | tf_op jit(solution)/shard_map/ppermute | solution.py:477
  26.0 7.8 %collective-permute-start.10 = (bf16[18,32,128]{2,1,0:T(8,128)(2,1)S(1)}, bf16[18,32,128]{2,1,0:T(8,128)(2,1)S(1)}, u32[]{:S(2)}, u32[]{:S(2)}) collective-permute-start(bf16[18,32,128]{2,1,0:T(8,128)(2,1)S(1)} %pad_maximum_fusion), channel_id=1, source_target_pairs={{2,0},{4,2},{6,4},{3,1},{5,3},{7,5},{10,8},{12,10},{14,12},{11,9},... | collective-permute-start | bytes 442376 | tf_op jit(solution)/shard_map/ppermute | solution.py:487
  29.6 9.2 %collective-permute-start.9 = (bf16[448,128]{1,0:T(8,128)(2,1)S(1)}, bf16[448,128]{1,0:T(8,128)(2,1)S(1)}, u32[]{:S(2)}, u32[]{:S(2)}) collective-permute-start(bf16[448,128]{1,0:T(8,128)(2,1)S(1)} %fusion.2), channel_id=1, source_target_pairs={{0,6},{1,7},{2,4},{3,5},{4,2},{5,3},{6,0},{7,1},{8,14},{9,15},{10,... | collective-permute-start | bytes 344072 | tf_op jit(solution)/shard_map/ppermute | solution.py:477
  32.4 6.8 %collective-permute-start.8 = (bf16[448,128]{1,0:T(8,128)(2,1)S(1)}, bf16[448,128]{1,0:T(8,128)(2,1)S(1)}, u32[]{:S(2)}, u32[]{:S(2)}) collective-permute-start(bf16[448,128]{1,0:T(8,128)(2,1)S(1)} %fusion.2), channel_id=1, source_target_pairs={{0,4},{1,3},{2,6},{3,1},{4,0},{5,7},{6,2},{7,5},{8,12},{9,11},{10,... | collective-permute-start | bytes 344072 | tf_op jit(solution)/shard_map/ppermute | solution.py:477
  32.9 6.3 %collective-permute-start.7 = (bf16[448,128]{1,0:T(8,128)(2,1)S(1)}, bf16[448,128]{1,0:T(8,128)(2,1)S(1)}, u32[]{:S(2)}, u32[]{:S(2)}) collective-permute-start(bf16[448,128]{1,0:T(8,128)(2,1)S(1)} %fusion.2), channel_id=1, source_target_pairs={{0,2},{1,5},{2,0},{3,7},{4,6},{5,1},{6,4},{7,3},{8,10},{9,13},{10,... | collective-permute-start | bytes 344072 | tf_op jit(solution)/shard_map/ppermute | solution.py:477
  39.2 1.4 %collective-permute-start.11 = (bf16[448,128]{1,0:T(8,128)(2,1)S(1)}, bf16[448,128]{1,0:T(8,128)(2,1)S(1)}, u32[]{:S(2)}, u32[]{:S(2)}) collective-permute-start(bf16[448,128]{1,0:T(8,128)(2,1)S(1)} %add_convert_fusion.1.own), channel_id=1, source_target_pairs={{0,1},{1,0},{2,3},{3,2},{4,5},{5,4},{6,7},{7,6},{8,9},{9,8},{10,11... | collective-permute-start | bytes 344072 | tf_op jit(solution)/shard_map/ppermute | solution.py:491

commit v9 on v8

--- a/solution.py
+++ b/solution.py
@@ -97,9 +97,13 @@
     taps[3 * rows :, 0:channels] = jnp.zeros((rows, channels), BF16)
     taps[0:rows, channels:] = jnp.zeros((rows, channels), BF16)
     taps[rows:, channels:] = kernel[...]
-    @pl.loop(0, frames)
+    @pl.loop(0, frames, unroll=2)
     def _(f):
         fill_windows(windows, f, x[f], edge[f], tile)
+
+    begun[...] = jnp.dot(
+        window_block([windows[0], windows[1]]), taps[2 * rows :], preferred_element_type=F32
+    )
 
     bias_copy.wait()
     up_copy.wait()
@@ -131,10 +135,6 @@
         turned[p] = jnp.concatenate([outs[0][1], outs[1][1]], axis=1).T
         total[...] += summed
         leave(p).start()
-
-    begun[...] = jnp.dot(
-        window_block([windows[0], windows[1]]), taps[2 * rows :], preferred_element_type=F32
-    )
 
     @pl.loop(0, frames // 2 - 1)
     def _(p):

time: 42 us -> 42 us (level)
  Pallas kernels: 15.3 us -> 16 us
  starting transfers between devices: 15.8 us -> 15.2 us
    pallas_call x7, Pallas kernels: 15.3 us -> 16 us  [call(): pl.pallas_call(kernel_body, out_shape=shapes, in_specs=[there if i in far...]
    ppermute x6, starting transfers between devices: 8.62 us -> 8.01 us  [exchange(): return lax.ppermute(block, (axis, 'tile'), route)]
  transfers between devices with their start and end apart: 12 -> 12, of which waited for: 5 -> 5; matrix products, arithmetic and copies ran while one was open for 3% -> 3% of each run, Pallas kernels for 27% -> 29%
where the time goes in v9:
time: 42 us; the launch traced here: 41.5 us
  Pallas kernels  16 us (38%)
  starting transfers between devices  15.2 us (36%)
  waiting for transfers between devices  7.31 us (17%)
  local copies, waits for them, and re-layouts  1.82 us (4%)
  between operations  0.85 us (2%)
    pallas_call x7, Pallas kernels, call(): pl.pallas_call(kernel_body, out_shape=shapes, in_specs=[there if i in far...  16 us
    ppermute x6, starting transfers between devices, exchange(): return lax.ppermute(block, (axis, 'tile'), route)  8.01 us
    ppermute x2, starting transfers between devices, passed_along(): return lax.ppermute(block, axis, route)  6.11 us
    ppermute x6, waiting for transfers between devices, exchange(): return lax.ppermute(block, (axis, 'tile'), route)  5.8 us
    ppermute x4, waiting for transfers between devices, swapped(): return lax.ppermute(block, 'tile', [(0, 1), (1, 0)])  1.5 us
    ppermute x4, starting transfers between devices, swapped(): return lax.ppermute(block, 'tile', [(0, 1), (1, 0)])  1.09 us
    slice x1, local copies, waits for them, and re-layouts, body(): x[frames - 2:].reshape(2 * height, breadth, channels)  0.91 us
    squeeze x1, local copies, waits for them, and re-layouts, body(): edge = swapped(lax.dynamic_index_in_dim(x, row, 1, False))  0.85 us
  transfers between devices with their start and end apart: 12, of which 5 were waited for; matrix products, arithmetic and copies ran while one was open for 3% of the time, Pallas kernels for 29%

profile of v9, /device:TPU:0, one launch (start us, length us, event | category | flops | bytes accessed | tf_op | source)
XLA Modules:
  0.0 41.5 jit_solution(7753032712004291646)
XLA Ops:
  0.6 0.9 %dynamic-slice_bitcast_fusion = bf16[8,32,128]{2,1,0:T(8,128)(2,1)S(1)} fusion(bf16[1,8,8,32,128]{4,3,2,1,0:T(8,128)(2,1)} %param.4, s32[]{:T(128)S(6)} %select_n.6), kind=kLoop, calls=%fused_computation.10 | loop fusion | bytes 131076 | tf_op jit(solution)/shard_map/jit(dynamic_index_in_dim)/squeeze | solution.py:537
  1.5 0.5 %collective-permute-start = (bf16[8,32,128]{2,1,0:T(8,128)(2,1)S(1)}, bf16[8,32,128]{2,1,0:T(8,128)(2,1)S(1)}, u32[]{:S(2)}, u32[]{:S(2)}) collective-permute-start(bf16[8,32,128]{2,1,0:T(8,128)(2,1)S(1)} %dynamic-slice_bitcast_fusion), channel_id=1, source_target_pairs={{0,1},{1,0},{2,3},{3,2},{4,5},{5,4},{6,7},{7,6},{8,9},{9,8},{10,11... | collective-permute-start | bytes 196616 | tf_op jit(solution)/shard_map/ppermute | solution.py:491
  1.9 0.9 %slice.19 = bf16[1,2,8,32,128]{4,3,2,1,0:T(8,128)(2,1)S(1)} slice(bf16[1,8,8,32,128]{4,3,2,1,0:T(8,128)(2,1)} %param.4), slice={[0:1], [6:8], [0:8], [0:32], [0:128]} | slice | bytes 262144 | tf_op jit(solution)/shard_map/slice | solution.py:546
  2.9 0.0 copy-start
  2.9 0.0 copy-start.1
  2.9 0.0 copy-start.3
  2.9 4.8 %collective-permute-start.1 = (bf16[18,32,128]{2,1,0:T(8,128)(2,1)S(1)}, bf16[18,32,128]{2,1,0:T(8,128)(2,1)S(1)}, u32[]{:S(2)}, u32[]{:S(2)}) collective-permute-start(bf16[18,32,128]{2,1,0:T(8,128)(2,1)S(1)} %border_rows.1), channel_id=1, source_target_pairs={{0,2},{2,4},{4,6},{1,3},{3,5},{5,7},{8,10},{10,12},{12,14},{9,11},... | collective-permute-start | bytes 442376 | tf_op jit(solution)/shard_map/ppermute | solution.py:487
  7.8 4.9 %forward_interior.1 = (bf16[8,8,32,128]{3,2,1,0:T(8,128)(2,1)}, bf16[8,10,32,384]{3,2,1,0:T(8,128)(2,1)S(1)}, bf16[4608,256]{1,0:T(8,128)(2,1)S(1)}, bf16[3,256,...) custom-call(bf16[8,8,32,128]{3,2,1,0:T(8,128)(2,1)S(1)} %bitcast.25,, ...), custom_call_target="tpu_custom_call" | custom-call | flops 2717908992 | bytes 4194304 | tf_op jit(solution)/shard_map/forward_interior/pallas_call | solution.py:519
  12.7 3.3 %first_frames_and_leaving_half.1 = (bf16[8,8,32,128]{3,2,1,0:T(8,128)(2,1)}, bf16[2,8,32,128]{3,2,1,0:T(8,128)(2,1)S(1)}, bf16[8,32,128]{2,1,0:T(8,128)(2,1)S(1)...) custom-call(bf16[8,8,32,128]{3,2,1,0:T(8,128)(2,1)} %get-tuple-eleme, ...), custom_call_target="tpu_custom_call", output_to_operand_aliasing={{0}: (0, {})} | custom-call | flops 2899102976 | bytes 4194304 | tf_op jit(solution)/shard_map/first_frames_and_leaving_half/pallas_call | solution.py:519
  16.0 0.1 collective-permute-start.3
  16.1 0.5 %collective-permute-start.2 = (bf16[8,32,128]{2,1,0:T(8,128)(2,1)S(1)}, bf16[8,32,128]{2,1,0:T(8,128)(2,1)S(1)}, u32[]{:S(2)}, u32[]{:S(2)}) collective-permute-start(bf16[8,32,128]{2,1,0:T(8,128)(2,1)S(1)} %get-tuple-element.41), channel_id=1, source_target_pairs={{0,1},{1,0},{2,3},{3,2},{4,5},{5,4},{6,7},{7,6},{8,9},{9,8},{10,11... | collective-permute-start | bytes 196616 | tf_op jit(solution)/shard_map/ppermute | solution.py:491
  16.6 1.1 %staying_half.1 = bf16[4,448,128]{2,1,0:T(8,128)(2,1)S(1)} custom-call(bf16[9,384,128]{2,1,0:T(8,128)(2,1)S(1)} %get-tuple-element.42.blocks_in, bf16[4,10,32,384]{3,2,1,0:T(8,128)(2,1)S(1)} %get-tuple-element.43.front, bf16[8,10,32,384]{3,2,1,0:T(8,128)(2,1)S(1)} %get-tuple-element.34.windows, bf16[128,2048]{1,0:T(8,128)(2,1)S(1)} %get-tuple-element.44.grads, ...), custom_call_target="tpu_custom_call" | custom-call | flops 1630745344 | bytes 4194304 | tf_op jit(solution)/shard_map/staying_half/pallas_call | solution.py:519
  17.7 0.2 collective-permute-done.3
  17.9 0.1 add_convert_fusion
  18.0 2.7 %collective-permute-start.4 = (bf16[448,128]{1,0:T(8,128)(2,1)S(1)}, bf16[448,128]{1,0:T(8,128)(2,1)S(1)}, u32[]{:S(2)}, u32[]{:S(2)}) collective-permute-start(bf16[448,128]{1,0:T(8,128)(2,1)S(1)} %get-tuple-element.62), channel_id=1, source_target_pairs={{0,16},{1,17},{8,24},{9,25},{16,0},{17,1},{24,8},{25,9},{2,18},{3,... | collective-permute-start | bytes 344072 | tf_op jit(solution)/shard_map/ppermute | solution.py:477
  20.7 1.6 %collective-permute-start.6 = (bf16[448,128]{1,0:T(8,128)(2,1)S(1)}, bf16[448,128]{1,0:T(8,128)(2,1)S(1)}, u32[]{:S(2)}, u32[]{:S(2)}) collective-permute-start(bf16[448,128]{1,0:T(8,128)(2,1)S(1)} %get-tuple-element.63), channel_id=1, source_target_pairs={{0,8},{1,9},{8,0},{9,1},{16,24},{17,25},{24,16},{25,17},{2,10},{3,... | collective-permute-start | bytes 344072 | tf_op jit(solution)/shard_map/ppermute | solution.py:477
  22.3 0.2 collective-permute-start.5
  22.5 4.1 %input_gradient_interior.1 = (bf16[8,8,32,128]{3,2,1,0:T(8,128)(2,1)}, bf16[2,10,32,384]{3,2,1,0:T(8,128)(2,1)S(1)}, bf16[256,4608]{1,0:T(8,128)(2,1)S(1)}) custom-call(bf16[2,8,32,128]{3,2,1,0:T(8,128)(2,1)S(1)} %get-tuple-element.48.early, bf16[6,8,32,128]{3,2,1,0:T(8,128)(2,1)S(1)} %get-tuple-element.49.g, ...), custom_call_target="tpu_custom_call" | custom-call | flops 2717908992 | bytes 4194304 | tf_op jit(solution)/shard_map/input_gradient_interior/pallas_call | solution.py:519
  26.7 1.3 %collective-permute-start.10 = (bf16[18,32,128]{2,1,0:T(8,128)(2,1)S(1)}, bf16[18,32,128]{2,1,0:T(8,128)(2,1)S(1)}, u32[]{:S(2)}, u32[]{:S(2)}) collective-permute-start(bf16[18,32,128]{2,1,0:T(8,128)(2,1)S(1)} %pad_maximum_fusion), channel_id=1, source_target_pairs={{2,0},{4,2},{6,4},{3,1},{5,3},{7,5},{10,8},{12,10},{14,12},{11,9},... | collective-permute-start | bytes 442376 | tf_op jit(solution)/shard_map/ppermute | solution.py:487
  28.0 0.0 collective-permute-done.4
  28.0 2.3 %collective-permute-done.5 = bf16[448,128]{1,0:T(8,128)(2,1)S(1)} collective-permute-done((bf16[448,128]{1,0:T(8,128)(2,1)S(1)}, bf16[448,128]{1,0:T(8,128)(2,1)S(1)}, u32[]{:S(2)}, u32[]{:S(2)}) %collective-permute-start.5) | collective-permute-done | bytes 114720 | tf_op jit(solution)/shard_map/ppermute | solution.py:477
  30.3 0.1 fusion.2
  30.3 2.0 %collective-permute-start.9 = (bf16[448,128]{1,0:T(8,128)(2,1)S(1)}, bf16[448,128]{1,0:T(8,128)(2,1)S(1)}, u32[]{:S(2)}, u32[]{:S(2)}) collective-permute-start(bf16[448,128]{1,0:T(8,128)(2,1)S(1)} %fusion.2), channel_id=1, source_target_pairs={{0,6},{1,7},{2,4},{3,5},{4,2},{5,3},{6,0},{7,1},{8,14},{9,15},{10,... | collective-permute-start | bytes 344072 | tf_op jit(solution)/shard_map/ppermute | solution.py:477
  32.4 1.0 %collective-permute-start.8 = (bf16[448,128]{1,0:T(8,128)(2,1)S(1)}, bf16[448,128]{1,0:T(8,128)(2,1)S(1)}, u32[]{:S(2)}, u32[]{:S(2)}) collective-permute-start(bf16[448,128]{1,0:T(8,128)(2,1)S(1)} %fusion.2), channel_id=1, source_target_pairs={{0,4},{1,3},{2,6},{3,1},{4,0},{5,7},{6,2},{7,5},{8,12},{9,11},{10,... | collective-permute-start | bytes 344072 | tf_op jit(solution)/shard_map/ppermute | solution.py:477
  33.4 0.5 %collective-permute-start.7 = (bf16[448,128]{1,0:T(8,128)(2,1)S(1)}, bf16[448,128]{1,0:T(8,128)(2,1)S(1)}, u32[]{:S(2)}, u32[]{:S(2)}) collective-permute-start(bf16[448,128]{1,0:T(8,128)(2,1)S(1)} %fusion.2), channel_id=1, source_target_pairs={{0,2},{1,5},{2,0},{3,7},{4,6},{5,1},{6,4},{7,3},{8,10},{9,13},{10,... | collective-permute-start | bytes 344072 | tf_op jit(solution)/shard_map/ppermute | solution.py:477
  33.9 1.7 %input_gradient_last.1 = bf16[8,8,32,128]{3,2,1,0:T(8,128)(2,1)} custom-call(bf16[8,8,32,128]{3,2,1,0:T(8,128)(2,1)} %get-tuple-element.53.grad_in, bf16[2,10,32,384]{3,2,1,0:T(8,128)(2,1)S(1)} %get-tuple-element.55.last, bf16[18,32,128]{2,1,0:T(8,128)(2,1)S(1)} %collective-permute-done.10.after, ...), custom_call_target="tpu_custom_call", output_to_operand_aliasing={{}: (0, {})} | custom-call | flops 905969664 | bytes 4194304 | tf_op jit(solution)/shard_map/input_gradient_last/pallas_call | solution.py:519
  35.7 3.2 %collective-permute-done.9 = bf16[448,128]{1,0:T(8,128)(2,1)S(1)} collective-permute-done((bf16[448,128]{1,0:T(8,128)(2,1)S(1)}, bf16[448,128]{1,0:T(8,128)(2,1)S(1)}, u32[]{:S(2)}, u32[]{:S(2)}) %collective-permute-start.9) | collective-permute-done | bytes 114720 | tf_op jit(solution)/shard_map/ppermute | solution.py:477
  38.9 0.3 collective-permute-done.8
  39.2 0.1 add_convert_fusion.1.own
  39.2 0.1 collective-permute-start.11
  39.3 1.3 %collective-permute-done.11.other = bf16[448,128]{1,0:T(8,128)(2,1)S(1)} collective-permute-done((bf16[448,128]{1,0:T(8,128)(2,1)S(1)}, bf16[448,128]{1,0:T(8,128)(2,1)S(1)}, u32[]{:S(2)}, u32[]{:S(2)}) %collective-permute-start.11) | collective-permute-done | bytes 114720 | tf_op jit(solution)/shard_map/ppermute | solution.py:491
  40.6 0.9 %scaled_weights.1 = (f32[864,128]{1,0:T(8,128)}, f32[1,32]{1,0:T(1,128)}) custom-call(bf16[448,128]{1,0:T(8,128)(2,1)S(1)} %add_convert_fusion.1.own, bf16[448,128]{1,0:T(8,128)(2,1)S(1)} %collective-permute-done.11.other), custom_call_target="tpu_custom_call" | custom-call | flops 36238784 | bytes 4194304 | tf_op jit(solution)/shard_map/scaled_weights/pallas_call | solution.py:519
  (15 shorter events, 0.1 us)
Async XLA Ops:
  1.5 1.4 %collective-permute-start = (bf16[8,32,128]{2,1,0:T(8,128)(2,1)S(1)}, bf16[8,32,128]{2,1,0:T(8,128)(2,1)S(1)}, u32[]{:S(2)}, u32[]{:S(2)}) collective-permute-start(bf16[8,32,128]{2,1,0:T(8,128)(2,1)S(1)} %dynamic-slice_bitcast_fusion), channel_id=1, source_target_pairs={{0,1},{1,0},{2,3},{3,2},{4,5},{5,4},{6,7},{7,6},{8,9},{9,8},{10,11... | collective-permute-start | bytes 196616 | tf_op jit(solution)/shard_map/ppermute | solution.py:491
  2.9 4.9 %copy-start = (bf16[1,8,8,32,128]{4,3,2,1,0:T(8,128)(2,1)S(1)}, bf16[1,8,8,32,128]{4,3,2,1,0:T(8,128)(2,1)}, u32[]{:S(2)}) copy-start(bf16[1,8,8,32,128]{4,3,2,1,0:T(8,128)(2,1)} %param.7) | copy-start | bytes 1572868
  2.9 4.9 %copy-start.1 = (bf16[1,8,8,32,128]{4,3,2,1,0:T(8,128)(2,1)S(1)}, bf16[1,8,8,32,128]{4,3,2,1,0:T(8,128)(2,1)}, u32[]{:S(2)}) copy-start(bf16[1,8,8,32,128]{4,3,2,1,0:T(8,128)(2,1)} %param.4) | copy-start | bytes 1572868
  2.9 4.9 %copy-start.2 = (bf16[3456,128]{1,0:T(8,128)(2,1)S(1)}, bf16[3456,128]{1,0:T(8,128)(2,1)}, u32[]{:S(2)}) copy-start(bf16[3456,128]{1,0:T(8,128)(2,1)} %kernel.3) | copy-start | bytes 2654212
  2.9 4.9 %copy-start.3 = (f32[128]{0:T(128)S(1)}, f32[128]{0:T(128)}, u32[]{:S(2)}) copy-start(f32[128]{0:T(128)} %param.6) | copy-start | bytes 1540
  2.9 9.8 %collective-permute-start.1 = (bf16[18,32,128]{2,1,0:T(8,128)(2,1)S(1)}, bf16[18,32,128]{2,1,0:T(8,128)(2,1)S(1)}, u32[]{:S(2)}, u32[]{:S(2)}) collective-permute-start(bf16[18,32,128]{2,1,0:T(8,128)(2,1)S(1)} %border_rows.1), channel_id=1, source_target_pairs={{0,2},{2,4},{4,6},{1,3},{3,5},{5,7},{8,10},{10,12},{12,14},{9,11},... | collective-permute-start | bytes 442376 | tf_op jit(solution)/shard_map/ppermute | solution.py:487
  16.0 1.9 %collective-permute-start.3 = (bf16[4,448,128]{2,1,0:T(8,128)(2,1)S(1)}, bf16[4,448,128]{2,1,0:T(8,128)(2,1)S(1)}, u32[]{:S(2)}, u32[]{:S(2)}) collective-permute-start(bf16[4,448,128]{2,1,0:T(8,128)(2,1)S(1)} %get-tuple-element.46), channel_id=1, source_target_pairs={{0,1},{1,0},{2,3},{3,2},{4,5},{5,4},{6,7},{7,6},{8,9},{9,8},{10,11... | collective-permute-start | bytes 1376264 | tf_op jit(solution)/shard_map/ppermute | solution.py:491
  16.1 1.9 %collective-permute-start.2 = (bf16[8,32,128]{2,1,0:T(8,128)(2,1)S(1)}, bf16[8,32,128]{2,1,0:T(8,128)(2,1)S(1)}, u32[]{:S(2)}, u32[]{:S(2)}) collective-permute-start(bf16[8,32,128]{2,1,0:T(8,128)(2,1)S(1)} %get-tuple-element.41), channel_id=1, source_target_pairs={{0,1},{1,0},{2,3},{3,2},{4,5},{5,4},{6,7},{7,6},{8,9},{9,8},{10,11... | collective-permute-start | bytes 196616 | tf_op jit(solution)/shard_map/ppermute | solution.py:491
  18.0 10.0 %collective-permute-start.4 = (bf16[448,128]{1,0:T(8,128)(2,1)S(1)}, bf16[448,128]{1,0:T(8,128)(2,1)S(1)}, u32[]{:S(2)}, u32[]{:S(2)}) collective-permute-start(bf16[448,128]{1,0:T(8,128)(2,1)S(1)} %get-tuple-element.62), channel_id=1, source_target_pairs={{0,16},{1,17},{8,24},{9,25},{16,0},{17,1},{24,8},{25,9},{2,18},{3,... | collective-permute-start | bytes 344072 | tf_op jit(solution)/shard_map/ppermute | solution.py:477
  20.7 7.3 %collective-permute-start.6 = (bf16[448,128]{1,0:T(8,128)(2,1)S(1)}, bf16[448,128]{1,0:T(8,128)(2,1)S(1)}, u32[]{:S(2)}, u32[]{:S(2)}) collective-permute-start(bf16[448,128]{1,0:T(8,128)(2,1)S(1)} %get-tuple-element.63), channel_id=1, source_target_pairs={{0,8},{1,9},{8,0},{9,1},{16,24},{17,25},{24,16},{25,17},{2,10},{3,... | collective-permute-start | bytes 344072 | tf_op jit(solution)/shard_map/ppermute | solution.py:477
  22.3 8.0 %collective-permute-start.5 = (bf16[448,128]{1,0:T(8,128)(2,1)S(1)}, bf16[448,128]{1,0:T(8,128)(2,1)S(1)}, u32[]{:S(2)}, u32[]{:S(2)}) collective-permute-start(bf16[448,128]{1,0:T(8,128)(2,1)S(1)} %get-tuple-element.64), channel_id=1, source_target_pairs={{0,24},{1,25},{8,16},{9,17},{16,8},{17,9},{24,0},{25,1},{2,26},{3,... | collective-permute-start | bytes 344072 | tf_op jit(solution)/shard_map/ppermute | solution.py:477
  26.7 7.2 %collective-permute-start.10 = (bf16[18,32,128]{2,1,0:T(8,128)(2,1)S(1)}, bf16[18,32,128]{2,1,0:T(8,128)(2,1)S(1)}, u32[]{:S(2)}, u32[]{:S(2)}) collective-permute-start(bf16[18,32,128]{2,1,0:T(8,128)(2,1)S(1)} %pad_maximum_fusion), channel_id=1, source_target_pairs={{2,0},{4,2},{6,4},{3,1},{5,3},{7,5},{10,8},{12,10},{14,12},{11,9},... | collective-permute-start | bytes 442376 | tf_op jit(solution)/shard_map/ppermute | solution.py:487
  30.3 8.5 %collective-permute-start.9 = (bf16[448,128]{1,0:T(8,128)(2,1)S(1)}, bf16[448,128]{1,0:T(8,128)(2,1)S(1)}, u32[]{:S(2)}, u32[]{:S(2)}) collective-permute-start(bf16[448,128]{1,0:T(8,128)(2,1)S(1)} %fusion.2), channel_id=1, source_target_pairs={{0,6},{1,7},{2,4},{3,5},{4,2},{5,3},{6,0},{7,1},{8,14},{9,15},{10,... | collective-permute-start | bytes 344072 | tf_op jit(solution)/shard_map/ppermute | solution.py:477
  32.4 6.8 %collective-permute-start.8 = (bf16[448,128]{1,0:T(8,128)(2,1)S(1)}, bf16[448,128]{1,0:T(8,128)(2,1)S(1)}, u32[]{:S(2)}, u32[]{:S(2)}) collective-permute-start(bf16[448,128]{1,0:T(8,128)(2,1)S(1)} %fusion.2), channel_id=1, source_target_pairs={{0,4},{1,3},{2,6},{3,1},{4,0},{5,7},{6,2},{7,5},{8,12},{9,11},{10,... | collective-permute-start | bytes 344072 | tf_op jit(solution)/shard_map/ppermute | solution.py:477
  33.4 5.8 %collective-permute-start.7 = (bf16[448,128]{1,0:T(8,128)(2,1)S(1)}, bf16[448,128]{1,0:T(8,128)(2,1)S(1)}, u32[]{:S(2)}, u32[]{:S(2)}) collective-permute-start(bf16[448,128]{1,0:T(8,128)(2,1)S(1)} %fusion.2), channel_id=1, source_target_pairs={{0,2},{1,5},{2,0},{3,7},{4,6},{5,1},{6,4},{7,3},{8,10},{9,13},{10,... | collective-permute-start | bytes 344072 | tf_op jit(solution)/shard_map/ppermute | solution.py:477
  39.2 1.4 %collective-permute-start.11 = (bf16[448,128]{1,0:T(8,128)(2,1)S(1)}, bf16[448,128]{1,0:T(8,128)(2,1)S(1)}, u32[]{:S(2)}, u32[]{:S(2)}) collective-permute-start(bf16[448,128]{1,0:T(8,128)(2,1)S(1)} %add_convert_fusion.1.own), channel_id=1, source_target_pairs={{0,1},{1,0},{2,3},{3,2},{4,5},{5,4},{6,7},{7,6},{8,9},{9,8},{10,11... | collective-permute-start | bytes 344072 | tf_op jit(solution)/shard_map/ppermute | solution.py:491
